TPU v7x, 128 devices: a whole 4x4x4 slice. The times are simulated.
128 devices in a mesh: ri: 16 (over z, y), ao: 8 (over x, core).
Axes of the slice: x: 4, y: 4, z: 4, core: 2. Of those that a mesh axis runs over, the one named last changes fastest.
Arguments:
- three_center: bfloat16 [64, 16, 4, 128, 128], P('ri', 'ao'), may hold values from -6 to 6
- neighbors: int32 [16, 4], P('ao'), may hold values from 0 to 15, as said below
- block_sizes: int32 [16], replicated, may hold values from 64 to 128
- green_occ: bfloat16 [2048, 2048], P(('ri', 'ao')), may hold values from -0.25 to 0.25
- green_virt: bfloat16 [2048, 2048], P(('ri', 'ao')), may hold values from -0.125 to 0.125
Outputs:
- contracted: float32 [64, 2048, 2048], P('ri', None, 'ao')
Inputs may be any that keep to these rules, and one draw needn't show every extreme that they name: neighbors[a, 0] = a, and the 4 entries of a row differ.
All inputs are finite; a program needn't handle non-finite values.
Results may differ from a plain program's by a relative error of at most 0.0029.
Values may be sent and summed in bfloat16 or wider, within the bound.
No kernel may reach another device: no remote copies, remote signals or barrier semaphores. Data moves between devices by JAX's collectives and lax.ppermute only.
A program may use at most 128 MiB of HBM per device.

v0:
```python
import jax
import jax.numpy as jnp
from jax import lax
from jax.sharding import PartitionSpec as P


def whole_occ(green_occ):
    return lax.all_gather(green_occ, ("ri", "ao"), axis=0, tiled=True)


def body(three_center, neighbors, block_sizes, green_occ, green_virt):
    rows_local = three_center.shape[0]
    atoms_local = three_center.shape[1]
    width = three_center.shape[3]
    atoms_total = block_sizes.shape[0]
    ao_total = atoms_total * width
    position = jnp.arange(width, dtype=jnp.int32)
    live_blocks = (position[None, :] < block_sizes[:, None]).astype(jnp.bfloat16)
    live_flat = live_blocks.reshape(ao_total).astype(jnp.float32)
    virt_whole = lax.all_gather(green_virt, ("ri", "ao"), axis=0, tiled=True)
    col_width = ao_total // lax.axis_size("ao")
    first_col = lax.axis_index("ao") * col_width
    col_live = lax.dynamic_slice_in_dim(live_flat, first_col, col_width, 0)
    occ_whole = whole_occ(green_occ)
    first_atom = lax.axis_index("ao") * atoms_local
    local_live = lax.dynamic_slice_in_dim(live_blocks, first_atom, atoms_local, 0)
    masked = (
        three_center
        * local_live[None, :, None, :, None]
        * live_blocks[neighbors][None, :, :, None, :]
    )
    occ_blocks = occ_whole.reshape(atoms_total, width, ao_total)[neighbors]
    partial_rows = jnp.einsum(
        "pajik,ajkl->pail", masked, occ_blocks, preferred_element_type=jnp.float32
    )
    outgoing = partial_rows.astype(jnp.bfloat16).reshape(rows_local, atoms_local * width, ao_total)
    result = jnp.einsum(
        "sm,pml->psl",
        virt_whole,
        lax.all_to_all(outgoing, "ao", split_axis=2, concat_axis=1, tiled=True),
        preferred_element_type=jnp.float32,
    )
    return result * live_flat[None, :, None] * col_live[None, None, :]


def solution(mesh):
    in_specs = (
        P("ri", "ao", None, None, None),
        P("ao", None),
        P(),
        P(("ri", "ao"), None),
        P(("ri", "ao"), None),
    )
    out_specs = P("ri", None, "ao")
    return jax.shard_map(body, mesh=mesh, in_specs=in_specs, out_specs=out_specs, check_vma=False)
```

profile of v0, /device:TPU:1, one launch (start us, length us, event | category | flops | bytes accessed | tf_op | source)
XLA Modules:
  0.0 208.1 jit_solution(14758978293015296477)
XLA Ops:
  6.5 0.0 all-gather.3.cloned.1.call-start
  6.5 0.7 all-gather.3.cloned.1.call-update
  7.3 0.0 all-gather.5.cloned.1.call-start
  7.3 0.7 all-gather.5.cloned.1.call-update
  8.0 0.7 compare_select_fusion
  8.7 0.1 reshape.35
  8.8 0.7 bitcast_convert_fusion.1
  9.5 0.6 gather_fusion.1
  10.1 74.1 %all-gather.3.cloned.1.call-done = bf16[2048,2048]{1,0:T(8,128)(2,1)} async-done(((bf16[16,2048]{1,0:T(8,128)(2,1)}), bf16[2048,2048]{1,0:T(8,128)(2,1)}) %all-gather.3.cloned.1.call-update) | async-done | bytes 8388624 | tf_op jit(solution)/shard_map/all_gather | solution.py:8
  84.1 0.0 copy-start
  84.2 6.3 %gather_fusion = bf16[8,128,2048]{2,1,0:T(8,128)(2,1)} fusion(bf16[16,128,2048]{2,1,0:T(8,128)(2,1)} %bitcast.36, s32[1024]{0:T(1024)S(1)} %pad_clamp_fusion), kind=kCustom, calls=%fused_computation | custom fusion | bytes 8388640 | tf_op jit(solution)/shard_map/gather | solution.py:32
  90.4 0.0 copy-done
  90.4 4.8 %fusion.4 = bf16[4,2,128,2048]{3,2,0,1:T(8,128)(2,1)S(1)} fusion(bf16[2,4,128,2048,1]{3,2,1,4,0:T(8,128)(2,1)} %bitcast.35, bf16[4,2,4,128,128]{4,3,2,1,0:T(8,128)(2,1)S(1)} %copy-done, bf16[2,4,128]{2,1,0:T(4,128)(2,1)S(1)} %bitcast.37, bf16[2,128]{1,0:T(2,128)(2,1)S(1)} %constant_dynamic-slice_fusion), kind=kOutput, calls=%fused_computation.6 | convolution fusion | flops 2150629376 | bytes 9439744 | tf_op jit(solution)/shard_map/pajik,ajkl->pail/dot_general | solution.py:33
  95.3 2.5 %copy.14 = bf16[4,2,128,2048]{3,2,1,0:T(8,128)(2,1)} copy(bf16[4,2,128,2048]{3,2,0,1:T(8,128)(2,1)S(1)} %fusion.4) | data formatting | bytes 8388608 | tf_op jit(solution)/shard_map/convert_element_type | solution.py:36
  97.8 7.5 %copy.15 = bf16[4,256,2048]{1,0,2:T(4,128)(2,1)} copy(bf16[4,256,2048]{2,1,0:T(8,128)(2,1)} %bitcast.32) | data formatting | bytes 8388608 | tf_op jit(solution)/shard_map/reshape | solution.py:36
  105.3 4.7 %all-to-all-start = ((bf16[4,256,2048]{1,0,2:T(4,128)(2,1)}), bf16[4,256,2048]{1,0,2:T(4,128)(2,1)}, u32[]{:S(2)}, u32[]{:S(2)}) async-start(bf16[4,256,2048]{1,0,2:T(4,128)(2,1)} %copy.15), calls=%async_computation | async-start | bytes 8388608 | tf_op jit(solution)/shard_map/all_to_all | solution.py:40
  110.0 0.1 dynamic_slice.7
  110.1 62.7 %all-to-all-done = bf16[4,256,2048]{1,0,2:T(4,128)(2,1)} async-done(((bf16[4,256,2048]{1,0,2:T(4,128)(2,1)}), bf16[4,256,2048]{1,0,2:T(4,128)(2,1)}, u32[]{:S(2)}, u32[]{:S(2)}) %all-to-all-start) | async-done | bytes 4194336 | tf_op jit(solution)/shard_map/all_to_all | solution.py:40
  172.8 2.7 %copy.16 = bf16[4,256,2048]{1,2,0:T(8,128)(2,1)S(1)} copy(bf16[4,256,2048]{1,0,2:T(4,128)(2,1)} %all-to-all-done) | data formatting | bytes 8388608 | tf_op jit(solution)/shard_map/all_to_all | solution.py:40
  175.5 2.6 %copy.21 = bf16[4,8,32,8,256]{4,3,1,2,0:T(8,128)(2,1)} copy(bf16[4,8,32,8,256]{4,3,2,1,0:T(8,128)(2,1)S(1)} %bitcast.33) | data formatting | bytes 8388608 | tf_op jit(solution)/shard_map/all_to_all | solution.py:40
  178.1 0.0 all-gather.5.cloned.1.call-done
  178.1 14.5 %multiply_bitcast_fusion = f32[4,2048,256]{1,2,0:T(8,128)} fusion(bf16[4,2048,256]{1,2,0:T(8,128)(2,1)} %bitcast.34, bf16[2048,2048]{1,0:T(8,128)(2,1)} %all-gather.5.cloned.1.call-done, f32[256]{0:T(256)S(1)} %dynamic_slice.7, f32[2048]{0:T(1024)S(1)} %get-tuple-element.5), kind=kOutput, calls=%fused_computation.5 | convolution fusion | flops 8594128896 | bytes 20980736 | tf_op jit(solution)/shard_map/sm,pml->psl/dot_general | solution.py:37
  192.6 8.7 %copy.18 = f32[4,2048,256]{2,1,0:T(8,128)} copy(f32[4,2048,256]{1,2,0:T(8,128)} %multiply_bitcast_fusion) | data formatting | bytes 16777216 | tf_op jit(solution)/shard_map/mul | solution.py:43
  (2 shorter events, 0.0 us)
Async XLA Ops:
  6.5 77.6 %all-gather.3.cloned.1.call-start = ((), (), s32[]{:S(2)}) async-start(), calls=%async_computation.1 | async-start | bytes 8454144 | tf_op jit(solution)/shard_map/all_gather | solution.py:8
  7.3 170.8 %all-gather.5.cloned.1.call-start = ((), (), s32[]{:S(2)}) async-start(), calls=%async_computation.2 | async-start | bytes 8454144 | tf_op jit(solution)/shard_map/all_gather | solution.py:20
  84.1 6.3 %copy-start = (bf16[4,2,4,128,128]{4,3,2,1,0:T(8,128)(2,1)S(1)}, bf16[4,2,4,128,128]{4,3,2,1,0:T(8,128)(2,1)}, u32[]{:S(2)}) copy-start(bf16[4,2,4,128,128]{4,3,2,1,0:T(8,128)(2,1)} %param.5) | copy-start | bytes 3145732
  105.3 67.5 %all-to-all-start = ((bf16[4,256,2048]{1,0,2:T(4,128)(2,1)}), bf16[4,256,2048]{1,0,2:T(4,128)(2,1)}, u32[]{:S(2)}, u32[]{:S(2)}) async-start(bf16[4,256,2048]{1,0,2:T(4,128)(2,1)} %copy.15), calls=%async_computation | async-start | bytes 8388608 | tf_op jit(solution)/shard_map/all_to_all | solution.py:40
Sparse Core Ops, SparseCore 0:
  10.3 73.7 all-gather.2
  87.1 77.5 all-gather.4
where the time goes:
time: 209 us; the launch traced here: 208 us
  waiting for transfers between devices  138 us (66%)
  local copies, waits for them, and re-layouts  31 us (15%)
  matrix products  19.3 us (9%)
  between operations  13.4 us (6%)
  starting transfers between devices  4.77 us (2%)
    all_gather x1, waiting for transfers between devices, whole_occ(): return lax.all_gather(green_occ, ('ri', 'ao'), axis=0, tiled=True)  74.1 us
    all_to_all x1, waiting for transfers between devices, body(): lax.all_to_all(outgoing, 'ao', split_axis=2, concat_axis=1, tiled=True)  62.7 us
    dot_general x1, matrix products, body(): jnp.einsum('sm,pml->psl', virt_whole, lax.all_to_all(outgoing, 'ao', spli...  14.5 us
    mul x1, local copies, waits for them, and re-layouts, body(): return result * live_flat[None, :, None] * col_live[None, None, :]  8.67 us
    reshape x1, local copies, waits for them, and re-layouts, body(): partial_rows.astype(jnp.bfloat16)  7.46 us
    gather x1, local copies, waits for them, and re-layouts, body(): occ_blocks = occ_whole.reshape(atoms_total, width, ao_total)[neighbors]  6.3 us
    all_to_all x2, local copies, waits for them, and re-layouts, body(): lax.all_to_all(outgoing, 'ao', split_axis=2, concat_axis=1, tiled=True)  5.33 us
    dot_general x1, matrix products, body(): jnp.einsum('pajik,ajkl->pail', masked, occ_blocks, preferred_element_type...  4.82 us
  transfers between devices with their start and end apart: 3, of which 2 were waited for; matrix products, arithmetic and copies ran while one was open for 14% of the time, Pallas kernels for 0%

commit v1 on v0

v1 whole, which is shorter than its diff:
```python
import functools

import jax
import jax.numpy as jnp
from jax import lax
from jax.experimental import pallas as pl
from jax.experimental.pallas import tpu as pltpu
from jax.sharding import PartitionSpec as P

AXES = ("ri", "ao")
GROUPS = 2
VMEM_LIMIT = 56 * 1024 * 1024
VMEM = pl.BlockSpec(memory_space=pltpu.VMEM)
SMEM = pl.BlockSpec(memory_space=pltpu.SMEM)
ANY = pl.BlockSpec(memory_space=pl.ANY)


def pairs(step):
    out = []
    for z in range(4):
        for y in range(4):
            for x in range(4):
                for c in range(2):
                    tz, ty, tx, tc = step(z, y, x, c)
                    target = (((tz % 4) * 4 + ty % 4) * 4 + tx % 4) * 2 + tc
                    out.append((((z * 4 + y) * 4 + x) * 2 + c, target))
    return out


CORE = pairs(lambda z, y, x, c: (z, y, x, 1 - c))
RING_X = pairs(lambda z, y, x, c: (z, y, x + 1 - 2 * c, c))
SHIFT_X = [None] + [pairs(lambda z, y, x, c, d=d: (z, y, x + d, c)) for d in (1, 2, 3)]
STAGE_A = [None] + [
    pairs(lambda z, y, x, c, d=d: (z + d * c, y + d * (1 - c), x, c)) for d in (1, 2, 3)
]
STAGE_B = [None] + [
    pairs(lambda z, y, x, c, d=d: (z + d * (1 - c), y + d * c, x, c)) for d in (1, 2, 3)
]


def move(value, perm):
    return lax.ppermute(value, AXES, perm)


def spread(value, stage):
    return [value] + [move(value, stage[d]) for d in (1, 2, 3)]


def first_kernel(group, place, neighbors, *refs):
    chunks, occ_mine, occ_other, keep, send, occ = refs[:4], *refs[4:9]
    z, y, x, c = place[0], place[1], place[2], place[3]
    for far in range(4):
        for near in range(4):
            a_mine = lax.rem(z - jnp.where(c == 0, far, near) + 4, 4) * 4 + lax.rem(
                y - jnp.where(c == 0, near, far) + 4, 4
            )
            a_other = lax.rem(z - jnp.where(c == 0, near, far) + 4, 4) * 4 + lax.rem(
                y - jnp.where(c == 0, far, near) + 4, 4
            )
            for shard in range(4):
                occ[a_mine, pl.ds(pl.multiple_of(shard * 32 + c * 16, 16), 16), :] = occ_mine[
                    far, near, shard
                ]
                row = pl.ds(pl.multiple_of(shard * 32 + (1 - c) * 16, 16), 16)
                occ[a_other, row, 0:256] = occ_other[far, near, shard, :, 256:512]
                occ[a_other, row, 256:512] = occ_other[far, near, shard, :, 0:256]
    for step in range(4):
        at = lax.rem(x + jnp.where(c == 0, 4 - step, step), 4)
        for atom in range(2):
            right = jnp.concatenate(
                [occ[neighbors[at, atom * 4 + j]] for j in range(4)], axis=0
            )
            left = jnp.concatenate(
                [
                    jnp.concatenate([chunks[step][p, atom, j] for j in range(4)], axis=1)
                    for p in range(group)
                ],
                axis=0,
            )
            done = jnp.dot(left, right, preferred_element_type=jnp.float32).astype(jnp.bfloat16)
            for p in range(group):
                rows = pl.ds(atom * 128, 128)
                keep[p, at, rows, :] = done[p * 128 : (p + 1) * 128, :256]
                send[p, at, rows, :] = done[p * 128 : (p + 1) * 128, 256:]


def first_call(group, place, neighbors, chunks, occ_mine, occ_other):
    shape = jax.ShapeDtypeStruct((group, 4, 256, 256), jnp.bfloat16)
    return pl.pallas_call(
        functools.partial(first_kernel, group),
        out_shape=(shape, shape),
        in_specs=[SMEM, SMEM] + [VMEM] * 6,
        out_specs=(VMEM, VMEM),
        scratch_shapes=[pltpu.VMEM((16, 128, 512), jnp.bfloat16)],
        compiler_params=pltpu.CompilerParams(vmem_limit_bytes=VMEM_LIMIT),
        cost_estimate=pl.CostEstimate(
            flops=group * 2 * 1024 * 512 * 512, bytes_accessed=group * 3 * 2**20, transcendentals=0
        ),
    )(place, neighbors, *chunks, occ_mine, occ_other)


def second_kernel(group, base, place, keep, other, *refs):
    pieces, _, out, whole, held, result, in_sems, out_sems = refs[:8], *refs[8:15]
    z, y, c = place[0], place[1], place[3]
    total = 8

    def fetch(i):
        return pltpu.make_async_copy(pieces[i], held.at[i % 2], in_sems.at[i % 2])

    def stores(i):
        far, core = i % 4, c if i < 4 else 1 - c
        copies = []
        for near in range(4):
            block = lax.rem(z - jnp.where(core == 0, far, near) + 4, 4) * 4 + lax.rem(
                y - jnp.where(core == 0, near, far) + 4, 4
            )
            copies.append(
                pltpu.make_async_copy(
                    result.at[i % 2, :, near],
                    out.at[pl.ds(base, group), block, :, core],
                    out_sems.at[i % 2, near],
                )
            )
        return copies

    fetch(0).start()
    for shard in range(4):
        for p in range(group):
            whole[p, pl.ds(pl.multiple_of((shard * 2 + c) * 256, 256), 256), :] = keep[p, shard]
            whole[p, pl.ds(pl.multiple_of((shard * 2 + 1 - c) * 256, 256), 256), :] = other[p, shard]
    for i in range(total):
        if i + 1 < total:
            fetch(i + 1).start()
        fetch(i).wait()
        if i >= 2:
            for copy in stores(i - 2):
                copy.wait()
        for p in range(group):
            done = jnp.dot(held[i % 2], whole[p], preferred_element_type=jnp.float32)
            result[i % 2, p] = done.reshape(4, 4, 16, 256)
        for copy in stores(i):
            copy.start()
    for i in (total - 2, total - 1):
        for copy in stores(i):
            copy.wait()


def second_call(group, base, place, keep, other, pieces, out):
    return pl.pallas_call(
        functools.partial(second_kernel, group, base),
        out_shape=jax.ShapeDtypeStruct(out.shape, out.dtype),
        in_specs=[SMEM] + [VMEM] * 2 + [ANY] * 9,
        out_specs=ANY,
        scratch_shapes=[
            pltpu.VMEM((group, 2048, 256), jnp.bfloat16),
            pltpu.VMEM((2, 256, 2048), jnp.bfloat16),
            pltpu.VMEM((2, group, 4, 4, 16, 256), jnp.float32),
            pltpu.SemaphoreType.DMA((2,)),
            pltpu.SemaphoreType.DMA((2, 4)),
        ],
        input_output_aliases={11: 0},
        compiler_params=pltpu.CompilerParams(vmem_limit_bytes=VMEM_LIMIT),
        cost_estimate=pl.CostEstimate(
            flops=group * 2 * 2048 * 2048 * 256,
            bytes_accessed=(8 + group * 3) * 2**20,
            transcendentals=0,
        ),
    )(place, keep, other, *pieces, out)


def blank_kernel(out):
    pass


def blank(shape, dtype):
    return pl.pallas_call(
        blank_kernel, out_shape=jax.ShapeDtypeStruct(shape, dtype), out_specs=ANY
    )()


def body(three_center, neighbors, block_sizes, green_occ, green_virt):
    ri, ao = lax.axis_index("ri"), lax.axis_index("ao")
    z, y, x, c = ri // 4, ri % 4, ao // 2, ao % 2
    place = jnp.stack([z, y, x, c]).astype(jnp.int32)
    group = three_center.shape[0] // GROUPS

    position = jnp.arange(128, dtype=jnp.int32)
    live = (position[None, :] < block_sizes[:, None]).astype(jnp.bfloat16).reshape(2048)
    live_rows = lax.dynamic_slice_in_dim(live, (ri * 8 + ao) * 16, 16, 0)
    mask = live_rows[:, None] * live[None, :]
    occ = green_occ * mask
    virt = green_virt * mask
    near = jnp.zeros((16, 128), jnp.bfloat16).at[0, :8].set(
        neighbors.reshape(8).astype(jnp.bfloat16)
    )

    def pack(d):
        to = lax.rem(x + d, 4) * 512
        mine = lax.dynamic_slice_in_dim(occ, to + c * 256, 256, 1)
        other = lax.dynamic_slice_in_dim(occ, to + (1 - c) * 256, 256, 1)
        return jnp.concatenate([virt, mine, other, near], axis=1)

    packs = [pack(0)] + [move(pack((4 - t) % 4), SHIFT_X[4 - t]) for t in (1, 2, 3)]
    packs = lax.dynamic_slice_in_dim(jnp.stack(packs + packs[:3]), lax.rem(4 - x, 4), 4, 0)
    near_all = packs[:, 0, 2560:2568].astype(jnp.int32)

    occ_a = jnp.stack(spread(packs[:, :, 2048:2560], STAGE_A))
    occ_mine = jnp.stack(spread(occ_a, STAGE_B))
    occ_other = move(occ_mine, CORE)

    virt_a = jnp.concatenate(spread(packs[:, :, :2048].reshape(64, 2048), STAGE_A))
    virt_mine = spread(virt_a, STAGE_B)
    virt_pieces = virt_mine + [move(v, CORE) for v in virt_mine]

    rounds = [[three_center[g * group : (g + 1) * group] for g in range(GROUPS)]]
    for _ in range(3):
        rounds.append([move(piece, RING_X) for piece in rounds[-1]])

    out = blank((64 // 16, 16, 4, 2, 16, 256), jnp.float32)
    for g in range(GROUPS):
        keep, send = first_call(
            group, place, near_all, [r[g] for r in rounds], occ_mine, occ_other
        )
        out = second_call(group, g * group, place, keep, move(send, CORE), virt_pieces, out)
    return out.reshape(4, 2048, 256)


def solution(mesh):
    in_specs = (
        P("ri", "ao", None, None, None),
        P("ao", None),
        P(),
        P(("ri", "ao"), None),
        P(("ri", "ao"), None),
    )
    out_specs = P("ri", None, "ao")
    return jax.shard_map(body, mesh=mesh, in_specs=in_specs, out_specs=out_specs, check_vma=False)
```

time: 209 us -> 123 us (0.59)
  waiting for transfers between devices: 138 us -> 35.4 us
  starting transfers between devices: 4.77 us -> 43.2 us
  Pallas kernels: 0 us -> 33.4 us
  local copies, waits for them, and re-layouts: 31 us -> 4.58 us
  matrix products: 19.3 us -> 0 us
  between operations: 13.4 us -> 0.4 us
  other arithmetic: 1.42 us -> 4.58 us
    all_gather x2 -> x0, waiting for transfers between devices: 74.1 us -> none  [the longest x1 74.1 us: whole_occ(): return lax.all_gather(green_occ, ('ri', 'ao'), axis=0, tiled=True)]
    all_to_all x1 -> x0, waiting for transfers between devices: 62.7 us -> none  [body(): lax.all_to_all(outgoing, 'ao', split_axis=2, concat_axis=1, tiled=True)]
    ppermute x0 -> x28, starting transfers between devices: none -> 43.2 us  [move(): return lax.ppermute(value, AXES, perm)]
    ppermute x0 -> x28, waiting for transfers between devices: none -> 35.4 us  [move(): return lax.ppermute(value, AXES, perm)]
    pallas_call x0 -> x5, Pallas kernels: none -> 33.4 us  [the longest x2 23.4 us: second_call(): pl.pallas_call(functools.partial(second_kernel, group, base), out_shape=j...]
    dot_general x2 -> x0, matrix products: 19.3 us -> none  [the longest x1 14.5 us: body(): jnp.einsum('sm,pml->psl', virt_whole, lax.all_to_all(outgoing, 'ao', spli...]
    mul x1 -> x0, local copies, waits for them, and re-layouts: 8.67 us -> none  [body(): return result * live_flat[None, :, None] * col_live[None, None, :]]
    reshape x1 -> x0, local copies, waits for them, and re-layouts: 7.46 us -> none  [body(): partial_rows.astype(jnp.bfloat16)]
  transfers between devices with their start and end apart: 3 -> 28, of which waited for: 2 -> 7; matrix products, arithmetic and copies ran while one was open for 14% -> 3% of each run, Pallas kernels for 0% -> 18%
where the time goes in v1:
time: 123 us; the launch traced here: 121 us
  starting transfers between devices  43.2 us (35%)
  waiting for transfers between devices  35.4 us (29%)
  Pallas kernels  33.4 us (27%)
  other arithmetic  4.58 us (4%)
  local copies, waits for them, and re-layouts  4.58 us (4%)
    ppermute x28, starting transfers between devices, move(): return lax.ppermute(value, AXES, perm)  43.2 us
    ppermute x28, waiting for transfers between devices, move(): return lax.ppermute(value, AXES, perm)  35.4 us
    pallas_call x2, Pallas kernels, second_call(): pl.pallas_call(functools.partial(second_kernel, group, base), out_shape=j...  23.4 us
    pallas_call x2, Pallas kernels, first_call(): pl.pallas_call(functools.partial(first_kernel, group), out_shape=(shape,...  10 us
    unnamed x24, local copies, waits for them, and re-layouts  3.07 us
  transfers between devices with their start and end apart: 28, of which 7 were waited for; matrix products, arithmetic and copies ran while one was open for 3% of the time, Pallas kernels for 18%

profile of v1, /device:TPU:1, one launch (start us, length us, event | category | flops | bytes accessed | tf_op | source)
XLA Modules:
  0.0 121.5 jit_solution(2817187263320591223)
XLA Ops:
  0.0 0.7 convert_element_type.29
  0.7 0.1 convert_element_type.30
  0.8 0.7 fusion.13
  1.5 0.1 dynamic_slice.30
  1.6 1.0 multiply_multiply_fusion.1
  2.6 2.1 %collective-permute-start.2 = (bf16[16,2688]{1,0:T(8,128)(2,1)S(1)}, bf16[16,2688]{1,0:T(8,128)(2,1)S(1)}, u32[]{:S(2)}, u32[]{:S(2)}) collective-permute-start(bf16[16,2688]{1,0:T(8,128)(2,1)S(1)} %get-tuple-element.29), channel_id=1, source_target_pairs={{0,2},{1,3},{2,4},{3,5},{4,6},{5,7},{6,0},{7,1},{8,10},{9,11},{10,... | collective-permute-start | bytes 258056 | tf_op jit(solution)/shard_map/ppermute | solution.py:42
  4.7 1.3 %collective-permute-start = (bf16[16,2688]{1,0:T(8,128)(2,1)S(1)}, bf16[16,2688]{1,0:T(8,128)(2,1)S(1)}, u32[]{:S(2)}, u32[]{:S(2)}) collective-permute-start(bf16[16,2688]{1,0:T(8,128)(2,1)S(1)} %get-tuple-element.30), channel_id=1, source_target_pairs={{0,6},{1,7},{2,0},{3,1},{4,2},{5,3},{6,4},{7,5},{8,14},{9,15},{10,... | collective-permute-start | bytes 258056 | tf_op jit(solution)/shard_map/ppermute | solution.py:42
  6.1 1.6 %collective-permute-start.1 = (bf16[16,2688]{1,0:T(8,128)(2,1)S(1)}, bf16[16,2688]{1,0:T(8,128)(2,1)S(1)}, u32[]{:S(2)}, u32[]{:S(2)}) collective-permute-start(bf16[16,2688]{1,0:T(8,128)(2,1)S(1)} %get-tuple-element.31), channel_id=1, source_target_pairs={{0,4},{1,5},{2,6},{3,7},{4,0},{5,1},{6,2},{7,3},{8,12},{9,13},{10,... | collective-permute-start | bytes 258056 | tf_op jit(solution)/shard_map/ppermute | solution.py:42
  7.7 1.3 %fusion.16 = (bf16[2,2,4,128,128]{4,3,2,1,0:T(8,128)(2,1)S(1)}, bf16[2,2,4,128,128]{4,3,2,1,0:T(8,128)(2,1)S(1)}) fusion(bf16[4,2,4,128,128]{4,3,2,1,0:T(8,128)(2,1)} %param.7), kind=kLoop, calls=%fused_computation.44 | loop fusion | bytes 2097152 | tf_op jit(solution)/shard_map/slice | solution.py:215
  9.0 0.9 collective-permute-start.24
  10.0 1.1 collective-permute-done.1
  11.1 0.0 collective-permute-done.2
  11.2 3.7 %collective-permute-start.7 = (bf16[4,16,512]{2,1,0:T(8,128)(2,1)S(1)}, bf16[4,16,512]{2,1,0:T(8,128)(2,1)S(1)}, u32[]{:S(2)}, u32[]{:S(2)}) collective-permute-start(bf16[4,16,512]{2,1,0:T(8,128)(2,1)S(1)} %constant_dynamic-slice_fusion), channel_id=1, source_target_pairs={{0,16},{1,65},{2,18},{3,67},{4,20},{5,69},{6,22},{7,71},{8,24},{9,... | collective-permute-start | bytes 196616 | tf_op jit(solution)/shard_map/ppermute | solution.py:42
  14.9 0.7 collective-permute-start.6
  15.6 2.0 %collective-permute-start.16 = (bf16[64,2048]{1,0:T(8,128)(2,1)S(1)}, bf16[64,2048]{1,0:T(8,128)(2,1)S(1)}, u32[]{:S(2)}, u32[]{:S(2)}) collective-permute-start(bf16[64,2048]{1,0:T(8,128)(2,1)S(1)} %bitcast.33), channel_id=1, source_target_pairs={{0,24},{1,97},{2,26},{3,99},{4,28},{5,101},{6,30},{7,103},{8,0},{9... | collective-permute-start | bytes 786440 | tf_op jit(solution)/shard_map/ppermute | solution.py:42
  17.7 0.0 collective-permute-start.15
  17.7 0.0 collective-permute-done.7
  17.7 0.7 collective-permute-start.14
  18.3 1.3 %collective-permute-done.6 = bf16[4,16,512]{2,1,0:T(8,128)(2,1)S(1)} collective-permute-done((bf16[4,16,512]{2,1,0:T(8,128)(2,1)S(1)}, bf16[4,16,512]{2,1,0:T(8,128)(2,1)S(1)}, u32[]{:S(2)}, u32[]{:S(2)}) %collective-permute-start.6) | collective-permute-done | bytes 65568 | tf_op jit(solution)/shard_map/ppermute | solution.py:42
  19.6 0.7 collective-permute-start.8
  20.3 4.4 %collective-permute-done.8 = bf16[4,16,512]{2,1,0:T(8,128)(2,1)S(1)} collective-permute-done((bf16[4,16,512]{2,1,0:T(8,128)(2,1)S(1)}, bf16[4,16,512]{2,1,0:T(8,128)(2,1)S(1)}, u32[]{:S(2)}, u32[]{:S(2)}) %collective-permute-start.8) | collective-permute-done | bytes 65568 | tf_op jit(solution)/shard_map/ppermute | solution.py:42
  24.8 1.7 %collective-permute-start.3 = (bf16[2,2,4,128,128]{4,3,2,1,0:T(8,128)(2,1)S(1)}, bf16[2,2,4,128,128]{4,3,2,1,0:T(8,128)(2,1)S(1)}, u32[]{:S(2)}, u32[]{:S(2)}) collective-permute-start(bf16[2,2,4,128,128]{4,3,2,1,0:T(8,128)(2,1)S(1)} %get-tuple-element.26.refs_0_), channel_id=1, source_target_pairs={{0,2},{1,7},{2,4},{3,1},{4,6},{5,3},{6,0},{7,5},{8,10},{9,15},{10,... | collective-permute-start | bytes 1572872 | tf_op jit(solution)/shard_map/ppermute | solution.py:42
  26.6 3.0 %collective-permute-start.10 = (bf16[4,4,16,512]{3,2,1,0:T(8,128)(2,1)S(1)}, bf16[4,4,16,512]{3,2,1,0:T(8,128)(2,1)S(1)}, u32[]{:S(2)}, u32[]{:S(2)}) collective-permute-start(bf16[4,4,16,512]{3,2,1,0:T(8,128)(2,1)S(1)} %get-tuple-element.28), channel_id=1, source_target_pairs={{0,64},{1,17},{2,66},{3,19},{4,68},{5,21},{6,70},{7,23},{8,72},{9,... | collective-permute-start | bytes 786440 | tf_op jit(solution)/shard_map/ppermute | solution.py:42
  29.6 0.0 collective-permute-done.15
  29.6 0.4 collective-permute-start.9
  30.0 0.0 collective-permute-done.24.refs_1_
  30.0 0.0 collective-permute-start.25
  30.0 0.0 collective-permute-done.14
  30.0 0.1 pad_maximum_fusion.1.refs_0_
  30.1 2.3 %collective-permute-start.19 = (bf16[256,2048]{1,0:T(8,128)(2,1)S(1)}, bf16[256,2048]{1,0:T(8,128)(2,1)S(1)}, u32[]{:S(2)}, u32[]{:S(2)}) collective-permute-start(bf16[256,2048]{1,0:T(8,128)(2,1)S(1)} %pad_maximum_fusion.1.refs_0_), channel_id=1, source_target_pairs={{0,96},{1,25},{2,98},{3,27},{4,100},{5,29},{6,102},{7,31},{8,104},... | collective-permute-start | bytes 3145736 | tf_op jit(solution)/shard_map/ppermute | solution.py:42
  32.5 1.2 collective-permute-done.10
  33.7 3.0 %collective-permute-start.18 = (bf16[256,2048]{1,0:T(8,128)(2,1)S(1)}, bf16[256,2048]{1,0:T(8,128)(2,1)S(1)}, u32[]{:S(2)}, u32[]{:S(2)}) collective-permute-start(bf16[256,2048]{1,0:T(8,128)(2,1)S(1)} %pad_maximum_fusion.1.refs_0_), channel_id=1, source_target_pairs={{0,64},{1,17},{2,66},{3,19},{4,68},{5,21},{6,70},{7,23},{8,72},{9,... | collective-permute-start | bytes 3145736 | tf_op jit(solution)/shard_map/ppermute | solution.py:42
  36.6 0.8 collective-permute-start.11
  37.4 21.6 %collective-permute-done.11 = bf16[4,4,16,512]{3,2,1,0:T(8,128)(2,1)S(1)} collective-permute-done((bf16[4,4,16,512]{3,2,1,0:T(8,128)(2,1)S(1)}, bf16[4,4,16,512]{3,2,1,0:T(8,128)(2,1)S(1)}, u32[]{:S(2)}, u32[]{:S(2)}) %collective-permute-start.11) | collective-permute-done | bytes 262176 | tf_op jit(solution)/shard_map/ppermute | solution.py:42
  59.1 0.9 collective-permute-start.17
  60.0 0.0 collective-permute-done.3.refs_1_
  60.0 0.0 collective-permute-start.4
  60.0 0.1 pad_maximum_fusion.refs_4_
  60.1 0.0 copy-start.1
  60.1 5.9 %collective-permute-start.12 = (bf16[4,4,4,16,512]{4,3,2,1,0:T(8,128)(2,1)S(1)}, bf16[4,4,4,16,512]{4,3,2,1,0:T(8,128)(2,1)}, u32[]{:S(2)}, u32[]{:S(2)}) collective-permute-start(bf16[4,4,4,16,512]{4,3,2,1,0:T(8,128)(2,1)S(1)} %pad_maximum_fusion.refs_4_), channel_id=1, source_target_pairs={{0,1},{1,0},{2,3},{3,2},{4,5},{5,4},{6,7},{7,6},{8,9},{9,8},{10,11... | collective-permute-start | bytes 3145736 | tf_op jit(solution)/shard_map/ppermute | solution.py:42
  66.0 2.4 %collective-permute-done.4.refs_2_ = bf16[2,2,4,128,128]{4,3,2,1,0:T(8,128)(2,1)} collective-permute-done((bf16[2,2,4,128,128]{4,3,2,1,0:T(8,128)(2,1)S(1)}, bf16[2,2,4,128,128]{4,3,2,1,0:T(8,128)(2,1)}, u32[]{:S(2)}, u32[]{:S(2)}) %collective-permute-start.4) | collective-permute-done | bytes 524320 | tf_op jit(solution)/shard_map/ppermute | solution.py:42
  68.4 5.9 %collective-permute-start.20 = (bf16[256,2048]{1,0:T(8,128)(2,1)S(1)}, bf16[256,2048]{1,0:T(8,128)(2,1)}, u32[]{:S(2)}, u32[]{:S(2)}) collective-permute-start(bf16[256,2048]{1,0:T(8,128)(2,1)S(1)} %pad_maximum_fusion.1.refs_0_), channel_id=1, source_target_pairs={{0,1},{1,0},{2,3},{3,2},{4,5},{5,4},{6,7},{7,6},{8,9},{9,8},{10,11... | collective-permute-start | bytes 3145736 | tf_op jit(solution)/shard_map/ppermute | solution.py:42
  74.3 1.7 %collective-permute-start.26 = (bf16[2,2,4,128,128]{4,3,2,1,0:T(8,128)(2,1)}, bf16[2,2,4,128,128]{4,3,2,1,0:T(8,128)(2,1)}, u32[]{:S(2)}, u32[]{:S(2)}) collective-permute-start(bf16[2,2,4,128,128]{4,3,2,1,0:T(8,128)(2,1)} %collective-permute-done.25.refs_2_), channel_id=1, source_target_pairs={{0,2},{1,7},{2,4},{3,1},{4,6},{5,3},{6,0},{7,5},{8,10},{9,15},{10,... | collective-permute-start | bytes 1572872 | tf_op jit(solution)/shard_map/ppermute | solution.py:42
  76.1 1.0 copy-done.3
  77.1 0.1 collective-permute-start.5
  77.1 0.7 pad_add_fusion.place
  77.8 1.2 %fusion.14 = s32[4,1,8]{2,1,0:T(1,128)} fusion(bf16[7,16,2688]{2,1,0:T(8,128)(2,1)} %copy-done.9, s32[]{:T(128)S(6)} %select_n.61, s32[]{:T(128)S(6)} %add.106), kind=kLoop, calls=%fused_computation.41 | loop fusion | flops 32 | bytes 200 | tf_op jit(solution)/shard_map/convert_element_type | solution.py:205
  79.0 0.0 collective-permute-done.17.refs_1_
  79.0 0.7 collective-permute-start.23
  79.7 0.0 collective-permute-start.22
  79.7 3.2 %collective-permute-done.26.refs_3_ = bf16[2,2,4,128,128]{4,3,2,1,0:T(8,128)(2,1)} collective-permute-done((bf16[2,2,4,128,128]{4,3,2,1,0:T(8,128)(2,1)}, bf16[2,2,4,128,128]{4,3,2,1,0:T(8,128)(2,1)}, u32[]{:S(2)}, u32[]{:S(2)}) %collective-permute-start.26) | collective-permute-done | bytes 524320 | tf_op jit(solution)/shard_map/ppermute | solution.py:42
  83.0 2.1 %collective-permute-start.21 = (bf16[256,2048]{1,0:T(8,128)(2,1)}, bf16[256,2048]{1,0:T(8,128)(2,1)}, u32[]{:S(2)}, u32[]{:S(2)}) collective-permute-start(bf16[256,2048]{1,0:T(8,128)(2,1)} %collective-permute-done.17.refs_1_), channel_id=1, source_target_pairs={{0,1},{1,0},{2,3},{3,2},{4,5},{5,4},{6,7},{7,6},{8,9},{9,8},{10,11... | collective-permute-start | bytes 3145736 | tf_op jit(solution)/shard_map/ppermute | solution.py:42
  85.1 5.0 %shard_map.56 = (bf16[2,4,256,256]{3,2,1,0:T(8,128)(2,1)}, bf16[2,4,256,256]{3,2,1,0:T(8,128)(2,1)}) custom-call(s32[4]{0:T(128)} %pad_add_fusion.place, s32[4,8]{1,0:T(4,128)} %bitcast.43, bf16[2,2,4,128,128]{4,3,2,1,0:T(8,128)(2,1)} %copy-done.5, bf16[2,2,4,128,128]{4,3,2,1,0:T(8,128)(2,1)} %collective-permute-done.24.refs_1_, ...), custom_call_target="tpu_custom_call" | custom-call | flops 1073741824 | bytes 6291456 | tf_op jit(solution)/shard_map/pallas_call | solution.py:89
  90.2 0.6 collective-permute-start.27
  90.7 5.0 %shard_map.55 = (bf16[2,4,256,256]{3,2,1,0:T(8,128)(2,1)}, bf16[2,4,256,256]{3,2,1,0:T(8,128)(2,1)}) custom-call(s32[4]{0:T(128)} %pad_add_fusion.place, s32[4,8]{1,0:T(4,128)} %bitcast.44, bf16[2,2,4,128,128]{4,3,2,1,0:T(8,128)(2,1)} %copy-done.4, bf16[2,2,4,128,128]{4,3,2,1,0:T(8,128)(2,1)} %copy-done.8, ...), custom_call_target="tpu_custom_call" | custom-call | flops 1073741824 | bytes 6291456 | tf_op jit(solution)/shard_map/pallas_call | solution.py:89
  95.7 0.0 collective-permute-done.20.refs_4_
  95.7 0.2 collective-permute-start.13
  95.9 0.0 collective-permute-done.23.refs_7_
  95.9 0.0 collective-permute-done.22.refs_6_
  95.9 0.0 collective-permute-done.21.refs_5_
  95.9 1.0 copy-done.7
  96.9 11.7 %shard_map.58.refs_8_ = f32[4,16,4,2,16,256]{5,4,3,2,1,0:T(8,128)} custom-call(s32[4]{0:T(128)} %pad_add_fusion.place, bf16[2,4,256,256]{3,2,1,0:T(8,128)(2,1)} %get-tuple-element.23.keep, bf16[2,4,256,256]{3,2,1,0:T(8,128)(2,1)} %copy-done.7, bf16[256,2048]{1,0:T(8,128)(2,1)} %copy-done, ...), custom_call_target="tpu_custom_call", output_to_operand_aliasing={{}: (11, {})} | custom-call | flops 4294967296 | bytes 14680064 | tf_op jit(solution)/shard_map/pallas_call | solution.py:149
  108.6 1.0 copy-done.6
  109.6 11.7 %shard_map.59 = f32[4,16,4,2,16,256]{5,4,3,2,1,0:T(8,128)} custom-call(s32[4]{0:T(128)} %pad_add_fusion.place, bf16[2,4,256,256]{3,2,1,0:T(8,128)(2,1)} %get-tuple-element.21.keep, bf16[2,4,256,256]{3,2,1,0:T(8,128)(2,1)} %copy-done.6, bf16[256,2048]{1,0:T(8,128)(2,1)} %copy-done, ...), custom_call_target="tpu_custom_call", output_to_operand_aliasing={{}: (11, {})} | custom-call | flops 4294967296 | bytes 14680064 | tf_op jit(solution)/shard_map/pallas_call | solution.py:149
  (40 shorter events, 0.3 us)
Async XLA Ops:
  2.6 8.5 %collective-permute-start.2 = (bf16[16,2688]{1,0:T(8,128)(2,1)S(1)}, bf16[16,2688]{1,0:T(8,128)(2,1)S(1)}, u32[]{:S(2)}, u32[]{:S(2)}) collective-permute-start(bf16[16,2688]{1,0:T(8,128)(2,1)S(1)} %get-tuple-element.29), channel_id=1, source_target_pairs={{0,2},{1,3},{2,4},{3,5},{4,6},{5,7},{6,0},{7,1},{8,10},{9,11},{10,... | collective-permute-start | bytes 258056 | tf_op jit(solution)/shard_map/ppermute | solution.py:42
  4.7 5.2 %collective-permute-start = (bf16[16,2688]{1,0:T(8,128)(2,1)S(1)}, bf16[16,2688]{1,0:T(8,128)(2,1)S(1)}, u32[]{:S(2)}, u32[]{:S(2)}) collective-permute-start(bf16[16,2688]{1,0:T(8,128)(2,1)S(1)} %get-tuple-element.30), channel_id=1, source_target_pairs={{0,6},{1,7},{2,0},{3,1},{4,2},{5,3},{6,4},{7,5},{8,14},{9,15},{10,... | collective-permute-start | bytes 258056 | tf_op jit(solution)/shard_map/ppermute | solution.py:42
  6.1 5.0 %collective-permute-start.1 = (bf16[16,2688]{1,0:T(8,128)(2,1)S(1)}, bf16[16,2688]{1,0:T(8,128)(2,1)S(1)}, u32[]{:S(2)}, u32[]{:S(2)}) collective-permute-start(bf16[16,2688]{1,0:T(8,128)(2,1)S(1)} %get-tuple-element.31), channel_id=1, source_target_pairs={{0,4},{1,5},{2,6},{3,7},{4,0},{5,1},{6,2},{7,3},{8,12},{9,13},{10,... | collective-permute-start | bytes 258056 | tf_op jit(solution)/shard_map/ppermute | solution.py:42
  9.0 21.0 %copy-start.5 = (bf16[2,2,4,128,128]{4,3,2,1,0:T(8,128)(2,1)}, bf16[2,2,4,128,128]{4,3,2,1,0:T(8,128)(2,1)S(1)}, u32[]{:S(2)}) copy-start(bf16[2,2,4,128,128]{4,3,2,1,0:T(8,128)(2,1)S(1)} %get-tuple-element.25.refs_0_) | copy-start | bytes 1572868
  9.0 21.1 %copy-start.4 = (bf16[2,2,4,128,128]{4,3,2,1,0:T(8,128)(2,1)}, bf16[2,2,4,128,128]{4,3,2,1,0:T(8,128)(2,1)S(1)}, u32[]{:S(2)}) copy-start(bf16[2,2,4,128,128]{4,3,2,1,0:T(8,128)(2,1)S(1)} %get-tuple-element.26.refs_0_) | copy-start | bytes 1572868
  9.0 21.0 %collective-permute-start.24 = (bf16[2,2,4,128,128]{4,3,2,1,0:T(8,128)(2,1)S(1)}, bf16[2,2,4,128,128]{4,3,2,1,0:T(8,128)(2,1)}, u32[]{:S(2)}, u32[]{:S(2)}) collective-permute-start(bf16[2,2,4,128,128]{4,3,2,1,0:T(8,128)(2,1)S(1)} %get-tuple-element.25.refs_0_), channel_id=1, source_target_pairs={{0,2},{1,7},{2,4},{3,1},{4,6},{5,3},{6,0},{7,5},{8,10},{9,15},{10,... | collective-permute-start | bytes 1572872 | tf_op jit(solution)/shard_map/ppermute | solution.py:42
  11.2 18.8 %copy-start.9 = (bf16[7,16,2688]{2,1,0:T(8,128)(2,1)}, bf16[7,16,2688]{2,1,0:T(8,128)(2,1)S(1)}, u32[]{:S(2)}) copy-start(bf16[7,16,2688]{2,1,0:T(8,128)(2,1)S(1)} %bitcast_dynamic-update-slice_fusion.2) | copy-start | bytes 1806340
  11.2 6.5 %collective-permute-start.7 = (bf16[4,16,512]{2,1,0:T(8,128)(2,1)S(1)}, bf16[4,16,512]{2,1,0:T(8,128)(2,1)S(1)}, u32[]{:S(2)}, u32[]{:S(2)}) collective-permute-start(bf16[4,16,512]{2,1,0:T(8,128)(2,1)S(1)} %constant_dynamic-slice_fusion), channel_id=1, source_target_pairs={{0,16},{1,65},{2,18},{3,67},{4,20},{5,69},{6,22},{7,71},{8,24},{9,... | collective-permute-start | bytes 196616 | tf_op jit(solution)/shard_map/ppermute | solution.py:42
  14.9 4.7 %collective-permute-start.6 = (bf16[4,16,512]{2,1,0:T(8,128)(2,1)S(1)}, bf16[4,16,512]{2,1,0:T(8,128)(2,1)S(1)}, u32[]{:S(2)}, u32[]{:S(2)}) collective-permute-start(bf16[4,16,512]{2,1,0:T(8,128)(2,1)S(1)} %constant_dynamic-slice_fusion), channel_id=1, source_target_pairs={{0,8},{1,33},{2,10},{3,35},{4,12},{5,37},{6,14},{7,39},{8,16},{9,4... | collective-permute-start | bytes 196616 | tf_op jit(solution)/shard_map/ppermute | solution.py:42
  15.6 10.9 %collective-permute-start.16 = (bf16[64,2048]{1,0:T(8,128)(2,1)S(1)}, bf16[64,2048]{1,0:T(8,128)(2,1)S(1)}, u32[]{:S(2)}, u32[]{:S(2)}) collective-permute-start(bf16[64,2048]{1,0:T(8,128)(2,1)S(1)} %bitcast.33), channel_id=1, source_target_pairs={{0,24},{1,97},{2,26},{3,99},{4,28},{5,101},{6,30},{7,103},{8,0},{9... | collective-permute-start | bytes 786440 | tf_op jit(solution)/shard_map/ppermute | solution.py:42
  17.7 11.9 %collective-permute-start.15 = (bf16[64,2048]{1,0:T(8,128)(2,1)S(1)}, bf16[64,2048]{1,0:T(8,128)(2,1)S(1)}, u32[]{:S(2)}, u32[]{:S(2)}) collective-permute-start(bf16[64,2048]{1,0:T(8,128)(2,1)S(1)} %bitcast.34), channel_id=1, source_target_pairs={{0,16},{1,65},{2,18},{3,67},{4,20},{5,69},{6,22},{7,71},{8,24},{9,... | collective-permute-start | bytes 786440 | tf_op jit(solution)/shard_map/ppermute | solution.py:42
  17.7 12.3 %collective-permute-start.14 = (bf16[64,2048]{1,0:T(8,128)(2,1)S(1)}, bf16[64,2048]{1,0:T(8,128)(2,1)S(1)}, u32[]{:S(2)}, u32[]{:S(2)}) collective-permute-start(bf16[64,2048]{1,0:T(8,128)(2,1)S(1)} %bitcast.35), channel_id=1, source_target_pairs={{0,8},{1,33},{2,10},{3,35},{4,12},{5,37},{6,14},{7,39},{8,16},{9,4... | collective-permute-start | bytes 786440 | tf_op jit(solution)/shard_map/ppermute | solution.py:42
  19.6 5.2 %collective-permute-start.8 = (bf16[4,16,512]{2,1,0:T(8,128)(2,1)S(1)}, bf16[4,16,512]{2,1,0:T(8,128)(2,1)S(1)}, u32[]{:S(2)}, u32[]{:S(2)}) collective-permute-start(bf16[4,16,512]{2,1,0:T(8,128)(2,1)S(1)} %constant_dynamic-slice_fusion), channel_id=1, source_target_pairs={{0,24},{1,97},{2,26},{3,99},{4,28},{5,101},{6,30},{7,103},{8,0},{9... | collective-permute-start | bytes 196616 | tf_op jit(solution)/shard_map/ppermute | solution.py:42
  24.8 35.2 %collective-permute-start.3 = (bf16[2,2,4,128,128]{4,3,2,1,0:T(8,128)(2,1)S(1)}, bf16[2,2,4,128,128]{4,3,2,1,0:T(8,128)(2,1)S(1)}, u32[]{:S(2)}, u32[]{:S(2)}) collective-permute-start(bf16[2,2,4,128,128]{4,3,2,1,0:T(8,128)(2,1)S(1)} %get-tuple-element.26.refs_0_), channel_id=1, source_target_pairs={{0,2},{1,7},{2,4},{3,1},{4,6},{5,3},{6,0},{7,5},{8,10},{9,15},{10,... | collective-permute-start | bytes 1572872 | tf_op jit(solution)/shard_map/ppermute | solution.py:42
  26.6 7.1 %collective-permute-start.10 = (bf16[4,4,16,512]{3,2,1,0:T(8,128)(2,1)S(1)}, bf16[4,4,16,512]{3,2,1,0:T(8,128)(2,1)S(1)}, u32[]{:S(2)}, u32[]{:S(2)}) collective-permute-start(bf16[4,4,16,512]{3,2,1,0:T(8,128)(2,1)S(1)} %get-tuple-element.28), channel_id=1, source_target_pairs={{0,64},{1,17},{2,66},{3,19},{4,68},{5,21},{6,70},{7,23},{8,72},{9,... | collective-permute-start | bytes 786440 | tf_op jit(solution)/shard_map/ppermute | solution.py:42
  29.6 7.1 %collective-permute-start.9 = (bf16[4,4,16,512]{3,2,1,0:T(8,128)(2,1)S(1)}, bf16[4,4,16,512]{3,2,1,0:T(8,128)(2,1)S(1)}, u32[]{:S(2)}, u32[]{:S(2)}) collective-permute-start(bf16[4,4,16,512]{3,2,1,0:T(8,128)(2,1)S(1)} %get-tuple-element.28), channel_id=1, source_target_pairs={{0,32},{1,9},{2,34},{3,11},{4,36},{5,13},{6,38},{7,15},{8,40},{9,1... | collective-permute-start | bytes 786440 | tf_op jit(solution)/shard_map/ppermute | solution.py:42
  30.0 30.2 %collective-permute-start.25 = (bf16[2,2,4,128,128]{4,3,2,1,0:T(8,128)(2,1)}, bf16[2,2,4,128,128]{4,3,2,1,0:T(8,128)(2,1)}, u32[]{:S(2)}, u32[]{:S(2)}) collective-permute-start(bf16[2,2,4,128,128]{4,3,2,1,0:T(8,128)(2,1)} %collective-permute-done.24.refs_1_), channel_id=1, source_target_pairs={{0,2},{1,7},{2,4},{3,1},{4,6},{5,3},{6,0},{7,5},{8,10},{9,15},{10,... | collective-permute-start | bytes 1572872 | tf_op jit(solution)/shard_map/ppermute | solution.py:42
  30.1 60.0 %copy-start = (bf16[256,2048]{1,0:T(8,128)(2,1)}, bf16[256,2048]{1,0:T(8,128)(2,1)S(1)}, u32[]{:S(2)}) copy-start(bf16[256,2048]{1,0:T(8,128)(2,1)S(1)} %pad_maximum_fusion.1.refs_0_) | copy-start | bytes 3145732
  30.1 44.2 %collective-permute-start.19 = (bf16[256,2048]{1,0:T(8,128)(2,1)S(1)}, bf16[256,2048]{1,0:T(8,128)(2,1)S(1)}, u32[]{:S(2)}, u32[]{:S(2)}) collective-permute-start(bf16[256,2048]{1,0:T(8,128)(2,1)S(1)} %pad_maximum_fusion.1.refs_0_), channel_id=1, source_target_pairs={{0,96},{1,25},{2,98},{3,27},{4,100},{5,29},{6,102},{7,31},{8,104},... | collective-permute-start | bytes 3145736 | tf_op jit(solution)/shard_map/ppermute | solution.py:42
  33.7 42.4 %collective-permute-start.18 = (bf16[256,2048]{1,0:T(8,128)(2,1)S(1)}, bf16[256,2048]{1,0:T(8,128)(2,1)S(1)}, u32[]{:S(2)}, u32[]{:S(2)}) collective-permute-start(bf16[256,2048]{1,0:T(8,128)(2,1)S(1)} %pad_maximum_fusion.1.refs_0_), channel_id=1, source_target_pairs={{0,64},{1,17},{2,66},{3,19},{4,68},{5,21},{6,70},{7,23},{8,72},{9,... | collective-permute-start | bytes 3145736 | tf_op jit(solution)/shard_map/ppermute | solution.py:42
  36.6 22.4 %collective-permute-start.11 = (bf16[4,4,16,512]{3,2,1,0:T(8,128)(2,1)S(1)}, bf16[4,4,16,512]{3,2,1,0:T(8,128)(2,1)S(1)}, u32[]{:S(2)}, u32[]{:S(2)}) collective-permute-start(bf16[4,4,16,512]{3,2,1,0:T(8,128)(2,1)S(1)} %get-tuple-element.28), channel_id=1, source_target_pairs={{0,96},{1,25},{2,98},{3,27},{4,100},{5,29},{6,102},{7,31},{8,104},... | collective-permute-start | bytes 786440 | tf_op jit(solution)/shard_map/ppermute | solution.py:42
  59.1 20.0 %collective-permute-start.17 = (bf16[256,2048]{1,0:T(8,128)(2,1)S(1)}, bf16[256,2048]{1,0:T(8,128)(2,1)}, u32[]{:S(2)}, u32[]{:S(2)}) collective-permute-start(bf16[256,2048]{1,0:T(8,128)(2,1)S(1)} %pad_maximum_fusion.1.refs_0_), channel_id=1, source_target_pairs={{0,32},{1,9},{2,34},{3,11},{4,36},{5,13},{6,38},{7,15},{8,40},{9,1... | collective-permute-start | bytes 3145736 | tf_op jit(solution)/shard_map/ppermute | solution.py:42
  60.0 16.1 %copy-start.8 = (bf16[2,2,4,128,128]{4,3,2,1,0:T(8,128)(2,1)}, bf16[2,2,4,128,128]{4,3,2,1,0:T(8,128)(2,1)S(1)}, u32[]{:S(2)}) copy-start(bf16[2,2,4,128,128]{4,3,2,1,0:T(8,128)(2,1)S(1)} %collective-permute-done.3.refs_1_) | copy-start | bytes 1572868
  60.0 8.4 %collective-permute-start.4 = (bf16[2,2,4,128,128]{4,3,2,1,0:T(8,128)(2,1)S(1)}, bf16[2,2,4,128,128]{4,3,2,1,0:T(8,128)(2,1)}, u32[]{:S(2)}, u32[]{:S(2)}) collective-permute-start(bf16[2,2,4,128,128]{4,3,2,1,0:T(8,128)(2,1)S(1)} %collective-permute-done.3.refs_1_), channel_id=1, source_target_pairs={{0,2},{1,7},{2,4},{3,1},{4,6},{5,3},{6,0},{7,5},{8,10},{9,15},{10,... | collective-permute-start | bytes 1572872 | tf_op jit(solution)/shard_map/ppermute | solution.py:42
  60.1 25.0 %copy-start.1 = (bf16[4,4,4,16,512]{4,3,2,1,0:T(8,128)(2,1)}, bf16[4,4,4,16,512]{4,3,2,1,0:T(8,128)(2,1)S(1)}, u32[]{:S(2)}) copy-start(bf16[4,4,4,16,512]{4,3,2,1,0:T(8,128)(2,1)S(1)} %pad_maximum_fusion.refs_4_) | copy-start | bytes 3145732
  60.1 19.6 %collective-permute-start.12 = (bf16[4,4,4,16,512]{4,3,2,1,0:T(8,128)(2,1)S(1)}, bf16[4,4,4,16,512]{4,3,2,1,0:T(8,128)(2,1)}, u32[]{:S(2)}, u32[]{:S(2)}) collective-permute-start(bf16[4,4,4,16,512]{4,3,2,1,0:T(8,128)(2,1)S(1)} %pad_maximum_fusion.refs_4_), channel_id=1, source_target_pairs={{0,1},{1,0},{2,3},{3,2},{4,5},{5,4},{6,7},{7,6},{8,9},{9,8},{10,11... | collective-permute-start | bytes 3145736 | tf_op jit(solution)/shard_map/ppermute | solution.py:42
  68.4 27.3 %collective-permute-start.20 = (bf16[256,2048]{1,0:T(8,128)(2,1)S(1)}, bf16[256,2048]{1,0:T(8,128)(2,1)}, u32[]{:S(2)}, u32[]{:S(2)}) collective-permute-start(bf16[256,2048]{1,0:T(8,128)(2,1)S(1)} %pad_maximum_fusion.1.refs_0_), channel_id=1, source_target_pairs={{0,1},{1,0},{2,3},{3,2},{4,5},{5,4},{6,7},{7,6},{8,9},{9,8},{10,11... | collective-permute-start | bytes 3145736 | tf_op jit(solution)/shard_map/ppermute | solution.py:42
  74.3 15.8 %copy-start.2 = (bf16[256,2048]{1,0:T(8,128)(2,1)}, bf16[256,2048]{1,0:T(8,128)(2,1)S(1)}, u32[]{:S(2)}) copy-start(bf16[256,2048]{1,0:T(8,128)(2,1)S(1)} %collective-permute-done.19.refs_3_) | copy-start | bytes 3145732
  74.3 8.6 %collective-permute-start.26 = (bf16[2,2,4,128,128]{4,3,2,1,0:T(8,128)(2,1)}, bf16[2,2,4,128,128]{4,3,2,1,0:T(8,128)(2,1)}, u32[]{:S(2)}, u32[]{:S(2)}) collective-permute-start(bf16[2,2,4,128,128]{4,3,2,1,0:T(8,128)(2,1)} %collective-permute-done.25.refs_2_), channel_id=1, source_target_pairs={{0,2},{1,7},{2,4},{3,1},{4,6},{5,3},{6,0},{7,5},{8,10},{9,15},{10,... | collective-permute-start | bytes 1572872 | tf_op jit(solution)/shard_map/ppermute | solution.py:42
  76.1 1.0 copy-start.3
  77.1 13.1 %collective-permute-start.5 = (bf16[2,2,4,128,128]{4,3,2,1,0:T(8,128)(2,1)}, bf16[2,2,4,128,128]{4,3,2,1,0:T(8,128)(2,1)}, u32[]{:S(2)}, u32[]{:S(2)}) collective-permute-start(bf16[2,2,4,128,128]{4,3,2,1,0:T(8,128)(2,1)} %collective-permute-done.4.refs_2_), channel_id=1, source_target_pairs={{0,2},{1,7},{2,4},{3,1},{4,6},{5,3},{6,0},{7,5},{8,10},{9,15},{10,... | collective-permute-start | bytes 1572872 | tf_op jit(solution)/shard_map/ppermute | solution.py:42
  79.0 16.8 %collective-permute-start.23 = (bf16[256,2048]{1,0:T(8,128)(2,1)S(1)}, bf16[256,2048]{1,0:T(8,128)(2,1)}, u32[]{:S(2)}, u32[]{:S(2)}) collective-permute-start(bf16[256,2048]{1,0:T(8,128)(2,1)S(1)} %collective-permute-done.19.refs_3_), channel_id=1, source_target_pairs={{0,1},{1,0},{2,3},{3,2},{4,5},{5,4},{6,7},{7,6},{8,9},{9,8},{10,11... | collective-permute-start | bytes 3145736 | tf_op jit(solution)/shard_map/ppermute | solution.py:42
  79.7 16.2 %collective-permute-start.22 = (bf16[256,2048]{1,0:T(8,128)(2,1)}, bf16[256,2048]{1,0:T(8,128)(2,1)}, u32[]{:S(2)}, u32[]{:S(2)}) collective-permute-start(bf16[256,2048]{1,0:T(8,128)(2,1)} %copy-done.3), channel_id=1, source_target_pairs={{0,1},{1,0},{2,3},{3,2},{4,5},{5,4},{6,7},{7,6},{8,9},{9,8},{10,11... | collective-permute-start | bytes 3145736 | tf_op jit(solution)/shard_map/ppermute | solution.py:42
  83.0 12.9 %collective-permute-start.21 = (bf16[256,2048]{1,0:T(8,128)(2,1)}, bf16[256,2048]{1,0:T(8,128)(2,1)}, u32[]{:S(2)}, u32[]{:S(2)}) collective-permute-start(bf16[256,2048]{1,0:T(8,128)(2,1)} %collective-permute-done.17.refs_1_), channel_id=1, source_target_pairs={{0,1},{1,0},{2,3},{3,2},{4,5},{5,4},{6,7},{7,6},{8,9},{9,8},{10,11... | collective-permute-start | bytes 3145736 | tf_op jit(solution)/shard_map/ppermute | solution.py:42
  90.2 5.7 %collective-permute-start.27 = (bf16[2,4,256,256]{3,2,1,0:T(8,128)(2,1)}, bf16[2,4,256,256]{3,2,1,0:T(8,128)(2,1)S(1)}, u32[]{:S(2)}, u32[]{:S(2)}) collective-permute-start(bf16[2,4,256,256]{3,2,1,0:T(8,128)(2,1)} %get-tuple-element.24), channel_id=1, source_target_pairs={{0,1},{1,0},{2,3},{3,2},{4,5},{5,4},{6,7},{7,6},{8,9},{9,8},{10,11... | collective-permute-start | bytes 3145736 | tf_op jit(solution)/shard_map/ppermute | solution.py:42
  95.7 13.0 %collective-permute-start.13 = (bf16[2,4,256,256]{3,2,1,0:T(8,128)(2,1)}, bf16[2,4,256,256]{3,2,1,0:T(8,128)(2,1)S(1)}, u32[]{:S(2)}, u32[]{:S(2)}) collective-permute-start(bf16[2,4,256,256]{3,2,1,0:T(8,128)(2,1)} %get-tuple-element.22), channel_id=1, source_target_pairs={{0,1},{1,0},{2,3},{3,2},{4,5},{5,4},{6,7},{7,6},{8,9},{9,8},{10,11... | collective-permute-start | bytes 3145736 | tf_op jit(solution)/shard_map/ppermute | solution.py:42
  95.9 1.0 copy-start.7
  108.6 1.0 copy-start.6

commit v2 on v0

v2 whole, which is shorter than its diff:
```python
import jax
import jax.numpy as jnp
from jax import lax
from jax.experimental import pallas as pl
from jax.experimental.pallas import tpu as pltpu
from jax.sharding import PartitionSpec as P

AXES = ("ri", "ao")
VMEM_LIMIT = 56 * 1024 * 1024
SMEM = pl.BlockSpec(memory_space=pltpu.SMEM)
ANY = pl.BlockSpec(memory_space=pl.ANY)


def pairs(step):
    out = []
    for z in range(4):
        for y in range(4):
            for x in range(4):
                for c in range(2):
                    tz, ty, tx, tc = step(z, y, x, c)
                    target = (((tz % 4) * 4 + ty % 4) * 4 + tx % 4) * 2 + tc
                    out.append((((z * 4 + y) * 4 + x) * 2 + c, target))
    return out


CORE = pairs(lambda z, y, x, c: (z, y, x, 1 - c))
RING_X = pairs(lambda z, y, x, c: (z, y, x + 1 - 2 * c, c))
SHIFT_X = [None] + [pairs(lambda z, y, x, c, d=d: (z, y, x + d, c)) for d in (1, 2, 3)]
STAGE_A = [None] + [
    pairs(lambda z, y, x, c, d=d: (z + d * c, y + d * (1 - c), x, c)) for d in (1, 2, 3)
]
STAGE_B = [None] + [
    pairs(lambda z, y, x, c, d=d: (z + d * (1 - c), y + d * c, x, c)) for d in (1, 2, 3)
]
AHEAD, PACE = 3, 2
KINDS = tuple((far, mine) for far in (0, 1, 3, 2) for mine in (True, False))


def move(value, perm):
    return lax.ppermute(value, AXES, perm)


def spread(value, stage):
    return [value] + [move(value, stage[d]) for d in (1, 2, 3)]


def after(value, *earlier):
    return lax.optimization_barrier((value,) + earlier)[0]


def kernel(place, near, *refs):
    mine_chunks, other_chunks, refs = refs[:4], refs[4:8], refs[8:]
    sources = [
        [(r[0], 0), (r[0], 160)] + [(r[1], 0), (r[1], 160)] + [(r[2], 0), (r[3], 0)] + [(r[4], 0), (r[4], 160)]
        for r in (refs[:5], refs[5:10])
    ]
    mine, other = [[src[2 * far : 2 * far + 2] for far in range(4)] for src in sources]
    out, chunks, occ_in, occ, first, held, result, chunk_sems, occ_sems, in_sems, out_sems = refs[10:]
    z, y, x, c = place[0], place[1], place[2], place[3]

    def block(core, far, b):
        return ((z - jnp.where(core == 0, far, b)) & 3) * 4 + ((y - jnp.where(core == 0, b, far)) & 3)

    blocks = [
        pltpu.make_async_copy((mine_chunks + other_chunks)[i], chunks.at[i], chunk_sems.at[i])
        for i in range(8)
    ]
    greens, fetches = [], []
    for far in range(4):
        for h, (ref, top) in enumerate(mine[far]):
            greens.append(
                pltpu.make_async_copy(
                    ref.at[pl.ds(top + 128, 32)], occ_in.at[far, pl.ds(h * 32, 32)], occ_sems.at[far, h]
                )
            )
    for i, (far, own) in enumerate(KINDS):
        fetches.append(
            [
                pltpu.make_async_copy(
                    ref.at[pl.ds(top, 128)], held.at[i, pl.ds(h * 128, 128)], in_sems.at[i, h]
                )
                for h, (ref, top) in enumerate((mine if own else other)[far])
            ]
        )
    queue = [[copy] for copy in blocks] + fetches

    def ask(count):
        for _ in range(min(count, len(queue))):
            for copy in queue.pop(0):
                copy.start()

    for copy in greens:
        copy.start()
    ask(AHEAD)

    for far in range(4):
        for copy in greens[2 * far : 2 * far + 2]:
            copy.wait()
        for b in range(4):
            at = block(c, far, b)
            for g in range(8):
                occ[at, g * 16 : (g + 1) * 16, :] = occ_in[
                    far, b * 16 : (b + 1) * 16, g * 256 : (g + 1) * 256
                ]

    for i in range(8):
        core = c if i < 4 else 1 - c
        at = (x + jnp.where(core == 0, -(i % 4), i % 4)) & 3
        blocks[i].wait()
        ask(PACE if i % 2 else 1)
        for atom in range(2):
            right = jnp.concatenate(
                [occ[near[at, core * 8 + atom * 4 + j]] for j in range(4)], axis=0
            )
            left = jnp.concatenate(
                [
                    jnp.concatenate([chunks[i, p, atom, j] for j in range(4)], axis=1)
                    for p in range(4)
                ],
                axis=0,
            )
            done = jnp.dot(left, right, preferred_element_type=jnp.float32).astype(jnp.bfloat16)
            rows = pl.ds(pl.multiple_of((core * 4 + at) * 256 + atom * 128, 128), 128)
            for p in range(4):
                first[p, rows, :] = done[p * 128 : (p + 1) * 128]

    def stores(i):
        far, own = KINDS[i]
        core = c if own else 1 - c
        return [
            pltpu.make_async_copy(
                result.at[i % 2, :, b], out.at[:, block(core, far, b), :, core], out_sems.at[i % 2, b]
            )
            for b in range(4)
        ]

    for i in range(8):
        for copy in fetches[i]:
            copy.wait()
        ask(1)
        if i >= 2:
            for copy in stores(i - 2):
                copy.wait()
        for p in range(4):
            done = jnp.dot(held[i], first[p], preferred_element_type=jnp.float32)
            result[i % 2, p] = done.reshape(4, 4, 16, 256)
        for copy in stores(i):
            copy.start()
    for i in (6, 7):
        for copy in stores(i):
            copy.wait()


def contract(place, near, mine_chunks, other_chunks, mine, other):
    return pl.pallas_call(
        kernel,
        out_shape=jax.ShapeDtypeStruct((4, 16, 4, 2, 16, 256), jnp.float32),
        in_specs=[SMEM, SMEM] + [ANY] * 18,
        out_specs=ANY,
        scratch_shapes=[
            pltpu.VMEM((8, 4, 2, 4, 128, 128), jnp.bfloat16),
            pltpu.VMEM((4, 64, 2048), jnp.bfloat16),
            pltpu.VMEM((16, 128, 256), jnp.bfloat16),
            pltpu.VMEM((4, 2048, 256), jnp.bfloat16),
            pltpu.VMEM((8, 256, 2048), jnp.bfloat16),
            pltpu.VMEM((2, 4, 4, 4, 16, 256), jnp.float32),
            pltpu.SemaphoreType.DMA((8,)),
            pltpu.SemaphoreType.DMA((4, 2)),
            pltpu.SemaphoreType.DMA((8, 2)),
            pltpu.SemaphoreType.DMA((2, 4)),
        ],
        compiler_params=pltpu.CompilerParams(vmem_limit_bytes=VMEM_LIMIT),
        cost_estimate=pl.CostEstimate(
            flops=10 * 2**30, bytes_accessed=26 * 2**20, transcendentals=0
        ),
    )(place, near, *mine_chunks, *other_chunks, *mine, *other)


def body(three_center, neighbors, block_sizes, green_occ, green_virt):
    ri, ao = lax.axis_index("ri"), lax.axis_index("ao")
    z, y, x, c = ri // 4, ri % 4, ao // 2, ao % 2
    place = jnp.stack([z, y, x, c]).astype(jnp.int32)

    position = jnp.arange(128, dtype=jnp.int32)
    live = (position[None, :] < block_sizes[:, None]).astype(jnp.bfloat16).reshape(2048)
    live_rows = lax.dynamic_slice_in_dim(live, (ri * 8 + ao) * 16, 16, 0)
    mask = live_rows[:, None] * live[None, :]
    occ = green_occ * mask
    virt = green_virt * mask

    sides = [
        jnp.concatenate([occ[:, b * 512 + k * 256 : b * 512 + k * 256 + 256] for b in range(4)], axis=1)
        for k in range(2)
    ]
    near = lax.dynamic_update_slice(
        jnp.zeros((16, 128), jnp.bfloat16), neighbors.reshape(1, 8).astype(jnp.bfloat16), (0, c * 8)
    )
    own, away = jnp.where(c == 0, sides[0], sides[1]), jnp.where(c == 0, sides[1], sides[0])
    swapped = move(jnp.concatenate([away, near], axis=1), CORE)
    near = near + swapped[:, 1024:]
    rows = [
        jnp.where(c == 0, own, swapped[:, :1024]),
        jnp.where(c == 0, swapped[:, :1024], own),
    ]
    virt = jnp.concatenate(
        [virt[:, b * 512 + k * 256 : b * 512 + k * 256 + 256] for k in range(2) for b in range(4)], axis=1
    )

    def pack(d):
        to = lax.rem(x + d, 4) * 256
        return jnp.concatenate(
            [virt] + [lax.dynamic_slice_in_dim(r, to, 256, 1) for r in rows] + [near], axis=1
        )

    arrived = [pack(0)] + [move(pack((4 - t) % 4), SHIFT_X[4 - t]) for t in (1, 2, 3)]
    packs = lax.dynamic_slice_in_dim(jnp.stack(arrived + arrived[:3]), lax.rem(4 - x, 4), 4, 0)
    near = packs[:, 0, 2560:2576].astype(jnp.int32)

    greens = jnp.concatenate(
        [packs[:, :, :2048].reshape(64, 2048)]
        + [jnp.concatenate([packs[b, :, 2048:2560] for b in range(4)], axis=1)]
    )
    chunks = [three_center]
    other_chunks = [move(three_center, CORE)]
    first_other = other_chunks[0]
    chunks.append(move(after(three_center, arrived[1]), RING_X))
    other_chunks.append(move(chunks[1], CORE))
    chunks.append(move(chunks[1], RING_X))
    other_chunks.append(move(chunks[2], CORE))
    greens = spread(after(greens, other_chunks[0]), STAGE_A)
    greens = jnp.concatenate(
        [g[rows] for pair in (greens[:2], greens[2:]) for rows in (slice(0, 64), slice(64, 80)) for g in pair]
    )
    first_green = move(greens, CORE)
    chunks.append(move(after(chunks[2], other_chunks[1], first_green), RING_X))
    other_chunks.append(move(chunks[3], CORE))
    up, down = move(greens, STAGE_B[1]), move(greens, STAGE_B[3])
    beyond = [move(up[:160], STAGE_B[1]), move(down[160:], STAGE_B[3])]
    mine = [greens, up] + beyond + [down]
    other = [first_green] + [move(after(up, other_chunks[2]), CORE)] + [move(b, CORE) for b in beyond] + [move(after(down, other_chunks[2]), CORE)]

    return contract(place, near, chunks, other_chunks, mine, other).reshape(4, 2048, 256)


def solution(mesh):
    in_specs = (
        P("ri", "ao", None, None, None),
        P("ao", None),
        P(),
        P(("ri", "ao"), None),
        P(("ri", "ao"), None),
    )
    out_specs = P("ri", None, "ao")
    return jax.shard_map(body, mesh=mesh, in_specs=in_specs, out_specs=out_specs, check_vma=False)
```

time: 209 us -> 87.3 us (0.42)
  waiting for transfers between devices: 138 us -> 26.2 us
  starting transfers between devices: 4.77 us -> 36.6 us
  local copies, waits for them, and re-layouts: 31 us -> 2.44 us
  matrix products: 19.3 us -> 0 us
  Pallas kernels: 0 us -> 17.4 us
  between operations: 13.4 us -> 0.63 us
  other arithmetic: 1.42 us -> 3.81 us
    all_gather x2 -> x0, waiting for transfers between devices: 74.1 us -> none  [the longest x1 74.1 us: whole_occ(): return lax.all_gather(green_occ, ('ri', 'ao'), axis=0, tiled=True)]
    all_to_all x1 -> x0, waiting for transfers between devices: 62.7 us -> none  [body(): lax.all_to_all(outgoing, 'ao', split_axis=2, concat_axis=1, tiled=True)]
    ppermute x0 -> x23, starting transfers between devices: none -> 36.6 us  [move(): return lax.ppermute(value, AXES, perm)]
    ppermute x0 -> x23, waiting for transfers between devices: none -> 26.2 us  [move(): return lax.ppermute(value, AXES, perm)]
    dot_general x2 -> x0, matrix products: 19.3 us -> none  [the longest x1 14.5 us: body(): jnp.einsum('sm,pml->psl', virt_whole, lax.all_to_all(outgoing, 'ao', spli...]
    pallas_call x0 -> x1, Pallas kernels: none -> 17.4 us  [contract(): pl.pallas_call(kernel, out_shape=jax.ShapeDtypeStruct((4, 16, 4, 2, 16, 2...]
    mul x1 -> x0, local copies, waits for them, and re-layouts: 8.67 us -> none  [body(): return result * live_flat[None, :, None] * col_live[None, None, :]]
    reshape x1 -> x0, local copies, waits for them, and re-layouts: 7.46 us -> none  [body(): partial_rows.astype(jnp.bfloat16)]
  transfers between devices with their start and end apart: 3 -> 23, of which waited for: 2 -> 8; matrix products, arithmetic and copies ran while one was open for 14% -> 2% of each run, Pallas kernels for 0% -> 0%
where the time goes in v2:
time: 87.3 us; the launch traced here: 87.1 us
  starting transfers between devices  36.6 us (42%)
  waiting for transfers between devices  26.2 us (30%)
  Pallas kernels  17.4 us (20%)
  other arithmetic  3.81 us (4%)
  local copies, waits for them, and re-layouts  2.44 us (3%)
    ppermute x23, starting transfers between devices, move(): return lax.ppermute(value, AXES, perm)  36.6 us
    ppermute x23, waiting for transfers between devices, move(): return lax.ppermute(value, AXES, perm)  26.2 us
    pallas_call x1, Pallas kernels, contract(): pl.pallas_call(kernel, out_shape=jax.ShapeDtypeStruct((4, 16, 4, 2, 16, 2...  17.4 us
  transfers between devices with their start and end apart: 23, of which 8 were waited for; matrix products, arithmetic and copies ran while one was open for 2% of the time, Pallas kernels for 0%

profile of v2, /device:TPU:1, one launch (start us, length us, event | category | flops | bytes accessed | tf_op | source)
XLA Modules:
  0.0 87.1 jit_solution(13807201724269860322)
XLA Ops:
  0.0 0.8 convert_element_type.32
  0.8 0.1 convert_element_type.33
  0.9 0.7 fusion.1
  1.6 0.1 dynamic_slice.30
  1.7 1.0 %multiply_multiply_fusion = (bf16[16,2048]{1,0:T(8,128)(2,1)S(1)}, bf16[16,2048]{1,0:T(8,128)(2,1)S(1)}) fusion(bf16[16,2048]{1,0:T(8,128)(2,1)} %param.8, bf16[2048]{0:T(1024)(128)(2,1)S(1)} %fusion.1, bf16[16]{0:T(256)(128)(2,1)S(1)} %dynamic_slice.30, bf16[16,2048]{1,0:T(8,128)(2,1)} %param.9), kind=kLoop, calls=%fused_computation.60 | loop fusion | flops 98304 | bytes 266272 | tf_op jit(solution)/shard_map/mul | solution.py:188
  2.7 0.3 dynamic_update_slice.5
  3.0 1.4 %collective-permute-start = (bf16[16,1152]{1,0:T(8,128)(2,1)S(1)}, bf16[16,1152]{1,0:T(8,128)(2,1)S(1)}, u32[]{:S(2)}, u32[]{:S(2)}) collective-permute-start(bf16[16,1152]{1,0:T(8,128)(2,1)S(1)} %pad_maximum_fusion), channel_id=1, source_target_pairs={{0,1},{1,0},{2,3},{3,2},{4,5},{5,4},{6,7},{7,6},{8,9},{9,8},{10,11... | collective-permute-start | bytes 110600 | tf_op jit(solution)/shard_map/ppermute | solution.py:40
  4.4 0.1 collective-permute-start.7
  4.6 0.7 collective-permute-done
  5.3 0.1 fusion.3
  5.4 0.2 add.56
  5.7 1.4 %collective-permute-start.3 = (bf16[16,2688]{1,0:T(8,128)(2,1)S(1)}, bf16[16,2688]{1,0:T(8,128)(2,1)S(1)}, u32[]{:S(2)}, u32[]{:S(2)}) collective-permute-start(bf16[16,2688]{1,0:T(8,128)(2,1)S(1)} %get-tuple-element.35), channel_id=1, source_target_pairs={{0,2},{1,3},{2,4},{3,5},{4,6},{5,7},{6,0},{7,1},{8,10},{9,11},{10,... | collective-permute-start | bytes 258056 | tf_op jit(solution)/shard_map/ppermute | solution.py:40
  7.1 2.5 %collective-permute-start.2 = (bf16[16,2688]{1,0:T(8,128)(2,1)S(1)}, bf16[16,2688]{1,0:T(8,128)(2,1)S(1)}, u32[]{:S(2)}, u32[]{:S(2)}) collective-permute-start(bf16[16,2688]{1,0:T(8,128)(2,1)S(1)} %get-tuple-element.36), channel_id=1, source_target_pairs={{0,4},{1,5},{2,6},{3,7},{4,0},{5,1},{6,2},{7,3},{8,12},{9,13},{10,... | collective-permute-start | bytes 258056 | tf_op jit(solution)/shard_map/ppermute | solution.py:40
  9.5 1.2 %collective-permute-start.1 = (bf16[16,2688]{1,0:T(8,128)(2,1)S(1)}, bf16[16,2688]{1,0:T(8,128)(2,1)S(1)}, u32[]{:S(2)}, u32[]{:S(2)}) collective-permute-start(bf16[16,2688]{1,0:T(8,128)(2,1)S(1)} %get-tuple-element.37), channel_id=1, source_target_pairs={{0,6},{1,7},{2,0},{3,1},{4,2},{5,3},{6,4},{7,5},{8,14},{9,15},{10,... | collective-permute-start | bytes 258056 | tf_op jit(solution)/shard_map/ppermute | solution.py:40
  10.7 2.2 %collective-permute-done.1 = bf16[16,2688]{1,0:T(8,128)(2,1)S(1)} collective-permute-done((bf16[16,2688]{1,0:T(8,128)(2,1)S(1)}, bf16[16,2688]{1,0:T(8,128)(2,1)S(1)}, u32[]{:S(2)}, u32[]{:S(2)}) %collective-permute-start.1) | collective-permute-done | bytes 86048 | tf_op jit(solution)/shard_map/ppermute | solution.py:40
  12.9 0.9 %collective-permute-done.2 = bf16[16,2688]{1,0:T(8,128)(2,1)S(1)} collective-permute-done((bf16[16,2688]{1,0:T(8,128)(2,1)S(1)}, bf16[16,2688]{1,0:T(8,128)(2,1)S(1)}, u32[]{:S(2)}, u32[]{:S(2)}) %collective-permute-start.2) | collective-permute-done | bytes 86048 | tf_op jit(solution)/shard_map/ppermute | solution.py:40
  13.8 0.0 collective-permute-done.3
  13.9 0.0 copy-done.4
  13.9 1.5 %collective-permute-start.4 = (bf16[4,2,4,128,128]{4,3,2,1,0:T(8,128)(2,1)S(1)}, bf16[4,2,4,128,128]{4,3,2,1,0:T(8,128)(2,1)S(1)}, u32[]{:S(2)}, u32[]{:S(2)}) collective-permute-start(bf16[4,2,4,128,128]{4,3,2,1,0:T(8,128)(2,1)S(1)} %copy-done.4), channel_id=1, source_target_pairs={{0,2},{1,7},{2,4},{3,1},{4,6},{5,3},{6,0},{7,5},{8,10},{9,15},{10,... | collective-permute-start | bytes 3145736 | tf_op jit(solution)/shard_map/ppermute | solution.py:40
  15.5 0.0 collective-permute-done.7.refs_4_
  15.5 0.0 copy-start.5
  15.5 3.9 %collective-permute-start.10 = (bf16[80,2048]{1,0:T(8,128)(2,1)S(1)}, bf16[80,2048]{1,0:T(8,128)(2,1)S(1)}, u32[]{:S(2)}, u32[]{:S(2)}) collective-permute-start(bf16[80,2048]{1,0:T(8,128)(2,1)S(1)} %maximum_maximum_fusion), channel_id=1, source_target_pairs={{0,24},{1,97},{2,26},{3,99},{4,28},{5,101},{6,30},{7,103},{8,0},{9... | collective-permute-start | bytes 983048 | tf_op jit(solution)/shard_map/ppermute | solution.py:40
  19.4 0.0 collective-permute-start.9
  19.4 0.7 collective-permute-start.8
  20.2 7.7 %collective-permute-done.4.refs_1_ = bf16[4,2,4,128,128]{4,3,2,1,0:T(8,128)(2,1)S(1)} collective-permute-done((bf16[4,2,4,128,128]{4,3,2,1,0:T(8,128)(2,1)S(1)}, bf16[4,2,4,128,128]{4,3,2,1,0:T(8,128)(2,1)S(1)}, u32[]{:S(2)}, u32[]{:S(2)}) %collective-permute-start.4) | collective-permute-done | bytes 1048608 | tf_op jit(solution)/shard_map/ppermute | solution.py:40
  27.9 2.7 %collective-permute-start.5 = (bf16[4,2,4,128,128]{4,3,2,1,0:T(8,128)(2,1)S(1)}, bf16[4,2,4,128,128]{4,3,2,1,0:T(8,128)(2,1)S(1)}, u32[]{:S(2)}, u32[]{:S(2)}) collective-permute-start(bf16[4,2,4,128,128]{4,3,2,1,0:T(8,128)(2,1)S(1)} %collective-permute-done.4.refs_1_), channel_id=1, source_target_pairs={{0,2},{1,7},{2,4},{3,1},{4,6},{5,3},{6,0},{7,5},{8,10},{9,15},{10,... | collective-permute-start | bytes 3145736 | tf_op jit(solution)/shard_map/ppermute | solution.py:40
  30.6 0.0 collective-permute-done.8
  30.6 0.0 collective-permute-done.9
  30.7 0.0 collective-permute-done.10
  30.7 0.0 copy-done.5
  30.7 0.0 copy-start.2
  30.7 1.2 %collective-permute-start.11 = (bf16[320,2048]{1,0:T(8,128)(2,1)S(1)}, bf16[320,2048]{1,0:T(8,128)(2,1)S(1)}, u32[]{:S(2)}, u32[]{:S(2)}) collective-permute-start(bf16[320,2048]{1,0:T(8,128)(2,1)S(1)} %constant_dynamic-update-slice_fusion.51.refs_8_), channel_id=1, source_target_pairs={{0,1},{1,0},{2,3},{3,2},{4,5},{5,4},{6,7},{7,6},{8,9},{9,8},{10,11... | collective-permute-start | bytes 3932168 | tf_op jit(solution)/shard_map/ppermute | solution.py:40
  31.9 0.1 collective-permute-start.6
  32.0 2.2 %collective-permute-start.17 = (bf16[320,2048]{1,0:T(8,128)(2,1)S(1)}, bf16[320,2048]{1,0:T(8,128)(2,1)S(1)}, u32[]{:S(2)}, u32[]{:S(2)}) collective-permute-start(bf16[320,2048]{1,0:T(8,128)(2,1)S(1)} %constant_dynamic-update-slice_fusion.51.refs_8_), channel_id=1, source_target_pairs={{0,96},{1,25},{2,98},{3,27},{4,100},{5,29},{6,102},{7,31},{8,104},... | collective-permute-start | bytes 3932168 | tf_op jit(solution)/shard_map/ppermute | solution.py:40
  34.3 0.0 collective-permute-start.15
  34.3 8.0 %collective-permute-done.5.refs_2_ = bf16[4,2,4,128,128]{4,3,2,1,0:T(8,128)(2,1)S(1)} collective-permute-done((bf16[4,2,4,128,128]{4,3,2,1,0:T(8,128)(2,1)S(1)}, bf16[4,2,4,128,128]{4,3,2,1,0:T(8,128)(2,1)S(1)}, u32[]{:S(2)}, u32[]{:S(2)}) %collective-permute-start.5) | collective-permute-done | bytes 1048608 | tf_op jit(solution)/shard_map/ppermute | solution.py:40
  42.3 4.7 %collective-permute-start.13 = (bf16[4,2,4,128,128]{4,3,2,1,0:T(8,128)(2,1)S(1)}, bf16[4,2,4,128,128]{4,3,2,1,0:T(8,128)(2,1)S(1)}, u32[]{:S(2)}, u32[]{:S(2)}) collective-permute-start(bf16[4,2,4,128,128]{4,3,2,1,0:T(8,128)(2,1)S(1)} %collective-permute-done.5.refs_2_), channel_id=1, source_target_pairs={{0,1},{1,0},{2,3},{3,2},{4,5},{5,4},{6,7},{7,6},{8,9},{9,8},{10,11... | collective-permute-start | bytes 3145736 | tf_op jit(solution)/shard_map/ppermute | solution.py:40
  47.0 0.0 collective-permute-done.6.refs_5_
  47.0 0.0 collective-permute-done.11.refs_13_
  47.0 0.0 copy-start.3
  47.0 0.1 collective-permute-start.12
  47.1 0.9 %copy-done.8 = bf16[4,2,4,128,128]{4,3,2,1,0:T(8,128)(2,1)} copy-done((bf16[4,2,4,128,128]{4,3,2,1,0:T(8,128)(2,1)}, bf16[4,2,4,128,128]{4,3,2,1,0:T(8,128)(2,1)S(1)}, u32[]{:S(2)}) %copy-start.8) | copy-done | bytes 1048600
  48.1 0.4 copy-done.3
  48.4 0.4 collective-permute-done.17.refs_12_
  48.9 3.5 %collective-permute-start.18 = (bf16[160,2048]{1,0:T(8,128)(2,1)S(1)}, bf16[160,2048]{1,0:T(8,128)(2,1)}, u32[]{:S(2)}, u32[]{:S(2)}) collective-permute-start(bf16[160,2048]{1,0:T(8,128)(2,1)S(1)} %slice.165), channel_id=1, source_target_pairs={{0,96},{1,25},{2,98},{3,27},{4,100},{5,29},{6,102},{7,31},{8,104},... | collective-permute-start | bytes 1966088 | tf_op jit(solution)/shard_map/ppermute | solution.py:40
  52.4 0.0 collective-permute-done.15.refs_9_
  52.4 0.1 collective-permute-start.16
  52.5 0.0 collective-permute-done.13.refs_6_
  52.5 3.2 %collective-permute-start.22 = (bf16[320,2048]{1,0:T(8,128)(2,1)S(1)}, bf16[320,2048]{1,0:T(8,128)(2,1)}, u32[]{:S(2)}, u32[]{:S(2)}) collective-permute-start(bf16[320,2048]{1,0:T(8,128)(2,1)S(1)} %collective-permute-done.17.refs_12_), channel_id=1, source_target_pairs={{0,1},{1,0},{2,3},{3,2},{4,5},{5,4},{6,7},{7,6},{8,9},{9,8},{10,11... | collective-permute-start | bytes 3932168 | tf_op jit(solution)/shard_map/ppermute | solution.py:40
  55.7 0.1 collective-permute-start.19
  55.8 5.4 %collective-permute-done.12.refs_3_ = bf16[4,2,4,128,128]{4,3,2,1,0:T(8,128)(2,1)} collective-permute-done((bf16[4,2,4,128,128]{4,3,2,1,0:T(8,128)(2,1)S(1)}, bf16[4,2,4,128,128]{4,3,2,1,0:T(8,128)(2,1)}, u32[]{:S(2)}, u32[]{:S(2)}) %collective-permute-start.12) | collective-permute-done | bytes 1048608 | tf_op jit(solution)/shard_map/ppermute | solution.py:40
  61.2 2.1 %collective-permute-start.14 = (bf16[4,2,4,128,128]{4,3,2,1,0:T(8,128)(2,1)}, bf16[4,2,4,128,128]{4,3,2,1,0:T(8,128)(2,1)}, u32[]{:S(2)}, u32[]{:S(2)}) collective-permute-start(bf16[4,2,4,128,128]{4,3,2,1,0:T(8,128)(2,1)} %collective-permute-done.12.refs_3_), channel_id=1, source_target_pairs={{0,1},{1,0},{2,3},{3,2},{4,5},{5,4},{6,7},{7,6},{8,9},{9,8},{10,11... | collective-permute-start | bytes 3145736 | tf_op jit(solution)/shard_map/ppermute | solution.py:40
  63.2 0.0 collective-permute-done.18.refs_11_
  63.2 0.3 collective-permute-start.21
  63.5 0.0 collective-permute-done.16.refs_10_
  63.6 3.9 %collective-permute-start.20 = (bf16[160,2048]{1,0:T(8,128)(2,1)}, bf16[160,2048]{1,0:T(8,128)(2,1)}, u32[]{:S(2)}, u32[]{:S(2)}) collective-permute-start(bf16[160,2048]{1,0:T(8,128)(2,1)} %collective-permute-done.16.refs_10_), channel_id=1, source_target_pairs={{0,1},{1,0},{2,3},{3,2},{4,5},{5,4},{6,7},{7,6},{8,9},{9,8},{10,11... | collective-permute-start | bytes 1966088 | tf_op jit(solution)/shard_map/ppermute | solution.py:40
  67.5 0.6 pad_add_fusion.place
  68.1 0.6 fusion.2
  68.7 0.0 collective-permute-done.21.refs_16_
  68.7 0.8 collective-permute-done.20.refs_15_
  69.5 0.0 collective-permute-done.22.refs_17_
  69.5 0.0 collective-permute-done.19.refs_14_
  69.5 0.0 collective-permute-done.14.refs_7_
  69.6 17.4 %shard_map.55 = f32[4,16,4,2,16,256]{5,4,3,2,1,0:T(8,128)} custom-call(s32[4]{0:T(128)} %pad_add_fusion.place, s32[4,16]{1,0:T(4,128)} %bitcast.29, bf16[4,2,4,128,128]{4,3,2,1,0:T(8,128)(2,1)} %refs_0_.1, bf16[4,2,4,128,128]{4,3,2,1,0:T(8,128)(2,1)} %copy-done.6, bf16[4,2,4,128,128]{4,3,2,1,0:T(8,128)(2,1)} %copy-done.7, ...), custom_call_target="tpu_custom_call" | custom-call | flops 10737418240 | bytes 27262976 | tf_op jit(solution)/shard_map/pallas_call | solution.py:155
  (55 shorter events, 0.5 us)
Async XLA Ops:
  0.0 13.9 %copy-start.4 = (bf16[4,2,4,128,128]{4,3,2,1,0:T(8,128)(2,1)S(1)}, bf16[4,2,4,128,128]{4,3,2,1,0:T(8,128)(2,1)}, u32[]{:S(2)}) copy-start(bf16[4,2,4,128,128]{4,3,2,1,0:T(8,128)(2,1)} %refs_0_.1) | copy-start | bytes 3145732
  3.0 2.3 %collective-permute-start = (bf16[16,1152]{1,0:T(8,128)(2,1)S(1)}, bf16[16,1152]{1,0:T(8,128)(2,1)S(1)}, u32[]{:S(2)}, u32[]{:S(2)}) collective-permute-start(bf16[16,1152]{1,0:T(8,128)(2,1)S(1)} %pad_maximum_fusion), channel_id=1, source_target_pairs={{0,1},{1,0},{2,3},{3,2},{4,5},{5,4},{6,7},{7,6},{8,9},{9,8},{10,11... | collective-permute-start | bytes 110600 | tf_op jit(solution)/shard_map/ppermute | solution.py:40
  4.4 11.1 %collective-permute-start.7 = (bf16[4,2,4,128,128]{4,3,2,1,0:T(8,128)(2,1)}, bf16[4,2,4,128,128]{4,3,2,1,0:T(8,128)(2,1)S(1)}, u32[]{:S(2)}, u32[]{:S(2)}) collective-permute-start(bf16[4,2,4,128,128]{4,3,2,1,0:T(8,128)(2,1)} %refs_0_.1), channel_id=1, source_target_pairs={{0,1},{1,0},{2,3},{3,2},{4,5},{5,4},{6,7},{7,6},{8,9},{9,8},{10,11... | collective-permute-start | bytes 3145736 | tf_op jit(solution)/shard_map/ppermute | solution.py:40
  5.7 8.1 %collective-permute-start.3 = (bf16[16,2688]{1,0:T(8,128)(2,1)S(1)}, bf16[16,2688]{1,0:T(8,128)(2,1)S(1)}, u32[]{:S(2)}, u32[]{:S(2)}) collective-permute-start(bf16[16,2688]{1,0:T(8,128)(2,1)S(1)} %get-tuple-element.35), channel_id=1, source_target_pairs={{0,2},{1,3},{2,4},{3,5},{4,6},{5,7},{6,0},{7,1},{8,10},{9,11},{10,... | collective-permute-start | bytes 258056 | tf_op jit(solution)/shard_map/ppermute | solution.py:40
  7.1 6.7 %collective-permute-start.2 = (bf16[16,2688]{1,0:T(8,128)(2,1)S(1)}, bf16[16,2688]{1,0:T(8,128)(2,1)S(1)}, u32[]{:S(2)}, u32[]{:S(2)}) collective-permute-start(bf16[16,2688]{1,0:T(8,128)(2,1)S(1)} %get-tuple-element.36), channel_id=1, source_target_pairs={{0,4},{1,5},{2,6},{3,7},{4,0},{5,1},{6,2},{7,3},{8,12},{9,13},{10,... | collective-permute-start | bytes 258056 | tf_op jit(solution)/shard_map/ppermute | solution.py:40
  9.5 3.3 %collective-permute-start.1 = (bf16[16,2688]{1,0:T(8,128)(2,1)S(1)}, bf16[16,2688]{1,0:T(8,128)(2,1)S(1)}, u32[]{:S(2)}, u32[]{:S(2)}) collective-permute-start(bf16[16,2688]{1,0:T(8,128)(2,1)S(1)} %get-tuple-element.37), channel_id=1, source_target_pairs={{0,6},{1,7},{2,0},{3,1},{4,2},{5,3},{6,4},{7,5},{8,14},{9,15},{10,... | collective-permute-start | bytes 258056 | tf_op jit(solution)/shard_map/ppermute | solution.py:40
  13.9 14.0 %collective-permute-start.4 = (bf16[4,2,4,128,128]{4,3,2,1,0:T(8,128)(2,1)S(1)}, bf16[4,2,4,128,128]{4,3,2,1,0:T(8,128)(2,1)S(1)}, u32[]{:S(2)}, u32[]{:S(2)}) collective-permute-start(bf16[4,2,4,128,128]{4,3,2,1,0:T(8,128)(2,1)S(1)} %copy-done.4), channel_id=1, source_target_pairs={{0,2},{1,7},{2,4},{3,1},{4,6},{5,3},{6,0},{7,5},{8,10},{9,15},{10,... | collective-permute-start | bytes 3145736 | tf_op jit(solution)/shard_map/ppermute | solution.py:40
  15.5 15.2 %copy-start.5 = (bf16[4,2,4,128,128]{4,3,2,1,0:T(8,128)(2,1)}, bf16[4,2,4,128,128]{4,3,2,1,0:T(8,128)(2,1)S(1)}, u32[]{:S(2)}) copy-start(bf16[4,2,4,128,128]{4,3,2,1,0:T(8,128)(2,1)S(1)} %collective-permute-done.7.refs_4_) | copy-start | bytes 3145732
  15.5 15.1 %collective-permute-start.10 = (bf16[80,2048]{1,0:T(8,128)(2,1)S(1)}, bf16[80,2048]{1,0:T(8,128)(2,1)S(1)}, u32[]{:S(2)}, u32[]{:S(2)}) collective-permute-start(bf16[80,2048]{1,0:T(8,128)(2,1)S(1)} %maximum_maximum_fusion), channel_id=1, source_target_pairs={{0,24},{1,97},{2,26},{3,99},{4,28},{5,101},{6,30},{7,103},{8,0},{9... | collective-permute-start | bytes 983048 | tf_op jit(solution)/shard_map/ppermute | solution.py:40
  19.4 11.2 %collective-permute-start.9 = (bf16[80,2048]{1,0:T(8,128)(2,1)S(1)}, bf16[80,2048]{1,0:T(8,128)(2,1)S(1)}, u32[]{:S(2)}, u32[]{:S(2)}) collective-permute-start(bf16[80,2048]{1,0:T(8,128)(2,1)S(1)} %maximum_maximum_fusion), channel_id=1, source_target_pairs={{0,16},{1,65},{2,18},{3,67},{4,20},{5,69},{6,22},{7,71},{8,24},{9,... | collective-permute-start | bytes 983048 | tf_op jit(solution)/shard_map/ppermute | solution.py:40
  19.4 11.1 %collective-permute-start.8 = (bf16[80,2048]{1,0:T(8,128)(2,1)S(1)}, bf16[80,2048]{1,0:T(8,128)(2,1)S(1)}, u32[]{:S(2)}, u32[]{:S(2)}) collective-permute-start(bf16[80,2048]{1,0:T(8,128)(2,1)S(1)} %maximum_maximum_fusion), channel_id=1, source_target_pairs={{0,8},{1,33},{2,10},{3,35},{4,12},{5,37},{6,14},{7,39},{8,16},{9,4... | collective-permute-start | bytes 983048 | tf_op jit(solution)/shard_map/ppermute | solution.py:40
  27.9 21.0 %copy-start.6 = (bf16[4,2,4,128,128]{4,3,2,1,0:T(8,128)(2,1)}, bf16[4,2,4,128,128]{4,3,2,1,0:T(8,128)(2,1)S(1)}, u32[]{:S(2)}) copy-start(bf16[4,2,4,128,128]{4,3,2,1,0:T(8,128)(2,1)S(1)} %collective-permute-done.4.refs_1_) | copy-start | bytes 3145732
  27.9 14.4 %collective-permute-start.5 = (bf16[4,2,4,128,128]{4,3,2,1,0:T(8,128)(2,1)S(1)}, bf16[4,2,4,128,128]{4,3,2,1,0:T(8,128)(2,1)S(1)}, u32[]{:S(2)}, u32[]{:S(2)}) collective-permute-start(bf16[4,2,4,128,128]{4,3,2,1,0:T(8,128)(2,1)S(1)} %collective-permute-done.4.refs_1_), channel_id=1, source_target_pairs={{0,2},{1,7},{2,4},{3,1},{4,6},{5,3},{6,0},{7,5},{8,10},{9,15},{10,... | collective-permute-start | bytes 3145736 | tf_op jit(solution)/shard_map/ppermute | solution.py:40
  30.7 21.6 %copy-start.2 = (bf16[320,2048]{1,0:T(8,128)(2,1)}, bf16[320,2048]{1,0:T(8,128)(2,1)S(1)}, u32[]{:S(2)}) copy-start(bf16[320,2048]{1,0:T(8,128)(2,1)S(1)} %constant_dynamic-update-slice_fusion.51.refs_8_) | copy-start | bytes 3932164
  30.7 16.3 %collective-permute-start.11 = (bf16[320,2048]{1,0:T(8,128)(2,1)S(1)}, bf16[320,2048]{1,0:T(8,128)(2,1)S(1)}, u32[]{:S(2)}, u32[]{:S(2)}) collective-permute-start(bf16[320,2048]{1,0:T(8,128)(2,1)S(1)} %constant_dynamic-update-slice_fusion.51.refs_8_), channel_id=1, source_target_pairs={{0,1},{1,0},{2,3},{3,2},{4,5},{5,4},{6,7},{7,6},{8,9},{9,8},{10,11... | collective-permute-start | bytes 3932168 | tf_op jit(solution)/shard_map/ppermute | solution.py:40
  31.9 15.1 %collective-permute-start.6 = (bf16[4,2,4,128,128]{4,3,2,1,0:T(8,128)(2,1)S(1)}, bf16[4,2,4,128,128]{4,3,2,1,0:T(8,128)(2,1)S(1)}, u32[]{:S(2)}, u32[]{:S(2)}) collective-permute-start(bf16[4,2,4,128,128]{4,3,2,1,0:T(8,128)(2,1)S(1)} %collective-permute-done.4.refs_1_), channel_id=1, source_target_pairs={{0,1},{1,0},{2,3},{3,2},{4,5},{5,4},{6,7},{7,6},{8,9},{9,8},{10,11... | collective-permute-start | bytes 3145736 | tf_op jit(solution)/shard_map/ppermute | solution.py:40
  32.0 16.8 %collective-permute-start.17 = (bf16[320,2048]{1,0:T(8,128)(2,1)S(1)}, bf16[320,2048]{1,0:T(8,128)(2,1)S(1)}, u32[]{:S(2)}, u32[]{:S(2)}) collective-permute-start(bf16[320,2048]{1,0:T(8,128)(2,1)S(1)} %constant_dynamic-update-slice_fusion.51.refs_8_), channel_id=1, source_target_pairs={{0,96},{1,25},{2,98},{3,27},{4,100},{5,29},{6,102},{7,31},{8,104},... | collective-permute-start | bytes 3932168 | tf_op jit(solution)/shard_map/ppermute | solution.py:40
  34.3 18.1 %collective-permute-start.15 = (bf16[320,2048]{1,0:T(8,128)(2,1)S(1)}, bf16[320,2048]{1,0:T(8,128)(2,1)S(1)}, u32[]{:S(2)}, u32[]{:S(2)}) collective-permute-start(bf16[320,2048]{1,0:T(8,128)(2,1)S(1)} %constant_dynamic-update-slice_fusion.51.refs_8_), channel_id=1, source_target_pairs={{0,32},{1,9},{2,34},{3,11},{4,36},{5,13},{6,38},{7,15},{8,40},{9,1... | collective-permute-start | bytes 3932168 | tf_op jit(solution)/shard_map/ppermute | solution.py:40
  42.3 21.2 %copy-start.7 = (bf16[4,2,4,128,128]{4,3,2,1,0:T(8,128)(2,1)}, bf16[4,2,4,128,128]{4,3,2,1,0:T(8,128)(2,1)S(1)}, u32[]{:S(2)}) copy-start(bf16[4,2,4,128,128]{4,3,2,1,0:T(8,128)(2,1)S(1)} %collective-permute-done.5.refs_2_) | copy-start | bytes 3145732
  42.3 10.2 %collective-permute-start.13 = (bf16[4,2,4,128,128]{4,3,2,1,0:T(8,128)(2,1)S(1)}, bf16[4,2,4,128,128]{4,3,2,1,0:T(8,128)(2,1)S(1)}, u32[]{:S(2)}, u32[]{:S(2)}) collective-permute-start(bf16[4,2,4,128,128]{4,3,2,1,0:T(8,128)(2,1)S(1)} %collective-permute-done.5.refs_2_), channel_id=1, source_target_pairs={{0,1},{1,0},{2,3},{3,2},{4,5},{5,4},{6,7},{7,6},{8,9},{9,8},{10,11... | collective-permute-start | bytes 3145736 | tf_op jit(solution)/shard_map/ppermute | solution.py:40
  47.0 1.0 %copy-start.8 = (bf16[4,2,4,128,128]{4,3,2,1,0:T(8,128)(2,1)}, bf16[4,2,4,128,128]{4,3,2,1,0:T(8,128)(2,1)S(1)}, u32[]{:S(2)}) copy-start(bf16[4,2,4,128,128]{4,3,2,1,0:T(8,128)(2,1)S(1)} %collective-permute-done.6.refs_5_) | copy-start | bytes 3145732
  47.0 1.4 %copy-start.3 = (bf16[320,2048]{1,0:T(8,128)(2,1)}, bf16[320,2048]{1,0:T(8,128)(2,1)S(1)}, u32[]{:S(2)}) copy-start(bf16[320,2048]{1,0:T(8,128)(2,1)S(1)} %collective-permute-done.11.refs_13_) | copy-start | bytes 3932164
  47.0 14.1 %collective-permute-start.12 = (bf16[4,2,4,128,128]{4,3,2,1,0:T(8,128)(2,1)S(1)}, bf16[4,2,4,128,128]{4,3,2,1,0:T(8,128)(2,1)}, u32[]{:S(2)}, u32[]{:S(2)}) collective-permute-start(bf16[4,2,4,128,128]{4,3,2,1,0:T(8,128)(2,1)S(1)} %collective-permute-done.5.refs_2_), channel_id=1, source_target_pairs={{0,2},{1,7},{2,4},{3,1},{4,6},{5,3},{6,0},{7,5},{8,10},{9,15},{10,... | collective-permute-start | bytes 3145736 | tf_op jit(solution)/shard_map/ppermute | solution.py:40
  48.8 3.7 %copy-start = (bf16[320,2048]{1,0:T(8,128)(2,1)}, bf16[320,2048]{1,0:T(8,128)(2,1)S(1)}, u32[]{:S(2)}) copy-start(bf16[320,2048]{1,0:T(8,128)(2,1)S(1)} %collective-permute-done.17.refs_12_) | copy-start | bytes 3932164
  48.9 14.4 %collective-permute-start.18 = (bf16[160,2048]{1,0:T(8,128)(2,1)S(1)}, bf16[160,2048]{1,0:T(8,128)(2,1)}, u32[]{:S(2)}, u32[]{:S(2)}) collective-permute-start(bf16[160,2048]{1,0:T(8,128)(2,1)S(1)} %slice.165), channel_id=1, source_target_pairs={{0,96},{1,25},{2,98},{3,27},{4,100},{5,29},{6,102},{7,31},{8,104},... | collective-permute-start | bytes 1966088 | tf_op jit(solution)/shard_map/ppermute | solution.py:40
  52.4 17.2 %copy-start.1 = (bf16[320,2048]{1,0:T(8,128)(2,1)}, bf16[320,2048]{1,0:T(8,128)(2,1)S(1)}, u32[]{:S(2)}) copy-start(bf16[320,2048]{1,0:T(8,128)(2,1)S(1)} %collective-permute-done.15.refs_9_) | copy-start | bytes 3932164
  52.4 11.1 %collective-permute-start.16 = (bf16[160,2048]{1,0:T(8,128)(2,1)S(1)}, bf16[160,2048]{1,0:T(8,128)(2,1)}, u32[]{:S(2)}, u32[]{:S(2)}) collective-permute-start(bf16[160,2048]{1,0:T(8,128)(2,1)S(1)} %slice.164), channel_id=1, source_target_pairs={{0,32},{1,9},{2,34},{3,11},{4,36},{5,13},{6,38},{7,15},{8,40},{9,1... | collective-permute-start | bytes 1966088 | tf_op jit(solution)/shard_map/ppermute | solution.py:40
  52.5 11.0 %copy-start.9 = (bf16[4,2,4,128,128]{4,3,2,1,0:T(8,128)(2,1)}, bf16[4,2,4,128,128]{4,3,2,1,0:T(8,128)(2,1)S(1)}, u32[]{:S(2)}) copy-start(bf16[4,2,4,128,128]{4,3,2,1,0:T(8,128)(2,1)S(1)} %collective-permute-done.13.refs_6_) | copy-start | bytes 3145732
  52.5 17.0 %collective-permute-start.22 = (bf16[320,2048]{1,0:T(8,128)(2,1)S(1)}, bf16[320,2048]{1,0:T(8,128)(2,1)}, u32[]{:S(2)}, u32[]{:S(2)}) collective-permute-start(bf16[320,2048]{1,0:T(8,128)(2,1)S(1)} %collective-permute-done.17.refs_12_), channel_id=1, source_target_pairs={{0,1},{1,0},{2,3},{3,2},{4,5},{5,4},{6,7},{7,6},{8,9},{9,8},{10,11... | collective-permute-start | bytes 3932168 | tf_op jit(solution)/shard_map/ppermute | solution.py:40
  55.7 13.9 %collective-permute-start.19 = (bf16[320,2048]{1,0:T(8,128)(2,1)S(1)}, bf16[320,2048]{1,0:T(8,128)(2,1)}, u32[]{:S(2)}, u32[]{:S(2)}) collective-permute-start(bf16[320,2048]{1,0:T(8,128)(2,1)S(1)} %collective-permute-done.15.refs_9_), channel_id=1, source_target_pairs={{0,1},{1,0},{2,3},{3,2},{4,5},{5,4},{6,7},{7,6},{8,9},{9,8},{10,11... | collective-permute-start | bytes 3932168 | tf_op jit(solution)/shard_map/ppermute | solution.py:40
  61.2 8.4 %collective-permute-start.14 = (bf16[4,2,4,128,128]{4,3,2,1,0:T(8,128)(2,1)}, bf16[4,2,4,128,128]{4,3,2,1,0:T(8,128)(2,1)}, u32[]{:S(2)}, u32[]{:S(2)}) collective-permute-start(bf16[4,2,4,128,128]{4,3,2,1,0:T(8,128)(2,1)} %collective-permute-done.12.refs_3_), channel_id=1, source_target_pairs={{0,1},{1,0},{2,3},{3,2},{4,5},{5,4},{6,7},{7,6},{8,9},{9,8},{10,11... | collective-permute-start | bytes 3145736 | tf_op jit(solution)/shard_map/ppermute | solution.py:40
  63.2 5.4 %collective-permute-start.21 = (bf16[160,2048]{1,0:T(8,128)(2,1)}, bf16[160,2048]{1,0:T(8,128)(2,1)}, u32[]{:S(2)}, u32[]{:S(2)}) collective-permute-start(bf16[160,2048]{1,0:T(8,128)(2,1)} %collective-permute-done.18.refs_11_), channel_id=1, source_target_pairs={{0,1},{1,0},{2,3},{3,2},{4,5},{5,4},{6,7},{7,6},{8,9},{9,8},{10,11... | collective-permute-start | bytes 1966088 | tf_op jit(solution)/shard_map/ppermute | solution.py:40
  63.6 6.0 %collective-permute-start.20 = (bf16[160,2048]{1,0:T(8,128)(2,1)}, bf16[160,2048]{1,0:T(8,128)(2,1)}, u32[]{:S(2)}, u32[]{:S(2)}) collective-permute-start(bf16[160,2048]{1,0:T(8,128)(2,1)} %collective-permute-done.16.refs_10_), channel_id=1, source_target_pairs={{0,1},{1,0},{2,3},{3,2},{4,5},{5,4},{6,7},{7,6},{8,9},{9,8},{10,11... | collective-permute-start | bytes 1966088 | tf_op jit(solution)/shard_map/ppermute | solution.py:40

commit v3 on v2

--- a/solution.py
+++ b/solution.py
@@ -51,11 +51,10 @@
 def kernel(place, near, *refs):
     mine_chunks, other_chunks, refs = refs[:4], refs[4:8], refs[8:]
     sources = [
-        [(r[0], 0), (r[0], 160)] + [(r[1], 0), (r[1], 160)] + [(r[2], 0), (r[3], 0)] + [(r[4], 0), (r[4], 160)]
-        for r in (refs[:5], refs[5:10])
+        [(r[0], 0), (r[0], 160)] + [(ref, 0) for ref in r[1:]] for r in (refs[:7], refs[7:14])
     ]
     mine, other = [[src[2 * far : 2 * far + 2] for far in range(4)] for src in sources]
-    out, chunks, occ_in, occ, first, held, result, chunk_sems, occ_sems, in_sems, out_sems = refs[10:]
+    out, chunks, occ_in, occ, first, held, result, chunk_sems, occ_sems, in_sems, out_sems = refs[14:]
     z, y, x, c = place[0], place[1], place[2], place[3]
 
     def block(core, far, b):
@@ -155,7 +154,7 @@
     return pl.pallas_call(
         kernel,
         out_shape=jax.ShapeDtypeStruct((4, 16, 4, 2, 16, 256), jnp.float32),
-        in_specs=[SMEM, SMEM] + [ANY] * 18,
+        in_specs=[SMEM, SMEM] + [ANY] * 22,
         out_specs=ANY,
         scratch_shapes=[
             pltpu.VMEM((8, 4, 2, 4, 128, 128), jnp.bfloat16),
@@ -212,7 +211,8 @@
             [virt] + [lax.dynamic_slice_in_dim(r, to, 256, 1) for r in rows] + [near], axis=1
         )
 
-    arrived = [pack(0)] + [move(pack((4 - t) % 4), SHIFT_X[4 - t]) for t in (1, 2, 3)]
+    packed = lax.optimization_barrier(tuple(pack((4 - t) % 4) for t in range(4)))
+    arrived = [packed[0]] + [move(packed[t], SHIFT_X[4 - t]) for t in (1, 2, 3)]
     packs = lax.dynamic_slice_in_dim(jnp.stack(arrived + arrived[:3]), lax.rem(4 - x, 4), 4, 0)
     near = packs[:, 0, 2560:2576].astype(jnp.int32)
 
@@ -220,24 +220,39 @@
         [packs[:, :, :2048].reshape(64, 2048)]
         + [jnp.concatenate([packs[b, :, 2048:2560] for b in range(4)], axis=1)]
     )
+    greens = jnp.concatenate(
+        [packs[:, :, :2048].reshape(64, 2048)]
+        + [jnp.concatenate([packs[b, :, 2048:2560] for b in range(4)], axis=1)]
+    )
     chunks = [three_center]
-    other_chunks = [move(three_center, CORE)]
-    first_other = other_chunks[0]
-    chunks.append(move(after(three_center, arrived[1]), RING_X))
-    other_chunks.append(move(chunks[1], CORE))
+    c_m = [move(three_center, CORE)]
+    chunks.append(move(after(three_center, *packed), RING_X))
+    c_m.append(move(chunks[1], CORE))
     chunks.append(move(chunks[1], RING_X))
-    other_chunks.append(move(chunks[2], CORE))
-    greens = spread(after(greens, other_chunks[0]), STAGE_A)
-    greens = jnp.concatenate(
-        [g[rows] for pair in (greens[:2], greens[2:]) for rows in (slice(0, 64), slice(64, 80)) for g in pair]
-    )
-    first_green = move(greens, CORE)
-    chunks.append(move(after(chunks[2], other_chunks[1], first_green), RING_X))
-    other_chunks.append(move(chunks[3], CORE))
-    up, down = move(greens, STAGE_B[1]), move(greens, STAGE_B[3])
-    beyond = [move(up[:160], STAGE_B[1]), move(down[160:], STAGE_B[3])]
-    mine = [greens, up] + beyond + [down]
-    other = [first_green] + [move(after(up, other_chunks[2]), CORE)] + [move(b, CORE) for b in beyond] + [move(after(down, other_chunks[2]), CORE)]
+
+    greens = spread(after(greens, c_m[0]), STAGE_A)
+    greens = lax.optimization_barrier(tuple(greens))
+    halves = [
+        jnp.concatenate([g[:64] for g in pair] + [g[64:] for g in pair])
+        for pair in (greens[:2], greens[2:])
+    ]
+    whole = jnp.concatenate(halves)
+    c_w = move(whole, CORE)
+    chunks.append(move(after(chunks[2], c_w), RING_X))
+    up0, down1 = move(halves[0], STAGE_B[1]), move(halves[1], STAGE_B[3])
+    c_m.append(move(chunks[2], CORE))
+    up1, down0 = [move(after(h, c_m[1], c_w), STAGE_B[d]) for h, d in ((halves[1], 1), (halves[0], 3))]
+    c_u0 = move(after(up0, c_m[2]), CORE)
+    c_d1 = move(after(down1, c_u0), CORE)
+    b0, b1 = move(up0, STAGE_B[1]), move(down1, STAGE_B[3])
+    c_u1 = move(after(up1, c_m[2]), CORE)
+    c_d0 = move(down0, CORE)
+    c_b0 = move(after(b0, c_m[2]), CORE)
+    c_b1 = move(after(b1, c_m[2]), CORE)
+    c_m.append(move(chunks[3], CORE))
+    other_chunks = c_m
+    mine = [whole, up0, up1, b0, b1, down0, down1]
+    other = [c_w, c_u0, c_u1, c_b0, c_b1, c_d0, c_d1]
 
     return contract(place, near, chunks, other_chunks, mine, other).reshape(4, 2048, 256)
 

time: 87.3 us -> 86.7 us (level)
  waiting for transfers between devices: 26.2 us -> 22.7 us
  starting transfers between devices: 36.6 us -> 39.2 us
    ppermute x23 -> x27, waiting for transfers between devices: 26.2 us -> 22.7 us  [move(): return lax.ppermute(value, AXES, perm)]
    ppermute x23 -> x27, starting transfers between devices: 36.6 us -> 39.2 us  [move(): return lax.ppermute(value, AXES, perm)]
    unnamed x48 -> x47, local copies, waits for them, and re-layouts: 1.62 us -> 1.78 us
  transfers between devices with their start and end apart: 23 -> 27, of which waited for: 8 -> 13; matrix products, arithmetic and copies ran while one was open for 2% -> 2% of each run, Pallas kernels for 0% -> 0%
where the time goes in v3:
time: 86.7 us; the launch traced here: 86.5 us
  starting transfers between devices  39.2 us (45%)
  waiting for transfers between devices  22.7 us (26%)
  Pallas kernels  17.4 us (20%)
  other arithmetic  3.88 us (4%)
  local copies, waits for them, and re-layouts  2.7 us (3%)
    ppermute x27, starting transfers between devices, move(): return lax.ppermute(value, AXES, perm)  39.2 us
    ppermute x27, waiting for transfers between devices, move(): return lax.ppermute(value, AXES, perm)  22.7 us
    pallas_call x1, Pallas kernels, contract(): pl.pallas_call(kernel, out_shape=jax.ShapeDtypeStruct((4, 16, 4, 2, 16, 2...  17.4 us
    unnamed x47, local copies, waits for them, and re-layouts  1.78 us
  transfers between devices with their start and end apart: 27, of which 13 were waited for; matrix products, arithmetic and copies ran while one was open for 2% of the time, Pallas kernels for 0%

profile of v3, /device:TPU:1, one launch (start us, length us, event | category | flops | bytes accessed | tf_op | source)
XLA Modules:
  0.0 86.5 jit_solution(12194898365782149025)
XLA Ops:
  0.0 0.8 convert_element_type.32
  0.8 0.1 convert_element_type.33
  0.9 0.7 fusion.1
  1.6 0.1 dynamic_slice.30
  1.7 1.0 %multiply_multiply_fusion = (bf16[16,2048]{1,0:T(8,128)(2,1)S(1)}, bf16[16,2048]{1,0:T(8,128)(2,1)S(1)}) fusion(bf16[16,2048]{1,0:T(8,128)(2,1)} %param.8, bf16[2048]{0:T(1024)(128)(2,1)S(1)} %fusion.1, bf16[16]{0:T(256)(128)(2,1)S(1)} %dynamic_slice.30, bf16[16,2048]{1,0:T(8,128)(2,1)} %param.9), kind=kLoop, calls=%fused_computation.62 | loop fusion | flops 98304 | bytes 266272 | tf_op jit(solution)/shard_map/mul | solution.py:187
  2.7 0.3 dynamic_update_slice.5
  3.0 1.4 %collective-permute-start = (bf16[16,1152]{1,0:T(8,128)(2,1)S(1)}, bf16[16,1152]{1,0:T(8,128)(2,1)S(1)}, u32[]{:S(2)}, u32[]{:S(2)}) collective-permute-start(bf16[16,1152]{1,0:T(8,128)(2,1)S(1)} %pad_maximum_fusion.2), channel_id=1, source_target_pairs={{0,1},{1,0},{2,3},{3,2},{4,5},{5,4},{6,7},{7,6},{8,9},{9,8},{10,11... | collective-permute-start | bytes 110600 | tf_op jit(solution)/shard_map/ppermute | solution.py:40
  4.4 0.1 collective-permute-start.6
  4.6 0.7 collective-permute-done
  5.3 0.1 fusion.3
  5.4 0.2 add.56
  5.7 2.6 %collective-permute-start.1 = (bf16[16,2688]{1,0:T(8,128)(2,1)S(1)}, bf16[16,2688]{1,0:T(8,128)(2,1)S(1)}, u32[]{:S(2)}, u32[]{:S(2)}) collective-permute-start(bf16[16,2688]{1,0:T(8,128)(2,1)S(1)} %get-tuple-element.24), channel_id=1, source_target_pairs={{0,6},{1,7},{2,0},{3,1},{4,2},{5,3},{6,4},{7,5},{8,14},{9,15},{10,... | collective-permute-start | bytes 258056 | tf_op jit(solution)/shard_map/ppermute | solution.py:40
  8.4 0.5 collective-permute-start.2
  8.9 0.6 collective-permute-start.3
  9.5 2.1 %collective-permute-start.4 = (bf16[4,2,4,128,128]{4,3,2,1,0:T(8,128)(2,1)S(1)}, bf16[4,2,4,128,128]{4,3,2,1,0:T(8,128)(2,1)S(1)}, u32[]{:S(2)}, u32[]{:S(2)}) collective-permute-start(bf16[4,2,4,128,128]{4,3,2,1,0:T(8,128)(2,1)S(1)} %copy-done.2), channel_id=1, source_target_pairs={{0,2},{1,7},{2,4},{3,1},{4,6},{5,3},{6,0},{7,5},{8,10},{9,15},{10,... | collective-permute-start | bytes 3145736 | tf_op jit(solution)/shard_map/ppermute | solution.py:40
  11.6 0.0 collective-permute-done.1
  11.7 1.6 %collective-permute-done.2 = bf16[16,2688]{1,0:T(8,128)(2,1)S(1)} collective-permute-done((bf16[16,2688]{1,0:T(8,128)(2,1)S(1)}, bf16[16,2688]{1,0:T(8,128)(2,1)S(1)}, u32[]{:S(2)}, u32[]{:S(2)}) %collective-permute-start.2) | collective-permute-done | bytes 86048 | tf_op jit(solution)/shard_map/ppermute | solution.py:40
  13.3 2.7 %collective-permute-done.3 = bf16[16,2688]{1,0:T(8,128)(2,1)S(1)} collective-permute-done((bf16[16,2688]{1,0:T(8,128)(2,1)S(1)}, bf16[16,2688]{1,0:T(8,128)(2,1)S(1)}, u32[]{:S(2)}, u32[]{:S(2)}) %collective-permute-start.3) | collective-permute-done | bytes 86048 | tf_op jit(solution)/shard_map/ppermute | solution.py:40
  16.1 0.0 collective-permute-done.6.refs_4_
  16.1 3.8 %collective-permute-start.9 = (bf16[80,2048]{1,0:T(8,128)(2,1)S(1)}, bf16[80,2048]{1,0:T(8,128)(2,1)S(1)}, u32[]{:S(2)}, u32[]{:S(2)}) collective-permute-start(bf16[80,2048]{1,0:T(8,128)(2,1)S(1)} %maximum_maximum_fusion), channel_id=1, source_target_pairs={{0,24},{1,97},{2,26},{3,99},{4,28},{5,101},{6,30},{7,103},{8,0},{9... | collective-permute-start | bytes 983048 | tf_op jit(solution)/shard_map/ppermute | solution.py:40
  20.0 0.0 collective-permute-start.8
  20.0 0.7 collective-permute-start.7
  20.7 3.2 %collective-permute-done.4.refs_1_ = bf16[4,2,4,128,128]{4,3,2,1,0:T(8,128)(2,1)S(1)} collective-permute-done((bf16[4,2,4,128,128]{4,3,2,1,0:T(8,128)(2,1)S(1)}, bf16[4,2,4,128,128]{4,3,2,1,0:T(8,128)(2,1)S(1)}, u32[]{:S(2)}, u32[]{:S(2)}) %collective-permute-start.4) | collective-permute-done | bytes 1048608 | tf_op jit(solution)/shard_map/ppermute | solution.py:40
  23.9 3.3 %collective-permute-start.5 = (bf16[4,2,4,128,128]{4,3,2,1,0:T(8,128)(2,1)S(1)}, bf16[4,2,4,128,128]{4,3,2,1,0:T(8,128)(2,1)S(1)}, u32[]{:S(2)}, u32[]{:S(2)}) collective-permute-start(bf16[4,2,4,128,128]{4,3,2,1,0:T(8,128)(2,1)S(1)} %collective-permute-done.4.refs_1_), channel_id=1, source_target_pairs={{0,2},{1,7},{2,4},{3,1},{4,6},{5,3},{6,0},{7,5},{8,10},{9,15},{10,... | collective-permute-start | bytes 3145736 | tf_op jit(solution)/shard_map/ppermute | solution.py:40
  27.2 0.3 collective-permute-done.9
  27.5 0.2 collective-permute-done.8
  27.7 3.2 %collective-permute-done.7 = bf16[80,2048]{1,0:T(8,128)(2,1)S(1)} collective-permute-done((bf16[80,2048]{1,0:T(8,128)(2,1)S(1)}, bf16[80,2048]{1,0:T(8,128)(2,1)S(1)}, u32[]{:S(2)}, u32[]{:S(2)}) %collective-permute-start.7) | collective-permute-done | bytes 327712 | tf_op jit(solution)/shard_map/ppermute | solution.py:40
  31.2 1.2 %collective-permute-start.10 = (bf16[320,2048]{1,0:T(8,128)(2,1)S(1)}, bf16[320,2048]{1,0:T(8,128)(2,1)S(1)}, u32[]{:S(2)}, u32[]{:S(2)}) collective-permute-start(bf16[320,2048]{1,0:T(8,128)(2,1)S(1)} %get-tuple-element.52.refs_8_), channel_id=1, source_target_pairs={{0,1},{1,0},{2,3},{3,2},{4,5},{5,4},{6,7},{7,6},{8,9},{9,8},{10,11... | collective-permute-start | bytes 3932168 | tf_op jit(solution)/shard_map/ppermute | solution.py:40
  32.3 0.1 pad_maximum_fusion
  32.4 0.1 collective-permute-start.15
  32.5 0.1 pad_maximum_fusion.1
  32.6 2.7 %collective-permute-start.18 = (bf16[160,2048]{1,0:T(8,128)(2,1)S(1)}, bf16[160,2048]{1,0:T(8,128)(2,1)}, u32[]{:S(2)}, u32[]{:S(2)}) collective-permute-start(bf16[160,2048]{1,0:T(8,128)(2,1)S(1)} %pad_maximum_fusion.1), channel_id=1, source_target_pairs={{0,96},{1,25},{2,98},{3,27},{4,100},{5,29},{6,102},{7,31},{8,104},... | collective-permute-start | bytes 1966088 | tf_op jit(solution)/shard_map/ppermute | solution.py:40
  35.3 2.1 %collective-permute-start.12 = (bf16[4,2,4,128,128]{4,3,2,1,0:T(8,128)(2,1)S(1)}, bf16[4,2,4,128,128]{4,3,2,1,0:T(8,128)(2,1)S(1)}, u32[]{:S(2)}, u32[]{:S(2)}) collective-permute-start(bf16[4,2,4,128,128]{4,3,2,1,0:T(8,128)(2,1)S(1)} %collective-permute-done.4.refs_1_), channel_id=1, source_target_pairs={{0,1},{1,0},{2,3},{3,2},{4,5},{5,4},{6,7},{7,6},{8,9},{9,8},{10,11... | collective-permute-start | bytes 3145736 | tf_op jit(solution)/shard_map/ppermute | solution.py:40
  37.4 1.5 %collective-permute-done.5.refs_2_ = bf16[4,2,4,128,128]{4,3,2,1,0:T(8,128)(2,1)S(1)} collective-permute-done((bf16[4,2,4,128,128]{4,3,2,1,0:T(8,128)(2,1)S(1)}, bf16[4,2,4,128,128]{4,3,2,1,0:T(8,128)(2,1)S(1)}, u32[]{:S(2)}, u32[]{:S(2)}) %collective-permute-start.5) | collective-permute-done | bytes 1048608 | tf_op jit(solution)/shard_map/ppermute | solution.py:40
  38.9 5.0 %collective-permute-start.13 = (bf16[4,2,4,128,128]{4,3,2,1,0:T(8,128)(2,1)S(1)}, bf16[4,2,4,128,128]{4,3,2,1,0:T(8,128)(2,1)S(1)}, u32[]{:S(2)}, u32[]{:S(2)}) collective-permute-start(bf16[4,2,4,128,128]{4,3,2,1,0:T(8,128)(2,1)S(1)} %collective-permute-done.5.refs_2_), channel_id=1, source_target_pairs={{0,1},{1,0},{2,3},{3,2},{4,5},{5,4},{6,7},{7,6},{8,9},{9,8},{10,11... | collective-permute-start | bytes 3145736 | tf_op jit(solution)/shard_map/ppermute | solution.py:40
  43.9 0.0 collective-permute-done.10.refs_15_
  43.9 0.0 collective-permute-start.11
  43.9 0.0 collective-permute-done.15.refs_9_
  43.9 1.4 %collective-permute-start.17 = (bf16[160,2048]{1,0:T(8,128)(2,1)S(1)}, bf16[160,2048]{1,0:T(8,128)(2,1)S(1)}, u32[]{:S(2)}, u32[]{:S(2)}) collective-permute-start(bf16[160,2048]{1,0:T(8,128)(2,1)S(1)} %collective-permute-done.15.refs_9_), channel_id=1, source_target_pairs={{0,32},{1,9},{2,34},{3,11},{4,36},{5,13},{6,38},{7,15},{8,40},{9,1... | collective-permute-start | bytes 1966088 | tf_op jit(solution)/shard_map/ppermute | solution.py:40
  45.3 0.0 collective-permute-done.18.refs_14_
  45.3 1.5 %collective-permute-start.19 = (bf16[160,2048]{1,0:T(8,128)(2,1)}, bf16[160,2048]{1,0:T(8,128)(2,1)}, u32[]{:S(2)}, u32[]{:S(2)}) collective-permute-start(bf16[160,2048]{1,0:T(8,128)(2,1)} %collective-permute-done.18.refs_14_), channel_id=1, source_target_pairs={{0,96},{1,25},{2,98},{3,27},{4,100},{5,29},{6,102},{7,31},{8,104},... | collective-permute-start | bytes 1966088 | tf_op jit(solution)/shard_map/ppermute | solution.py:40
  46.8 0.0 collective-permute-done.12.refs_5_
  46.8 0.0 collective-permute-done.13.refs_6_
  46.9 2.7 %collective-permute-start.20 = (bf16[160,2048]{1,0:T(8,128)(2,1)S(1)}, bf16[160,2048]{1,0:T(8,128)(2,1)}, u32[]{:S(2)}, u32[]{:S(2)}) collective-permute-start(bf16[160,2048]{1,0:T(8,128)(2,1)S(1)} %pad_maximum_fusion), channel_id=1, source_target_pairs={{0,96},{1,25},{2,98},{3,27},{4,100},{5,29},{6,102},{7,31},{8,104},... | collective-permute-start | bytes 1966088 | tf_op jit(solution)/shard_map/ppermute | solution.py:40
  49.5 5.5 %collective-permute-done.17.refs_11_ = bf16[160,2048]{1,0:T(8,128)(2,1)S(1)} collective-permute-done((bf16[160,2048]{1,0:T(8,128)(2,1)S(1)}, bf16[160,2048]{1,0:T(8,128)(2,1)S(1)}, u32[]{:S(2)}, u32[]{:S(2)}) %collective-permute-start.17) | collective-permute-done | bytes 655392 | tf_op jit(solution)/shard_map/ppermute | solution.py:40
  55.0 1.9 %collective-permute-start.21 = (bf16[160,2048]{1,0:T(8,128)(2,1)S(1)}, bf16[160,2048]{1,0:T(8,128)(2,1)S(1)}, u32[]{:S(2)}, u32[]{:S(2)}) collective-permute-start(bf16[160,2048]{1,0:T(8,128)(2,1)S(1)} %collective-permute-done.15.refs_9_), channel_id=1, source_target_pairs={{0,1},{1,0},{2,3},{3,2},{4,5},{5,4},{6,7},{7,6},{8,9},{9,8},{10,11... | collective-permute-start | bytes 1966088 | tf_op jit(solution)/shard_map/ppermute | solution.py:40
  56.9 0.8 collective-permute-start.23
  57.7 0.2 collective-permute-done.11.refs_3_
  58.0 2.0 %collective-permute-start.14 = (bf16[4,2,4,128,128]{4,3,2,1,0:T(8,128)(2,1)S(1)}, bf16[4,2,4,128,128]{4,3,2,1,0:T(8,128)(2,1)}, u32[]{:S(2)}, u32[]{:S(2)}) collective-permute-start(bf16[4,2,4,128,128]{4,3,2,1,0:T(8,128)(2,1)S(1)} %collective-permute-done.11.refs_3_), channel_id=1, source_target_pairs={{0,1},{1,0},{2,3},{3,2},{4,5},{5,4},{6,7},{7,6},{8,9},{9,8},{10,11... | collective-permute-start | bytes 3145736 | tf_op jit(solution)/shard_map/ppermute | solution.py:40
  60.0 2.1 %collective-permute-done.16.refs_10_ = bf16[160,2048]{1,0:T(8,128)(2,1)} collective-permute-done((bf16[160,2048]{1,0:T(8,128)(2,1)S(1)}, bf16[160,2048]{1,0:T(8,128)(2,1)}, u32[]{:S(2)}, u32[]{:S(2)}) %collective-permute-start.16) | collective-permute-done | bytes 655392 | tf_op jit(solution)/shard_map/ppermute | solution.py:40
  62.1 1.9 %collective-permute-start.24 = (bf16[160,2048]{1,0:T(8,128)(2,1)}, bf16[160,2048]{1,0:T(8,128)(2,1)}, u32[]{:S(2)}, u32[]{:S(2)}) collective-permute-start(bf16[160,2048]{1,0:T(8,128)(2,1)} %collective-permute-done.19.refs_12_), channel_id=1, source_target_pairs={{0,1},{1,0},{2,3},{3,2},{4,5},{5,4},{6,7},{7,6},{8,9},{9,8},{10,11... | collective-permute-start | bytes 1966088 | tf_op jit(solution)/shard_map/ppermute | solution.py:40
  64.0 0.0 collective-permute-done.20.refs_13_
  64.0 0.6 collective-permute-start.22
  64.6 0.0 collective-permute-done.21.refs_16_
  64.7 0.1 collective-permute-start.25
  64.8 0.7 copy-done.11
  65.5 0.9 copy-done.12
  66.3 0.0 collective-permute-start.26
  66.4 0.6 pad_add_fusion.place
  67.0 0.6 fusion.2
  67.5 0.4 collective-permute-done.25.refs_20_
  68.0 0.9 %collective-permute-done.26.refs_21_ = bf16[160,2048]{1,0:T(8,128)(2,1)} collective-permute-done((bf16[160,2048]{1,0:T(8,128)(2,1)}, bf16[160,2048]{1,0:T(8,128)(2,1)}, u32[]{:S(2)}, u32[]{:S(2)}) %collective-permute-start.26) | collective-permute-done | bytes 655392 | tf_op jit(solution)/shard_map/ppermute | solution.py:40
  68.9 0.0 collective-permute-done.14.refs_7_
  68.9 17.4 %shard_map.55 = f32[4,16,4,2,16,256]{5,4,3,2,1,0:T(8,128)} custom-call(s32[4]{0:T(128)} %pad_add_fusion.place, s32[4,16]{1,0:T(4,128)} %bitcast.29, bf16[4,2,4,128,128]{4,3,2,1,0:T(8,128)(2,1)} %refs_0_.1, bf16[4,2,4,128,128]{4,3,2,1,0:T(8,128)(2,1)} %copy-done.4, bf16[4,2,4,128,128]{4,3,2,1,0:T(8,128)(2,1)} %copy-done.5, ...), custom_call_target="tpu_custom_call" | custom-call | flops 10737418240 | bytes 27262976 | tf_op jit(solution)/shard_map/pallas_call | solution.py:154
  (69 shorter events, 0.6 us)
Async XLA Ops:
  0.0 9.5 %copy-start.2 = (bf16[4,2,4,128,128]{4,3,2,1,0:T(8,128)(2,1)S(1)}, bf16[4,2,4,128,128]{4,3,2,1,0:T(8,128)(2,1)}, u32[]{:S(2)}) copy-start(bf16[4,2,4,128,128]{4,3,2,1,0:T(8,128)(2,1)} %refs_0_.1) | copy-start | bytes 3145732
  3.0 2.3 %collective-permute-start = (bf16[16,1152]{1,0:T(8,128)(2,1)S(1)}, bf16[16,1152]{1,0:T(8,128)(2,1)S(1)}, u32[]{:S(2)}, u32[]{:S(2)}) collective-permute-start(bf16[16,1152]{1,0:T(8,128)(2,1)S(1)} %pad_maximum_fusion.2), channel_id=1, source_target_pairs={{0,1},{1,0},{2,3},{3,2},{4,5},{5,4},{6,7},{7,6},{8,9},{9,8},{10,11... | collective-permute-start | bytes 110600 | tf_op jit(solution)/shard_map/ppermute | solution.py:40
  4.4 11.7 %collective-permute-start.6 = (bf16[4,2,4,128,128]{4,3,2,1,0:T(8,128)(2,1)}, bf16[4,2,4,128,128]{4,3,2,1,0:T(8,128)(2,1)S(1)}, u32[]{:S(2)}, u32[]{:S(2)}) collective-permute-start(bf16[4,2,4,128,128]{4,3,2,1,0:T(8,128)(2,1)} %refs_0_.1), channel_id=1, source_target_pairs={{0,1},{1,0},{2,3},{3,2},{4,5},{5,4},{6,7},{7,6},{8,9},{9,8},{10,11... | collective-permute-start | bytes 3145736 | tf_op jit(solution)/shard_map/ppermute | solution.py:40
  5.7 5.9 %collective-permute-start.1 = (bf16[16,2688]{1,0:T(8,128)(2,1)S(1)}, bf16[16,2688]{1,0:T(8,128)(2,1)S(1)}, u32[]{:S(2)}, u32[]{:S(2)}) collective-permute-start(bf16[16,2688]{1,0:T(8,128)(2,1)S(1)} %get-tuple-element.24), channel_id=1, source_target_pairs={{0,6},{1,7},{2,0},{3,1},{4,2},{5,3},{6,4},{7,5},{8,14},{9,15},{10,... | collective-permute-start | bytes 258056 | tf_op jit(solution)/shard_map/ppermute | solution.py:40
  8.4 4.9 %collective-permute-start.2 = (bf16[16,2688]{1,0:T(8,128)(2,1)S(1)}, bf16[16,2688]{1,0:T(8,128)(2,1)S(1)}, u32[]{:S(2)}, u32[]{:S(2)}) collective-permute-start(bf16[16,2688]{1,0:T(8,128)(2,1)S(1)} %get-tuple-element.25), channel_id=1, source_target_pairs={{0,4},{1,5},{2,6},{3,7},{4,0},{5,1},{6,2},{7,3},{8,12},{9,13},{10,... | collective-permute-start | bytes 258056 | tf_op jit(solution)/shard_map/ppermute | solution.py:40
  8.9 7.1 %collective-permute-start.3 = (bf16[16,2688]{1,0:T(8,128)(2,1)S(1)}, bf16[16,2688]{1,0:T(8,128)(2,1)S(1)}, u32[]{:S(2)}, u32[]{:S(2)}) collective-permute-start(bf16[16,2688]{1,0:T(8,128)(2,1)S(1)} %get-tuple-element.26), channel_id=1, source_target_pairs={{0,2},{1,3},{2,4},{3,5},{4,6},{5,7},{6,0},{7,1},{8,10},{9,11},{10,... | collective-permute-start | bytes 258056 | tf_op jit(solution)/shard_map/ppermute | solution.py:40
  9.5 14.4 %collective-permute-start.4 = (bf16[4,2,4,128,128]{4,3,2,1,0:T(8,128)(2,1)S(1)}, bf16[4,2,4,128,128]{4,3,2,1,0:T(8,128)(2,1)S(1)}, u32[]{:S(2)}, u32[]{:S(2)}) collective-permute-start(bf16[4,2,4,128,128]{4,3,2,1,0:T(8,128)(2,1)S(1)} %copy-done.2), channel_id=1, source_target_pairs={{0,2},{1,7},{2,4},{3,1},{4,6},{5,3},{6,0},{7,5},{8,10},{9,15},{10,... | collective-permute-start | bytes 3145736 | tf_op jit(solution)/shard_map/ppermute | solution.py:40
  16.1 11.6 %copy-start.3 = (bf16[4,2,4,128,128]{4,3,2,1,0:T(8,128)(2,1)}, bf16[4,2,4,128,128]{4,3,2,1,0:T(8,128)(2,1)S(1)}, u32[]{:S(2)}) copy-start(bf16[4,2,4,128,128]{4,3,2,1,0:T(8,128)(2,1)S(1)} %collective-permute-done.6.refs_4_) | copy-start | bytes 3145732
  16.1 11.4 %collective-permute-start.9 = (bf16[80,2048]{1,0:T(8,128)(2,1)S(1)}, bf16[80,2048]{1,0:T(8,128)(2,1)S(1)}, u32[]{:S(2)}, u32[]{:S(2)}) collective-permute-start(bf16[80,2048]{1,0:T(8,128)(2,1)S(1)} %maximum_maximum_fusion), channel_id=1, source_target_pairs={{0,24},{1,97},{2,26},{3,99},{4,28},{5,101},{6,30},{7,103},{8,0},{9... | collective-permute-start | bytes 983048 | tf_op jit(solution)/shard_map/ppermute | solution.py:40
  20.0 7.8 %collective-permute-start.8 = (bf16[80,2048]{1,0:T(8,128)(2,1)S(1)}, bf16[80,2048]{1,0:T(8,128)(2,1)S(1)}, u32[]{:S(2)}, u32[]{:S(2)}) collective-permute-start(bf16[80,2048]{1,0:T(8,128)(2,1)S(1)} %maximum_maximum_fusion), channel_id=1, source_target_pairs={{0,16},{1,65},{2,18},{3,67},{4,20},{5,69},{6,22},{7,71},{8,24},{9,... | collective-permute-start | bytes 983048 | tf_op jit(solution)/shard_map/ppermute | solution.py:40
  20.0 10.9 %collective-permute-start.7 = (bf16[80,2048]{1,0:T(8,128)(2,1)S(1)}, bf16[80,2048]{1,0:T(8,128)(2,1)S(1)}, u32[]{:S(2)}, u32[]{:S(2)}) collective-permute-start(bf16[80,2048]{1,0:T(8,128)(2,1)S(1)} %maximum_maximum_fusion), channel_id=1, source_target_pairs={{0,8},{1,33},{2,10},{3,35},{4,12},{5,37},{6,14},{7,39},{8,16},{9,4... | collective-permute-start | bytes 983048 | tf_op jit(solution)/shard_map/ppermute | solution.py:40
  23.9 11.4 %copy-start.4 = (bf16[4,2,4,128,128]{4,3,2,1,0:T(8,128)(2,1)}, bf16[4,2,4,128,128]{4,3,2,1,0:T(8,128)(2,1)S(1)}, u32[]{:S(2)}) copy-start(bf16[4,2,4,128,128]{4,3,2,1,0:T(8,128)(2,1)S(1)} %collective-permute-done.4.refs_1_) | copy-start | bytes 3145732
  23.9 15.1 %collective-permute-start.5 = (bf16[4,2,4,128,128]{4,3,2,1,0:T(8,128)(2,1)S(1)}, bf16[4,2,4,128,128]{4,3,2,1,0:T(8,128)(2,1)S(1)}, u32[]{:S(2)}, u32[]{:S(2)}) collective-permute-start(bf16[4,2,4,128,128]{4,3,2,1,0:T(8,128)(2,1)S(1)} %collective-permute-done.4.refs_1_), channel_id=1, source_target_pairs={{0,2},{1,7},{2,4},{3,1},{4,6},{5,3},{6,0},{7,5},{8,10},{9,15},{10,... | collective-permute-start | bytes 3145736 | tf_op jit(solution)/shard_map/ppermute | solution.py:40
  31.1 1.4 %copy-start = (bf16[320,2048]{1,0:T(8,128)(2,1)}, bf16[320,2048]{1,0:T(8,128)(2,1)S(1)}, u32[]{:S(2)}) copy-start(bf16[320,2048]{1,0:T(8,128)(2,1)S(1)} %get-tuple-element.52.refs_8_) | copy-start | bytes 3932164
  31.2 12.7 %collective-permute-start.10 = (bf16[320,2048]{1,0:T(8,128)(2,1)S(1)}, bf16[320,2048]{1,0:T(8,128)(2,1)S(1)}, u32[]{:S(2)}, u32[]{:S(2)}) collective-permute-start(bf16[320,2048]{1,0:T(8,128)(2,1)S(1)} %get-tuple-element.52.refs_8_), channel_id=1, source_target_pairs={{0,1},{1,0},{2,3},{3,2},{4,5},{5,4},{6,7},{7,6},{8,9},{9,8},{10,11... | collective-permute-start | bytes 3932168 | tf_op jit(solution)/shard_map/ppermute | solution.py:40
  32.4 11.5 %collective-permute-start.15 = (bf16[160,2048]{1,0:T(8,128)(2,1)S(1)}, bf16[160,2048]{1,0:T(8,128)(2,1)S(1)}, u32[]{:S(2)}, u32[]{:S(2)}) collective-permute-start(bf16[160,2048]{1,0:T(8,128)(2,1)S(1)} %pad_maximum_fusion), channel_id=1, source_target_pairs={{0,32},{1,9},{2,34},{3,11},{4,36},{5,13},{6,38},{7,15},{8,40},{9,1... | collective-permute-start | bytes 1966088 | tf_op jit(solution)/shard_map/ppermute | solution.py:40
  32.6 12.7 %collective-permute-start.18 = (bf16[160,2048]{1,0:T(8,128)(2,1)S(1)}, bf16[160,2048]{1,0:T(8,128)(2,1)}, u32[]{:S(2)}, u32[]{:S(2)}) collective-permute-start(bf16[160,2048]{1,0:T(8,128)(2,1)S(1)} %pad_maximum_fusion.1), channel_id=1, source_target_pairs={{0,96},{1,25},{2,98},{3,27},{4,100},{5,29},{6,102},{7,31},{8,104},... | collective-permute-start | bytes 1966088 | tf_op jit(solution)/shard_map/ppermute | solution.py:40
  35.3 11.5 %collective-permute-start.12 = (bf16[4,2,4,128,128]{4,3,2,1,0:T(8,128)(2,1)S(1)}, bf16[4,2,4,128,128]{4,3,2,1,0:T(8,128)(2,1)S(1)}, u32[]{:S(2)}, u32[]{:S(2)}) collective-permute-start(bf16[4,2,4,128,128]{4,3,2,1,0:T(8,128)(2,1)S(1)} %collective-permute-done.4.refs_1_), channel_id=1, source_target_pairs={{0,1},{1,0},{2,3},{3,2},{4,5},{5,4},{6,7},{7,6},{8,9},{9,8},{10,11... | collective-permute-start | bytes 3145736 | tf_op jit(solution)/shard_map/ppermute | solution.py:40
  38.9 25.1 %copy-start.5 = (bf16[4,2,4,128,128]{4,3,2,1,0:T(8,128)(2,1)}, bf16[4,2,4,128,128]{4,3,2,1,0:T(8,128)(2,1)S(1)}, u32[]{:S(2)}) copy-start(bf16[4,2,4,128,128]{4,3,2,1,0:T(8,128)(2,1)S(1)} %collective-permute-done.5.refs_2_) | copy-start | bytes 3145732
  38.9 7.9 %collective-permute-start.13 = (bf16[4,2,4,128,128]{4,3,2,1,0:T(8,128)(2,1)S(1)}, bf16[4,2,4,128,128]{4,3,2,1,0:T(8,128)(2,1)S(1)}, u32[]{:S(2)}, u32[]{:S(2)}) collective-permute-start(bf16[4,2,4,128,128]{4,3,2,1,0:T(8,128)(2,1)S(1)} %collective-permute-done.5.refs_2_), channel_id=1, source_target_pairs={{0,1},{1,0},{2,3},{3,2},{4,5},{5,4},{6,7},{7,6},{8,9},{9,8},{10,11... | collective-permute-start | bytes 3145736 | tf_op jit(solution)/shard_map/ppermute | solution.py:40
  43.9 25.0 %copy-start.1 = (bf16[320,2048]{1,0:T(8,128)(2,1)}, bf16[320,2048]{1,0:T(8,128)(2,1)S(1)}, u32[]{:S(2)}) copy-start(bf16[320,2048]{1,0:T(8,128)(2,1)S(1)} %collective-permute-done.10.refs_15_) | copy-start | bytes 3932164
  43.9 14.1 %collective-permute-start.11 = (bf16[4,2,4,128,128]{4,3,2,1,0:T(8,128)(2,1)S(1)}, bf16[4,2,4,128,128]{4,3,2,1,0:T(8,128)(2,1)S(1)}, u32[]{:S(2)}, u32[]{:S(2)}) collective-permute-start(bf16[4,2,4,128,128]{4,3,2,1,0:T(8,128)(2,1)S(1)} %collective-permute-done.5.refs_2_), channel_id=1, source_target_pairs={{0,2},{1,7},{2,4},{3,1},{4,6},{5,3},{6,0},{7,5},{8,10},{9,15},{10,... | collective-permute-start | bytes 3145736 | tf_op jit(solution)/shard_map/ppermute | solution.py:40
  43.9 20.8 %copy-start.9 = (bf16[160,2048]{1,0:T(8,128)(2,1)}, bf16[160,2048]{1,0:T(8,128)(2,1)S(1)}, u32[]{:S(2)}) copy-start(bf16[160,2048]{1,0:T(8,128)(2,1)S(1)} %collective-permute-done.15.refs_9_) | copy-start | bytes 1966084
  43.9 11.1 %collective-permute-start.17 = (bf16[160,2048]{1,0:T(8,128)(2,1)S(1)}, bf16[160,2048]{1,0:T(8,128)(2,1)S(1)}, u32[]{:S(2)}, u32[]{:S(2)}) collective-permute-start(bf16[160,2048]{1,0:T(8,128)(2,1)S(1)} %collective-permute-done.15.refs_9_), channel_id=1, source_target_pairs={{0,32},{1,9},{2,34},{3,11},{4,36},{5,13},{6,38},{7,15},{8,40},{9,1... | collective-permute-start | bytes 1966088 | tf_op jit(solution)/shard_map/ppermute | solution.py:40
  45.3 11.6 %collective-permute-start.19 = (bf16[160,2048]{1,0:T(8,128)(2,1)}, bf16[160,2048]{1,0:T(8,128)(2,1)}, u32[]{:S(2)}, u32[]{:S(2)}) collective-permute-start(bf16[160,2048]{1,0:T(8,128)(2,1)} %collective-permute-done.18.refs_14_), channel_id=1, source_target_pairs={{0,96},{1,25},{2,98},{3,27},{4,100},{5,29},{6,102},{7,31},{8,104},... | collective-permute-start | bytes 1966088 | tf_op jit(solution)/shard_map/ppermute | solution.py:40
  46.8 17.8 %copy-start.6 = (bf16[4,2,4,128,128]{4,3,2,1,0:T(8,128)(2,1)}, bf16[4,2,4,128,128]{4,3,2,1,0:T(8,128)(2,1)S(1)}, u32[]{:S(2)}) copy-start(bf16[4,2,4,128,128]{4,3,2,1,0:T(8,128)(2,1)S(1)} %collective-permute-done.12.refs_5_) | copy-start | bytes 3145732
  46.8 15.3 %collective-permute-start.16 = (bf16[160,2048]{1,0:T(8,128)(2,1)S(1)}, bf16[160,2048]{1,0:T(8,128)(2,1)}, u32[]{:S(2)}, u32[]{:S(2)}) collective-permute-start(bf16[160,2048]{1,0:T(8,128)(2,1)S(1)} %pad_maximum_fusion.1), channel_id=1, source_target_pairs={{0,32},{1,9},{2,34},{3,11},{4,36},{5,13},{6,38},{7,15},{8,40},{9,1... | collective-permute-start | bytes 1966088 | tf_op jit(solution)/shard_map/ppermute | solution.py:40
  46.9 17.8 %copy-start.7 = (bf16[4,2,4,128,128]{4,3,2,1,0:T(8,128)(2,1)}, bf16[4,2,4,128,128]{4,3,2,1,0:T(8,128)(2,1)S(1)}, u32[]{:S(2)}) copy-start(bf16[4,2,4,128,128]{4,3,2,1,0:T(8,128)(2,1)S(1)} %collective-permute-done.13.refs_6_) | copy-start | bytes 3145732
  46.9 17.2 %collective-permute-start.20 = (bf16[160,2048]{1,0:T(8,128)(2,1)S(1)}, bf16[160,2048]{1,0:T(8,128)(2,1)}, u32[]{:S(2)}, u32[]{:S(2)}) collective-permute-start(bf16[160,2048]{1,0:T(8,128)(2,1)S(1)} %pad_maximum_fusion), channel_id=1, source_target_pairs={{0,96},{1,25},{2,98},{3,27},{4,100},{5,29},{6,102},{7,31},{8,104},... | collective-permute-start | bytes 1966088 | tf_op jit(solution)/shard_map/ppermute | solution.py:40
  55.0 9.8 %copy-start.10 = (bf16[160,2048]{1,0:T(8,128)(2,1)}, bf16[160,2048]{1,0:T(8,128)(2,1)S(1)}, u32[]{:S(2)}) copy-start(bf16[160,2048]{1,0:T(8,128)(2,1)S(1)} %collective-permute-done.17.refs_11_) | copy-start | bytes 1966084
  55.0 9.6 %collective-permute-start.21 = (bf16[160,2048]{1,0:T(8,128)(2,1)S(1)}, bf16[160,2048]{1,0:T(8,128)(2,1)S(1)}, u32[]{:S(2)}, u32[]{:S(2)}) collective-permute-start(bf16[160,2048]{1,0:T(8,128)(2,1)S(1)} %collective-permute-done.15.refs_9_), channel_id=1, source_target_pairs={{0,1},{1,0},{2,3},{3,2},{4,5},{5,4},{6,7},{7,6},{8,9},{9,8},{10,11... | collective-permute-start | bytes 1966088 | tf_op jit(solution)/shard_map/ppermute | solution.py:40
  56.9 7.9 %collective-permute-start.23 = (bf16[160,2048]{1,0:T(8,128)(2,1)S(1)}, bf16[160,2048]{1,0:T(8,128)(2,1)S(1)}, u32[]{:S(2)}, u32[]{:S(2)}) collective-permute-start(bf16[160,2048]{1,0:T(8,128)(2,1)S(1)} %collective-permute-done.17.refs_11_), channel_id=1, source_target_pairs={{0,1},{1,0},{2,3},{3,2},{4,5},{5,4},{6,7},{7,6},{8,9},{9,8},{10,11... | collective-permute-start | bytes 1966088 | tf_op jit(solution)/shard_map/ppermute | solution.py:40
  58.0 10.9 %copy-start.8 = (bf16[4,2,4,128,128]{4,3,2,1,0:T(8,128)(2,1)}, bf16[4,2,4,128,128]{4,3,2,1,0:T(8,128)(2,1)S(1)}, u32[]{:S(2)}) copy-start(bf16[4,2,4,128,128]{4,3,2,1,0:T(8,128)(2,1)S(1)} %collective-permute-done.11.refs_3_) | copy-start | bytes 3145732
  58.0 10.9 %collective-permute-start.14 = (bf16[4,2,4,128,128]{4,3,2,1,0:T(8,128)(2,1)S(1)}, bf16[4,2,4,128,128]{4,3,2,1,0:T(8,128)(2,1)}, u32[]{:S(2)}, u32[]{:S(2)}) collective-permute-start(bf16[4,2,4,128,128]{4,3,2,1,0:T(8,128)(2,1)S(1)} %collective-permute-done.11.refs_3_), channel_id=1, source_target_pairs={{0,1},{1,0},{2,3},{3,2},{4,5},{5,4},{6,7},{7,6},{8,9},{9,8},{10,11... | collective-permute-start | bytes 3145736 | tf_op jit(solution)/shard_map/ppermute | solution.py:40
  62.1 5.4 %collective-permute-start.24 = (bf16[160,2048]{1,0:T(8,128)(2,1)}, bf16[160,2048]{1,0:T(8,128)(2,1)}, u32[]{:S(2)}, u32[]{:S(2)}) collective-permute-start(bf16[160,2048]{1,0:T(8,128)(2,1)} %collective-permute-done.19.refs_12_), channel_id=1, source_target_pairs={{0,1},{1,0},{2,3},{3,2},{4,5},{5,4},{6,7},{7,6},{8,9},{9,8},{10,11... | collective-permute-start | bytes 1966088 | tf_op jit(solution)/shard_map/ppermute | solution.py:40
  64.0 3.5 %collective-permute-start.22 = (bf16[160,2048]{1,0:T(8,128)(2,1)}, bf16[160,2048]{1,0:T(8,128)(2,1)}, u32[]{:S(2)}, u32[]{:S(2)}) collective-permute-start(bf16[160,2048]{1,0:T(8,128)(2,1)} %collective-permute-done.16.refs_10_), channel_id=1, source_target_pairs={{0,1},{1,0},{2,3},{3,2},{4,5},{5,4},{6,7},{7,6},{8,9},{9,8},{10,11... | collective-permute-start | bytes 1966088 | tf_op jit(solution)/shard_map/ppermute | solution.py:40
  64.7 0.8 copy-start.11
  64.7 3.3 %collective-permute-start.25 = (bf16[160,2048]{1,0:T(8,128)(2,1)}, bf16[160,2048]{1,0:T(8,128)(2,1)}, u32[]{:S(2)}, u32[]{:S(2)}) collective-permute-start(bf16[160,2048]{1,0:T(8,128)(2,1)} %collective-permute-done.20.refs_13_), channel_id=1, source_target_pairs={{0,1},{1,0},{2,3},{3,2},{4,5},{5,4},{6,7},{7,6},{8,9},{9,8},{10,11... | collective-permute-start | bytes 1966088 | tf_op jit(solution)/shard_map/ppermute | solution.py:40
  65.5 0.9 copy-start.12
  66.3 2.5 %collective-permute-start.26 = (bf16[160,2048]{1,0:T(8,128)(2,1)}, bf16[160,2048]{1,0:T(8,128)(2,1)}, u32[]{:S(2)}, u32[]{:S(2)}) collective-permute-start(bf16[160,2048]{1,0:T(8,128)(2,1)} %collective-permute-done.18.refs_14_), channel_id=1, source_target_pairs={{0,1},{1,0},{2,3},{3,2},{4,5},{5,4},{6,7},{7,6},{8,9},{9,8},{10,11... | collective-permute-start | bytes 1966088 | tf_op jit(solution)/shard_map/ppermute | solution.py:40

commit v4 on v3

--- a/solution.py
+++ b/solution.py
@@ -32,7 +32,7 @@
 STAGE_B = [None] + [
     pairs(lambda z, y, x, c, d=d: (z + d * (1 - c), y + d * c, x, c)) for d in (1, 2, 3)
 ]
-AHEAD, PACE = 3, 2
+AHEAD, PACE = 4, 2
 KINDS = tuple((far, mine) for far in (0, 1, 3, 2) for mine in (True, False))
 
 

time: 86.7 us -> 87 us (level)
  no operation moved by 1% of the time
where the time goes in v4:
time: 87 us; the launch traced here: 86.8 us
  starting transfers between devices  39.2 us (45%)
  waiting for transfers between devices  22.7 us (26%)
  Pallas kernels  17.7 us (20%)
  other arithmetic  3.88 us (4%)
  local copies, waits for them, and re-layouts  2.7 us (3%)
    ppermute x27, starting transfers between devices, move(): return lax.ppermute(value, AXES, perm)  39.2 us
    ppermute x27, waiting for transfers between devices, move(): return lax.ppermute(value, AXES, perm)  22.7 us
    pallas_call x1, Pallas kernels, contract(): pl.pallas_call(kernel, out_shape=jax.ShapeDtypeStruct((4, 16, 4, 2, 16, 2...  17.7 us
    unnamed x47, local copies, waits for them, and re-layouts  1.78 us
  transfers between devices with their start and end apart: 27, of which 13 were waited for; matrix products, arithmetic and copies ran while one was open for 2% of the time, Pallas kernels for 0%

profile of v4, /device:TPU:1, one launch (start us, length us, event | category | flops | bytes accessed | tf_op | source)
XLA Modules:
  0.0 86.8 jit_solution(8196088432278851976)
XLA Ops:
  0.0 0.8 convert_element_type.32
  0.8 0.1 convert_element_type.33
  0.9 0.7 fusion.1
  1.6 0.1 dynamic_slice.30
  1.7 1.0 %multiply_multiply_fusion = (bf16[16,2048]{1,0:T(8,128)(2,1)S(1)}, bf16[16,2048]{1,0:T(8,128)(2,1)S(1)}) fusion(bf16[16,2048]{1,0:T(8,128)(2,1)} %param.8, bf16[2048]{0:T(1024)(128)(2,1)S(1)} %fusion.1, bf16[16]{0:T(256)(128)(2,1)S(1)} %dynamic_slice.30, bf16[16,2048]{1,0:T(8,128)(2,1)} %param.9), kind=kLoop, calls=%fused_computation.62 | loop fusion | flops 98304 | bytes 266272 | tf_op jit(solution)/shard_map/mul | solution.py:187
  2.7 0.3 dynamic_update_slice.5
  3.0 1.4 %collective-permute-start = (bf16[16,1152]{1,0:T(8,128)(2,1)S(1)}, bf16[16,1152]{1,0:T(8,128)(2,1)S(1)}, u32[]{:S(2)}, u32[]{:S(2)}) collective-permute-start(bf16[16,1152]{1,0:T(8,128)(2,1)S(1)} %pad_maximum_fusion.2), channel_id=1, source_target_pairs={{0,1},{1,0},{2,3},{3,2},{4,5},{5,4},{6,7},{7,6},{8,9},{9,8},{10,11... | collective-permute-start | bytes 110600 | tf_op jit(solution)/shard_map/ppermute | solution.py:40
  4.4 0.1 collective-permute-start.6
  4.6 0.7 collective-permute-done
  5.3 0.1 fusion.3
  5.4 0.2 add.56
  5.7 2.6 %collective-permute-start.1 = (bf16[16,2688]{1,0:T(8,128)(2,1)S(1)}, bf16[16,2688]{1,0:T(8,128)(2,1)S(1)}, u32[]{:S(2)}, u32[]{:S(2)}) collective-permute-start(bf16[16,2688]{1,0:T(8,128)(2,1)S(1)} %get-tuple-element.24), channel_id=1, source_target_pairs={{0,6},{1,7},{2,0},{3,1},{4,2},{5,3},{6,4},{7,5},{8,14},{9,15},{10,... | collective-permute-start | bytes 258056 | tf_op jit(solution)/shard_map/ppermute | solution.py:40
  8.4 0.5 collective-permute-start.2
  8.9 0.6 collective-permute-start.3
  9.5 2.1 %collective-permute-start.4 = (bf16[4,2,4,128,128]{4,3,2,1,0:T(8,128)(2,1)S(1)}, bf16[4,2,4,128,128]{4,3,2,1,0:T(8,128)(2,1)S(1)}, u32[]{:S(2)}, u32[]{:S(2)}) collective-permute-start(bf16[4,2,4,128,128]{4,3,2,1,0:T(8,128)(2,1)S(1)} %copy-done.2), channel_id=1, source_target_pairs={{0,2},{1,7},{2,4},{3,1},{4,6},{5,3},{6,0},{7,5},{8,10},{9,15},{10,... | collective-permute-start | bytes 3145736 | tf_op jit(solution)/shard_map/ppermute | solution.py:40
  11.6 0.0 collective-permute-done.1
  11.7 1.6 %collective-permute-done.2 = bf16[16,2688]{1,0:T(8,128)(2,1)S(1)} collective-permute-done((bf16[16,2688]{1,0:T(8,128)(2,1)S(1)}, bf16[16,2688]{1,0:T(8,128)(2,1)S(1)}, u32[]{:S(2)}, u32[]{:S(2)}) %collective-permute-start.2) | collective-permute-done | bytes 86048 | tf_op jit(solution)/shard_map/ppermute | solution.py:40
  13.3 2.7 %collective-permute-done.3 = bf16[16,2688]{1,0:T(8,128)(2,1)S(1)} collective-permute-done((bf16[16,2688]{1,0:T(8,128)(2,1)S(1)}, bf16[16,2688]{1,0:T(8,128)(2,1)S(1)}, u32[]{:S(2)}, u32[]{:S(2)}) %collective-permute-start.3) | collective-permute-done | bytes 86048 | tf_op jit(solution)/shard_map/ppermute | solution.py:40
  16.1 0.0 collective-permute-done.6.refs_4_
  16.1 3.8 %collective-permute-start.9 = (bf16[80,2048]{1,0:T(8,128)(2,1)S(1)}, bf16[80,2048]{1,0:T(8,128)(2,1)S(1)}, u32[]{:S(2)}, u32[]{:S(2)}) collective-permute-start(bf16[80,2048]{1,0:T(8,128)(2,1)S(1)} %maximum_maximum_fusion), channel_id=1, source_target_pairs={{0,24},{1,97},{2,26},{3,99},{4,28},{5,101},{6,30},{7,103},{8,0},{9... | collective-permute-start | bytes 983048 | tf_op jit(solution)/shard_map/ppermute | solution.py:40
  20.0 0.7 collective-permute-start.7
  20.7 3.2 %collective-permute-done.4.refs_1_ = bf16[4,2,4,128,128]{4,3,2,1,0:T(8,128)(2,1)S(1)} collective-permute-done((bf16[4,2,4,128,128]{4,3,2,1,0:T(8,128)(2,1)S(1)}, bf16[4,2,4,128,128]{4,3,2,1,0:T(8,128)(2,1)S(1)}, u32[]{:S(2)}, u32[]{:S(2)}) %collective-permute-start.4) | collective-permute-done | bytes 1048608 | tf_op jit(solution)/shard_map/ppermute | solution.py:40
  23.9 3.3 %collective-permute-start.5 = (bf16[4,2,4,128,128]{4,3,2,1,0:T(8,128)(2,1)S(1)}, bf16[4,2,4,128,128]{4,3,2,1,0:T(8,128)(2,1)S(1)}, u32[]{:S(2)}, u32[]{:S(2)}) collective-permute-start(bf16[4,2,4,128,128]{4,3,2,1,0:T(8,128)(2,1)S(1)} %collective-permute-done.4.refs_1_), channel_id=1, source_target_pairs={{0,2},{1,7},{2,4},{3,1},{4,6},{5,3},{6,0},{7,5},{8,10},{9,15},{10,... | collective-permute-start | bytes 3145736 | tf_op jit(solution)/shard_map/ppermute | solution.py:40
  27.2 0.3 collective-permute-done.9
  27.5 0.2 collective-permute-done.8
  27.7 3.2 %collective-permute-done.7 = bf16[80,2048]{1,0:T(8,128)(2,1)S(1)} collective-permute-done((bf16[80,2048]{1,0:T(8,128)(2,1)S(1)}, bf16[80,2048]{1,0:T(8,128)(2,1)S(1)}, u32[]{:S(2)}, u32[]{:S(2)}) %collective-permute-start.7) | collective-permute-done | bytes 327712 | tf_op jit(solution)/shard_map/ppermute | solution.py:40
  31.2 1.2 %collective-permute-start.10 = (bf16[320,2048]{1,0:T(8,128)(2,1)S(1)}, bf16[320,2048]{1,0:T(8,128)(2,1)S(1)}, u32[]{:S(2)}, u32[]{:S(2)}) collective-permute-start(bf16[320,2048]{1,0:T(8,128)(2,1)S(1)} %get-tuple-element.52.refs_8_), channel_id=1, source_target_pairs={{0,1},{1,0},{2,3},{3,2},{4,5},{5,4},{6,7},{7,6},{8,9},{9,8},{10,11... | collective-permute-start | bytes 3932168 | tf_op jit(solution)/shard_map/ppermute | solution.py:40
  32.3 0.1 pad_maximum_fusion
  32.4 0.1 collective-permute-start.15
  32.5 0.1 pad_maximum_fusion.1
  32.6 2.7 %collective-permute-start.18 = (bf16[160,2048]{1,0:T(8,128)(2,1)S(1)}, bf16[160,2048]{1,0:T(8,128)(2,1)}, u32[]{:S(2)}, u32[]{:S(2)}) collective-permute-start(bf16[160,2048]{1,0:T(8,128)(2,1)S(1)} %pad_maximum_fusion.1), channel_id=1, source_target_pairs={{0,96},{1,25},{2,98},{3,27},{4,100},{5,29},{6,102},{7,31},{8,104},... | collective-permute-start | bytes 1966088 | tf_op jit(solution)/shard_map/ppermute | solution.py:40
  35.3 2.1 %collective-permute-start.12 = (bf16[4,2,4,128,128]{4,3,2,1,0:T(8,128)(2,1)S(1)}, bf16[4,2,4,128,128]{4,3,2,1,0:T(8,128)(2,1)S(1)}, u32[]{:S(2)}, u32[]{:S(2)}) collective-permute-start(bf16[4,2,4,128,128]{4,3,2,1,0:T(8,128)(2,1)S(1)} %collective-permute-done.4.refs_1_), channel_id=1, source_target_pairs={{0,1},{1,0},{2,3},{3,2},{4,5},{5,4},{6,7},{7,6},{8,9},{9,8},{10,11... | collective-permute-start | bytes 3145736 | tf_op jit(solution)/shard_map/ppermute | solution.py:40
  37.4 1.5 %collective-permute-done.5.refs_2_ = bf16[4,2,4,128,128]{4,3,2,1,0:T(8,128)(2,1)S(1)} collective-permute-done((bf16[4,2,4,128,128]{4,3,2,1,0:T(8,128)(2,1)S(1)}, bf16[4,2,4,128,128]{4,3,2,1,0:T(8,128)(2,1)S(1)}, u32[]{:S(2)}, u32[]{:S(2)}) %collective-permute-start.5) | collective-permute-done | bytes 1048608 | tf_op jit(solution)/shard_map/ppermute | solution.py:40
  38.9 5.0 %collective-permute-start.13 = (bf16[4,2,4,128,128]{4,3,2,1,0:T(8,128)(2,1)S(1)}, bf16[4,2,4,128,128]{4,3,2,1,0:T(8,128)(2,1)S(1)}, u32[]{:S(2)}, u32[]{:S(2)}) collective-permute-start(bf16[4,2,4,128,128]{4,3,2,1,0:T(8,128)(2,1)S(1)} %collective-permute-done.5.refs_2_), channel_id=1, source_target_pairs={{0,1},{1,0},{2,3},{3,2},{4,5},{5,4},{6,7},{7,6},{8,9},{9,8},{10,11... | collective-permute-start | bytes 3145736 | tf_op jit(solution)/shard_map/ppermute | solution.py:40
  43.9 0.0 collective-permute-done.10.refs_15_
  43.9 0.0 collective-permute-start.11
  43.9 1.4 %collective-permute-start.17 = (bf16[160,2048]{1,0:T(8,128)(2,1)S(1)}, bf16[160,2048]{1,0:T(8,128)(2,1)S(1)}, u32[]{:S(2)}, u32[]{:S(2)}) collective-permute-start(bf16[160,2048]{1,0:T(8,128)(2,1)S(1)} %collective-permute-done.15.refs_9_), channel_id=1, source_target_pairs={{0,32},{1,9},{2,34},{3,11},{4,36},{5,13},{6,38},{7,15},{8,40},{9,1... | collective-permute-start | bytes 1966088 | tf_op jit(solution)/shard_map/ppermute | solution.py:40
  45.3 0.0 collective-permute-done.18.refs_14_
  45.3 1.5 %collective-permute-start.19 = (bf16[160,2048]{1,0:T(8,128)(2,1)}, bf16[160,2048]{1,0:T(8,128)(2,1)}, u32[]{:S(2)}, u32[]{:S(2)}) collective-permute-start(bf16[160,2048]{1,0:T(8,128)(2,1)} %collective-permute-done.18.refs_14_), channel_id=1, source_target_pairs={{0,96},{1,25},{2,98},{3,27},{4,100},{5,29},{6,102},{7,31},{8,104},... | collective-permute-start | bytes 1966088 | tf_op jit(solution)/shard_map/ppermute | solution.py:40
  46.8 0.0 collective-permute-done.12.refs_5_
  46.8 0.0 collective-permute-start.16
  46.8 0.0 collective-permute-done.13.refs_6_
  46.9 2.7 %collective-permute-start.20 = (bf16[160,2048]{1,0:T(8,128)(2,1)S(1)}, bf16[160,2048]{1,0:T(8,128)(2,1)}, u32[]{:S(2)}, u32[]{:S(2)}) collective-permute-start(bf16[160,2048]{1,0:T(8,128)(2,1)S(1)} %pad_maximum_fusion), channel_id=1, source_target_pairs={{0,96},{1,25},{2,98},{3,27},{4,100},{5,29},{6,102},{7,31},{8,104},... | collective-permute-start | bytes 1966088 | tf_op jit(solution)/shard_map/ppermute | solution.py:40
  49.5 5.5 %collective-permute-done.17.refs_11_ = bf16[160,2048]{1,0:T(8,128)(2,1)S(1)} collective-permute-done((bf16[160,2048]{1,0:T(8,128)(2,1)S(1)}, bf16[160,2048]{1,0:T(8,128)(2,1)S(1)}, u32[]{:S(2)}, u32[]{:S(2)}) %collective-permute-start.17) | collective-permute-done | bytes 655392 | tf_op jit(solution)/shard_map/ppermute | solution.py:40
  55.0 1.9 %collective-permute-start.21 = (bf16[160,2048]{1,0:T(8,128)(2,1)S(1)}, bf16[160,2048]{1,0:T(8,128)(2,1)S(1)}, u32[]{:S(2)}, u32[]{:S(2)}) collective-permute-start(bf16[160,2048]{1,0:T(8,128)(2,1)S(1)} %collective-permute-done.15.refs_9_), channel_id=1, source_target_pairs={{0,1},{1,0},{2,3},{3,2},{4,5},{5,4},{6,7},{7,6},{8,9},{9,8},{10,11... | collective-permute-start | bytes 1966088 | tf_op jit(solution)/shard_map/ppermute | solution.py:40
  56.9 0.8 collective-permute-start.23
  57.7 0.2 collective-permute-done.11.refs_3_
  58.0 2.0 %collective-permute-start.14 = (bf16[4,2,4,128,128]{4,3,2,1,0:T(8,128)(2,1)S(1)}, bf16[4,2,4,128,128]{4,3,2,1,0:T(8,128)(2,1)}, u32[]{:S(2)}, u32[]{:S(2)}) collective-permute-start(bf16[4,2,4,128,128]{4,3,2,1,0:T(8,128)(2,1)S(1)} %collective-permute-done.11.refs_3_), channel_id=1, source_target_pairs={{0,1},{1,0},{2,3},{3,2},{4,5},{5,4},{6,7},{7,6},{8,9},{9,8},{10,11... | collective-permute-start | bytes 3145736 | tf_op jit(solution)/shard_map/ppermute | solution.py:40
  60.0 2.1 %collective-permute-done.16.refs_10_ = bf16[160,2048]{1,0:T(8,128)(2,1)} collective-permute-done((bf16[160,2048]{1,0:T(8,128)(2,1)S(1)}, bf16[160,2048]{1,0:T(8,128)(2,1)}, u32[]{:S(2)}, u32[]{:S(2)}) %collective-permute-start.16) | collective-permute-done | bytes 655392 | tf_op jit(solution)/shard_map/ppermute | solution.py:40
  62.1 1.9 %collective-permute-start.24 = (bf16[160,2048]{1,0:T(8,128)(2,1)}, bf16[160,2048]{1,0:T(8,128)(2,1)}, u32[]{:S(2)}, u32[]{:S(2)}) collective-permute-start(bf16[160,2048]{1,0:T(8,128)(2,1)} %collective-permute-done.19.refs_12_), channel_id=1, source_target_pairs={{0,1},{1,0},{2,3},{3,2},{4,5},{5,4},{6,7},{7,6},{8,9},{9,8},{10,11... | collective-permute-start | bytes 1966088 | tf_op jit(solution)/shard_map/ppermute | solution.py:40
  64.0 0.6 collective-permute-start.22
  64.7 0.1 collective-permute-start.25
  64.8 0.0 collective-permute-done.23.refs_18_
  64.8 0.7 copy-done.11
  65.5 0.9 copy-done.12
  66.3 0.0 collective-permute-start.26
  66.4 0.6 pad_add_fusion.place
  67.0 0.6 fusion.2
  67.5 0.0 collective-permute-done.24.refs_19_
  67.5 0.0 collective-permute-done.22.refs_17_
  67.5 0.4 collective-permute-done.25.refs_20_
  68.0 0.9 %collective-permute-done.26.refs_21_ = bf16[160,2048]{1,0:T(8,128)(2,1)} collective-permute-done((bf16[160,2048]{1,0:T(8,128)(2,1)}, bf16[160,2048]{1,0:T(8,128)(2,1)}, u32[]{:S(2)}, u32[]{:S(2)}) %collective-permute-start.26) | collective-permute-done | bytes 655392 | tf_op jit(solution)/shard_map/ppermute | solution.py:40
  68.9 0.0 collective-permute-done.14.refs_7_
  68.9 17.7 %shard_map.55 = f32[4,16,4,2,16,256]{5,4,3,2,1,0:T(8,128)} custom-call(s32[4]{0:T(128)} %pad_add_fusion.place, s32[4,16]{1,0:T(4,128)} %bitcast.29, bf16[4,2,4,128,128]{4,3,2,1,0:T(8,128)(2,1)} %refs_0_.1, bf16[4,2,4,128,128]{4,3,2,1,0:T(8,128)(2,1)} %copy-done.4, bf16[4,2,4,128,128]{4,3,2,1,0:T(8,128)(2,1)} %copy-done.5, ...), custom_call_target="tpu_custom_call" | custom-call | flops 10737418240 | bytes 27262976 | tf_op jit(solution)/shard_map/pallas_call | solution.py:154
  (69 shorter events, 0.6 us)
Async XLA Ops:
  0.0 9.5 %copy-start.2 = (bf16[4,2,4,128,128]{4,3,2,1,0:T(8,128)(2,1)S(1)}, bf16[4,2,4,128,128]{4,3,2,1,0:T(8,128)(2,1)}, u32[]{:S(2)}) copy-start(bf16[4,2,4,128,128]{4,3,2,1,0:T(8,128)(2,1)} %refs_0_.1) | copy-start | bytes 3145732
  3.0 2.3 %collective-permute-start = (bf16[16,1152]{1,0:T(8,128)(2,1)S(1)}, bf16[16,1152]{1,0:T(8,128)(2,1)S(1)}, u32[]{:S(2)}, u32[]{:S(2)}) collective-permute-start(bf16[16,1152]{1,0:T(8,128)(2,1)S(1)} %pad_maximum_fusion.2), channel_id=1, source_target_pairs={{0,1},{1,0},{2,3},{3,2},{4,5},{5,4},{6,7},{7,6},{8,9},{9,8},{10,11... | collective-permute-start | bytes 110600 | tf_op jit(solution)/shard_map/ppermute | solution.py:40
  4.4 11.7 %collective-permute-start.6 = (bf16[4,2,4,128,128]{4,3,2,1,0:T(8,128)(2,1)}, bf16[4,2,4,128,128]{4,3,2,1,0:T(8,128)(2,1)S(1)}, u32[]{:S(2)}, u32[]{:S(2)}) collective-permute-start(bf16[4,2,4,128,128]{4,3,2,1,0:T(8,128)(2,1)} %refs_0_.1), channel_id=1, source_target_pairs={{0,1},{1,0},{2,3},{3,2},{4,5},{5,4},{6,7},{7,6},{8,9},{9,8},{10,11... | collective-permute-start | bytes 3145736 | tf_op jit(solution)/shard_map/ppermute | solution.py:40
  5.7 5.9 %collective-permute-start.1 = (bf16[16,2688]{1,0:T(8,128)(2,1)S(1)}, bf16[16,2688]{1,0:T(8,128)(2,1)S(1)}, u32[]{:S(2)}, u32[]{:S(2)}) collective-permute-start(bf16[16,2688]{1,0:T(8,128)(2,1)S(1)} %get-tuple-element.24), channel_id=1, source_target_pairs={{0,6},{1,7},{2,0},{3,1},{4,2},{5,3},{6,4},{7,5},{8,14},{9,15},{10,... | collective-permute-start | bytes 258056 | tf_op jit(solution)/shard_map/ppermute | solution.py:40
  8.4 4.9 %collective-permute-start.2 = (bf16[16,2688]{1,0:T(8,128)(2,1)S(1)}, bf16[16,2688]{1,0:T(8,128)(2,1)S(1)}, u32[]{:S(2)}, u32[]{:S(2)}) collective-permute-start(bf16[16,2688]{1,0:T(8,128)(2,1)S(1)} %get-tuple-element.25), channel_id=1, source_target_pairs={{0,4},{1,5},{2,6},{3,7},{4,0},{5,1},{6,2},{7,3},{8,12},{9,13},{10,... | collective-permute-start | bytes 258056 | tf_op jit(solution)/shard_map/ppermute | solution.py:40
  8.9 7.1 %collective-permute-start.3 = (bf16[16,2688]{1,0:T(8,128)(2,1)S(1)}, bf16[16,2688]{1,0:T(8,128)(2,1)S(1)}, u32[]{:S(2)}, u32[]{:S(2)}) collective-permute-start(bf16[16,2688]{1,0:T(8,128)(2,1)S(1)} %get-tuple-element.26), channel_id=1, source_target_pairs={{0,2},{1,3},{2,4},{3,5},{4,6},{5,7},{6,0},{7,1},{8,10},{9,11},{10,... | collective-permute-start | bytes 258056 | tf_op jit(solution)/shard_map/ppermute | solution.py:40
  9.5 14.4 %collective-permute-start.4 = (bf16[4,2,4,128,128]{4,3,2,1,0:T(8,128)(2,1)S(1)}, bf16[4,2,4,128,128]{4,3,2,1,0:T(8,128)(2,1)S(1)}, u32[]{:S(2)}, u32[]{:S(2)}) collective-permute-start(bf16[4,2,4,128,128]{4,3,2,1,0:T(8,128)(2,1)S(1)} %copy-done.2), channel_id=1, source_target_pairs={{0,2},{1,7},{2,4},{3,1},{4,6},{5,3},{6,0},{7,5},{8,10},{9,15},{10,... | collective-permute-start | bytes 3145736 | tf_op jit(solution)/shard_map/ppermute | solution.py:40
  16.1 11.6 %copy-start.3 = (bf16[4,2,4,128,128]{4,3,2,1,0:T(8,128)(2,1)}, bf16[4,2,4,128,128]{4,3,2,1,0:T(8,128)(2,1)S(1)}, u32[]{:S(2)}) copy-start(bf16[4,2,4,128,128]{4,3,2,1,0:T(8,128)(2,1)S(1)} %collective-permute-done.6.refs_4_) | copy-start | bytes 3145732
  16.1 11.4 %collective-permute-start.9 = (bf16[80,2048]{1,0:T(8,128)(2,1)S(1)}, bf16[80,2048]{1,0:T(8,128)(2,1)S(1)}, u32[]{:S(2)}, u32[]{:S(2)}) collective-permute-start(bf16[80,2048]{1,0:T(8,128)(2,1)S(1)} %maximum_maximum_fusion), channel_id=1, source_target_pairs={{0,24},{1,97},{2,26},{3,99},{4,28},{5,101},{6,30},{7,103},{8,0},{9... | collective-permute-start | bytes 983048 | tf_op jit(solution)/shard_map/ppermute | solution.py:40
  20.0 7.8 %collective-permute-start.8 = (bf16[80,2048]{1,0:T(8,128)(2,1)S(1)}, bf16[80,2048]{1,0:T(8,128)(2,1)S(1)}, u32[]{:S(2)}, u32[]{:S(2)}) collective-permute-start(bf16[80,2048]{1,0:T(8,128)(2,1)S(1)} %maximum_maximum_fusion), channel_id=1, source_target_pairs={{0,16},{1,65},{2,18},{3,67},{4,20},{5,69},{6,22},{7,71},{8,24},{9,... | collective-permute-start | bytes 983048 | tf_op jit(solution)/shard_map/ppermute | solution.py:40
  20.0 10.9 %collective-permute-start.7 = (bf16[80,2048]{1,0:T(8,128)(2,1)S(1)}, bf16[80,2048]{1,0:T(8,128)(2,1)S(1)}, u32[]{:S(2)}, u32[]{:S(2)}) collective-permute-start(bf16[80,2048]{1,0:T(8,128)(2,1)S(1)} %maximum_maximum_fusion), channel_id=1, source_target_pairs={{0,8},{1,33},{2,10},{3,35},{4,12},{5,37},{6,14},{7,39},{8,16},{9,4... | collective-permute-start | bytes 983048 | tf_op jit(solution)/shard_map/ppermute | solution.py:40
  23.9 11.4 %copy-start.4 = (bf16[4,2,4,128,128]{4,3,2,1,0:T(8,128)(2,1)}, bf16[4,2,4,128,128]{4,3,2,1,0:T(8,128)(2,1)S(1)}, u32[]{:S(2)}) copy-start(bf16[4,2,4,128,128]{4,3,2,1,0:T(8,128)(2,1)S(1)} %collective-permute-done.4.refs_1_) | copy-start | bytes 3145732
  23.9 15.1 %collective-permute-start.5 = (bf16[4,2,4,128,128]{4,3,2,1,0:T(8,128)(2,1)S(1)}, bf16[4,2,4,128,128]{4,3,2,1,0:T(8,128)(2,1)S(1)}, u32[]{:S(2)}, u32[]{:S(2)}) collective-permute-start(bf16[4,2,4,128,128]{4,3,2,1,0:T(8,128)(2,1)S(1)} %collective-permute-done.4.refs_1_), channel_id=1, source_target_pairs={{0,2},{1,7},{2,4},{3,1},{4,6},{5,3},{6,0},{7,5},{8,10},{9,15},{10,... | collective-permute-start | bytes 3145736 | tf_op jit(solution)/shard_map/ppermute | solution.py:40
  31.1 1.4 %copy-start = (bf16[320,2048]{1,0:T(8,128)(2,1)}, bf16[320,2048]{1,0:T(8,128)(2,1)S(1)}, u32[]{:S(2)}) copy-start(bf16[320,2048]{1,0:T(8,128)(2,1)S(1)} %get-tuple-element.52.refs_8_) | copy-start | bytes 3932164
  31.2 12.7 %collective-permute-start.10 = (bf16[320,2048]{1,0:T(8,128)(2,1)S(1)}, bf16[320,2048]{1,0:T(8,128)(2,1)S(1)}, u32[]{:S(2)}, u32[]{:S(2)}) collective-permute-start(bf16[320,2048]{1,0:T(8,128)(2,1)S(1)} %get-tuple-element.52.refs_8_), channel_id=1, source_target_pairs={{0,1},{1,0},{2,3},{3,2},{4,5},{5,4},{6,7},{7,6},{8,9},{9,8},{10,11... | collective-permute-start | bytes 3932168 | tf_op jit(solution)/shard_map/ppermute | solution.py:40
  32.4 11.5 %collective-permute-start.15 = (bf16[160,2048]{1,0:T(8,128)(2,1)S(1)}, bf16[160,2048]{1,0:T(8,128)(2,1)S(1)}, u32[]{:S(2)}, u32[]{:S(2)}) collective-permute-start(bf16[160,2048]{1,0:T(8,128)(2,1)S(1)} %pad_maximum_fusion), channel_id=1, source_target_pairs={{0,32},{1,9},{2,34},{3,11},{4,36},{5,13},{6,38},{7,15},{8,40},{9,1... | collective-permute-start | bytes 1966088 | tf_op jit(solution)/shard_map/ppermute | solution.py:40
  32.6 12.7 %collective-permute-start.18 = (bf16[160,2048]{1,0:T(8,128)(2,1)S(1)}, bf16[160,2048]{1,0:T(8,128)(2,1)}, u32[]{:S(2)}, u32[]{:S(2)}) collective-permute-start(bf16[160,2048]{1,0:T(8,128)(2,1)S(1)} %pad_maximum_fusion.1), channel_id=1, source_target_pairs={{0,96},{1,25},{2,98},{3,27},{4,100},{5,29},{6,102},{7,31},{8,104},... | collective-permute-start | bytes 1966088 | tf_op jit(solution)/shard_map/ppermute | solution.py:40
  35.3 11.5 %collective-permute-start.12 = (bf16[4,2,4,128,128]{4,3,2,1,0:T(8,128)(2,1)S(1)}, bf16[4,2,4,128,128]{4,3,2,1,0:T(8,128)(2,1)S(1)}, u32[]{:S(2)}, u32[]{:S(2)}) collective-permute-start(bf16[4,2,4,128,128]{4,3,2,1,0:T(8,128)(2,1)S(1)} %collective-permute-done.4.refs_1_), channel_id=1, source_target_pairs={{0,1},{1,0},{2,3},{3,2},{4,5},{5,4},{6,7},{7,6},{8,9},{9,8},{10,11... | collective-permute-start | bytes 3145736 | tf_op jit(solution)/shard_map/ppermute | solution.py:40
  38.9 25.1 %copy-start.5 = (bf16[4,2,4,128,128]{4,3,2,1,0:T(8,128)(2,1)}, bf16[4,2,4,128,128]{4,3,2,1,0:T(8,128)(2,1)S(1)}, u32[]{:S(2)}) copy-start(bf16[4,2,4,128,128]{4,3,2,1,0:T(8,128)(2,1)S(1)} %collective-permute-done.5.refs_2_) | copy-start | bytes 3145732
  38.9 7.9 %collective-permute-start.13 = (bf16[4,2,4,128,128]{4,3,2,1,0:T(8,128)(2,1)S(1)}, bf16[4,2,4,128,128]{4,3,2,1,0:T(8,128)(2,1)S(1)}, u32[]{:S(2)}, u32[]{:S(2)}) collective-permute-start(bf16[4,2,4,128,128]{4,3,2,1,0:T(8,128)(2,1)S(1)} %collective-permute-done.5.refs_2_), channel_id=1, source_target_pairs={{0,1},{1,0},{2,3},{3,2},{4,5},{5,4},{6,7},{7,6},{8,9},{9,8},{10,11... | collective-permute-start | bytes 3145736 | tf_op jit(solution)/shard_map/ppermute | solution.py:40
  43.9 25.0 %copy-start.1 = (bf16[320,2048]{1,0:T(8,128)(2,1)}, bf16[320,2048]{1,0:T(8,128)(2,1)S(1)}, u32[]{:S(2)}) copy-start(bf16[320,2048]{1,0:T(8,128)(2,1)S(1)} %collective-permute-done.10.refs_15_) | copy-start | bytes 3932164
  43.9 14.1 %collective-permute-start.11 = (bf16[4,2,4,128,128]{4,3,2,1,0:T(8,128)(2,1)S(1)}, bf16[4,2,4,128,128]{4,3,2,1,0:T(8,128)(2,1)S(1)}, u32[]{:S(2)}, u32[]{:S(2)}) collective-permute-start(bf16[4,2,4,128,128]{4,3,2,1,0:T(8,128)(2,1)S(1)} %collective-permute-done.5.refs_2_), channel_id=1, source_target_pairs={{0,2},{1,7},{2,4},{3,1},{4,6},{5,3},{6,0},{7,5},{8,10},{9,15},{10,... | collective-permute-start | bytes 3145736 | tf_op jit(solution)/shard_map/ppermute | solution.py:40
  43.9 20.8 %copy-start.9 = (bf16[160,2048]{1,0:T(8,128)(2,1)}, bf16[160,2048]{1,0:T(8,128)(2,1)S(1)}, u32[]{:S(2)}) copy-start(bf16[160,2048]{1,0:T(8,128)(2,1)S(1)} %collective-permute-done.15.refs_9_) | copy-start | bytes 1966084
  43.9 11.1 %collective-permute-start.17 = (bf16[160,2048]{1,0:T(8,128)(2,1)S(1)}, bf16[160,2048]{1,0:T(8,128)(2,1)S(1)}, u32[]{:S(2)}, u32[]{:S(2)}) collective-permute-start(bf16[160,2048]{1,0:T(8,128)(2,1)S(1)} %collective-permute-done.15.refs_9_), channel_id=1, source_target_pairs={{0,32},{1,9},{2,34},{3,11},{4,36},{5,13},{6,38},{7,15},{8,40},{9,1... | collective-permute-start | bytes 1966088 | tf_op jit(solution)/shard_map/ppermute | solution.py:40
  45.3 11.6 %collective-permute-start.19 = (bf16[160,2048]{1,0:T(8,128)(2,1)}, bf16[160,2048]{1,0:T(8,128)(2,1)}, u32[]{:S(2)}, u32[]{:S(2)}) collective-permute-start(bf16[160,2048]{1,0:T(8,128)(2,1)} %collective-permute-done.18.refs_14_), channel_id=1, source_target_pairs={{0,96},{1,25},{2,98},{3,27},{4,100},{5,29},{6,102},{7,31},{8,104},... | collective-permute-start | bytes 1966088 | tf_op jit(solution)/shard_map/ppermute | solution.py:40
  46.8 17.8 %copy-start.6 = (bf16[4,2,4,128,128]{4,3,2,1,0:T(8,128)(2,1)}, bf16[4,2,4,128,128]{4,3,2,1,0:T(8,128)(2,1)S(1)}, u32[]{:S(2)}) copy-start(bf16[4,2,4,128,128]{4,3,2,1,0:T(8,128)(2,1)S(1)} %collective-permute-done.12.refs_5_) | copy-start | bytes 3145732
  46.8 15.3 %collective-permute-start.16 = (bf16[160,2048]{1,0:T(8,128)(2,1)S(1)}, bf16[160,2048]{1,0:T(8,128)(2,1)}, u32[]{:S(2)}, u32[]{:S(2)}) collective-permute-start(bf16[160,2048]{1,0:T(8,128)(2,1)S(1)} %pad_maximum_fusion.1), channel_id=1, source_target_pairs={{0,32},{1,9},{2,34},{3,11},{4,36},{5,13},{6,38},{7,15},{8,40},{9,1... | collective-permute-start | bytes 1966088 | tf_op jit(solution)/shard_map/ppermute | solution.py:40
  46.9 17.8 %copy-start.7 = (bf16[4,2,4,128,128]{4,3,2,1,0:T(8,128)(2,1)}, bf16[4,2,4,128,128]{4,3,2,1,0:T(8,128)(2,1)S(1)}, u32[]{:S(2)}) copy-start(bf16[4,2,4,128,128]{4,3,2,1,0:T(8,128)(2,1)S(1)} %collective-permute-done.13.refs_6_) | copy-start | bytes 3145732
  46.9 17.2 %collective-permute-start.20 = (bf16[160,2048]{1,0:T(8,128)(2,1)S(1)}, bf16[160,2048]{1,0:T(8,128)(2,1)}, u32[]{:S(2)}, u32[]{:S(2)}) collective-permute-start(bf16[160,2048]{1,0:T(8,128)(2,1)S(1)} %pad_maximum_fusion), channel_id=1, source_target_pairs={{0,96},{1,25},{2,98},{3,27},{4,100},{5,29},{6,102},{7,31},{8,104},... | collective-permute-start | bytes 1966088 | tf_op jit(solution)/shard_map/ppermute | solution.py:40
  55.0 9.8 %copy-start.10 = (bf16[160,2048]{1,0:T(8,128)(2,1)}, bf16[160,2048]{1,0:T(8,128)(2,1)S(1)}, u32[]{:S(2)}) copy-start(bf16[160,2048]{1,0:T(8,128)(2,1)S(1)} %collective-permute-done.17.refs_11_) | copy-start | bytes 1966084
  55.0 9.6 %collective-permute-start.21 = (bf16[160,2048]{1,0:T(8,128)(2,1)S(1)}, bf16[160,2048]{1,0:T(8,128)(2,1)S(1)}, u32[]{:S(2)}, u32[]{:S(2)}) collective-permute-start(bf16[160,2048]{1,0:T(8,128)(2,1)S(1)} %collective-permute-done.15.refs_9_), channel_id=1, source_target_pairs={{0,1},{1,0},{2,3},{3,2},{4,5},{5,4},{6,7},{7,6},{8,9},{9,8},{10,11... | collective-permute-start | bytes 1966088 | tf_op jit(solution)/shard_map/ppermute | solution.py:40
  56.9 7.9 %collective-permute-start.23 = (bf16[160,2048]{1,0:T(8,128)(2,1)S(1)}, bf16[160,2048]{1,0:T(8,128)(2,1)S(1)}, u32[]{:S(2)}, u32[]{:S(2)}) collective-permute-start(bf16[160,2048]{1,0:T(8,128)(2,1)S(1)} %collective-permute-done.17.refs_11_), channel_id=1, source_target_pairs={{0,1},{1,0},{2,3},{3,2},{4,5},{5,4},{6,7},{7,6},{8,9},{9,8},{10,11... | collective-permute-start | bytes 1966088 | tf_op jit(solution)/shard_map/ppermute | solution.py:40
  58.0 10.9 %copy-start.8 = (bf16[4,2,4,128,128]{4,3,2,1,0:T(8,128)(2,1)}, bf16[4,2,4,128,128]{4,3,2,1,0:T(8,128)(2,1)S(1)}, u32[]{:S(2)}) copy-start(bf16[4,2,4,128,128]{4,3,2,1,0:T(8,128)(2,1)S(1)} %collective-permute-done.11.refs_3_) | copy-start | bytes 3145732
  58.0 10.9 %collective-permute-start.14 = (bf16[4,2,4,128,128]{4,3,2,1,0:T(8,128)(2,1)S(1)}, bf16[4,2,4,128,128]{4,3,2,1,0:T(8,128)(2,1)}, u32[]{:S(2)}, u32[]{:S(2)}) collective-permute-start(bf16[4,2,4,128,128]{4,3,2,1,0:T(8,128)(2,1)S(1)} %collective-permute-done.11.refs_3_), channel_id=1, source_target_pairs={{0,1},{1,0},{2,3},{3,2},{4,5},{5,4},{6,7},{7,6},{8,9},{9,8},{10,11... | collective-permute-start | bytes 3145736 | tf_op jit(solution)/shard_map/ppermute | solution.py:40
  62.1 5.4 %collective-permute-start.24 = (bf16[160,2048]{1,0:T(8,128)(2,1)}, bf16[160,2048]{1,0:T(8,128)(2,1)}, u32[]{:S(2)}, u32[]{:S(2)}) collective-permute-start(bf16[160,2048]{1,0:T(8,128)(2,1)} %collective-permute-done.19.refs_12_), channel_id=1, source_target_pairs={{0,1},{1,0},{2,3},{3,2},{4,5},{5,4},{6,7},{7,6},{8,9},{9,8},{10,11... | collective-permute-start | bytes 1966088 | tf_op jit(solution)/shard_map/ppermute | solution.py:40
  64.0 3.5 %collective-permute-start.22 = (bf16[160,2048]{1,0:T(8,128)(2,1)}, bf16[160,2048]{1,0:T(8,128)(2,1)}, u32[]{:S(2)}, u32[]{:S(2)}) collective-permute-start(bf16[160,2048]{1,0:T(8,128)(2,1)} %collective-permute-done.16.refs_10_), channel_id=1, source_target_pairs={{0,1},{1,0},{2,3},{3,2},{4,5},{5,4},{6,7},{7,6},{8,9},{9,8},{10,11... | collective-permute-start | bytes 1966088 | tf_op jit(solution)/shard_map/ppermute | solution.py:40
  64.7 0.8 copy-start.11
  64.7 3.3 %collective-permute-start.25 = (bf16[160,2048]{1,0:T(8,128)(2,1)}, bf16[160,2048]{1,0:T(8,128)(2,1)}, u32[]{:S(2)}, u32[]{:S(2)}) collective-permute-start(bf16[160,2048]{1,0:T(8,128)(2,1)} %collective-permute-done.20.refs_13_), channel_id=1, source_target_pairs={{0,1},{1,0},{2,3},{3,2},{4,5},{5,4},{6,7},{7,6},{8,9},{9,8},{10,11... | collective-permute-start | bytes 1966088 | tf_op jit(solution)/shard_map/ppermute | solution.py:40
  65.5 0.9 copy-start.12
  66.3 2.5 %collective-permute-start.26 = (bf16[160,2048]{1,0:T(8,128)(2,1)}, bf16[160,2048]{1,0:T(8,128)(2,1)}, u32[]{:S(2)}, u32[]{:S(2)}) collective-permute-start(bf16[160,2048]{1,0:T(8,128)(2,1)} %collective-permute-done.18.refs_14_), channel_id=1, source_target_pairs={{0,1},{1,0},{2,3},{3,2},{4,5},{5,4},{6,7},{7,6},{8,9},{9,8},{10,11... | collective-permute-start | bytes 1966088 | tf_op jit(solution)/shard_map/ppermute | solution.py:40
